TPU v7x, 128 devices: a whole 4x4x4 slice. The times are simulated.
128 devices in a mesh: var: 16 (over y_lo, z, core), samp: 8 (over y_hi, x).
Axes of the slice: x: 4, y: 4 (y_hi: 2, y_lo: 2; y = y_hi * 2 + y_lo), z: 4, core: 2. Of those that a mesh axis runs over, the one named last changes fastest.
Arguments:
- geno: bfloat16 [16384, 32768], P('samp', 'var'), may hold values from -5 to 5
- scale_index: int32 [128, 32768], P('samp', 'var'), may hold values from 0 to 15
- scale_table: float32 [16], replicated, may hold values from 0.25 to 4
- residual: float32 [8, 16384], P(None, 'samp'), may hold values from -6 to 6
- beta_active: float32 [8, 7168], P(None, 'var'), may hold values from -6 to 6
- block_inverse: float32 [32, 256, 256], P('var'), may hold values from -1 to 4
- active_ids: int32 [7168], P('var'), may hold values from 0 to 32767, as said below
- admit_ids: int32 [1024], P('var'), may hold values from 0 to 32767, as said below
Outputs:
- scores: float32 [8, 32768], P(None, 'var')
- coefficients: float32 [8, 8192], P(None, 'var')
- residual_out: float32 [8, 16384], P(None, 'samp')
Inputs may be any that keep to these rules, and one draw needn't show every extreme that they name: Variant ids, all different from one another and from those of admit_ids. The fitting slots of one index of var are its 448 entries of active_ids followed by its 64 entries of admit_ids; of these 512 slots at most 64 name variants held by any one index of var, and for every index of var some one holder reaches exactly 64. `admit_ids`: variant ids, as for active_ids.
All inputs are finite; a program needn't handle non-finite values.
Results may differ from a plain program's by a relative error of at most 0.004.
Values may be sent and summed in bfloat16 or wider, within the bound.
No kernel may reach another device: no remote copies, remote signals or barrier semaphores. Data moves between devices by JAX's collectives and lax.ppermute only.
A program may use at most 128 MiB of HBM per device.

v0:
```python
import math

import jax
import jax.numpy as jnp
from jax import lax
from jax.sharding import Mesh
from jax.sharding import PartitionSpec as P

PASSES = 3
VAR = ("var_0", "var_1", "var_2")


penalty = 0.5
epsilon = 1e-06


def copy_for_each(x, axis):
    copies = jnp.broadcast_to(x, (lax.axis_size(axis), *x.shape))
    return lax.all_to_all(copies, axis, split_axis=0, concat_axis=0, tiled=True)


def over_copies(x, axis):
    return copy_for_each(x, axis).sum(axis=0)


def joined_along(tiles, dim):
    tiles = jnp.moveaxis(tiles, 0, dim)
    lengths = tiles.shape
    return tiles.reshape(*lengths[:dim], lengths[dim] * lengths[dim + 1], *lengths[dim + 2 :])


def collect(x, axis, dim):
    tiles = copy_for_each(x, axis)
    return joined_along(tiles, dim)


def cut_along(x, dim, count):
    before, after = (x.shape[:dim], x.shape[dim + 1 :])
    return jnp.moveaxis(x.reshape(*before, count, -1, *after), dim, 0)


def moved_by_axis(tiles, axes, turns):
    lengths = [lax.axis_size(a) for a in axes]
    tiles = tiles.reshape(*lengths, *tiles.shape[1:])
    for k in turns:
        tiles = lax.all_to_all(tiles, axes[k], split_axis=k, concat_axis=k, tiled=True)
    return tiles.reshape(-1, *tiles.shape[len(axes) :])


def exchange_by_chip(x, groups, turns, split_dim, concat_dim):
    count = lax.axis_size(groups[0]) * lax.axis_size(groups[1])
    tiles = cut_along(x, split_dim, count)
    return joined_along(moved_by_axis(tiles, groups, turns), concat_dim)


def together(arrays, axis):
    ravelled, at, done = (jnp.concatenate([a.reshape(-1) for a in arrays]), 0, [])
    running = over_copies(ravelled, axis)
    for a in arrays:
        done.append(running[at : at + a.size].reshape(a.shape))
        at += a.size
    return tuple(done)


def dequantize(values, indices, lookup):
    levels = lookup.shape[0]
    onehot = (indices[:, :, None] == jnp.arange(levels, dtype=jnp.int32)).astype(jnp.float32)
    scales = jnp.dot(onehot, lookup, precision=lax.Precision.HIGHEST)
    groups = indices.shape[0]
    widened = (
        values.reshape(groups, values.shape[0] // groups, values.shape[1]).astype(jnp.float32)
        * scales[:, None, :]
    )
    return widened.reshape(values.shape).astype(jnp.bfloat16)


def slot_layout(variant_ids, var_width, var_count):
    holder = variant_ids // var_width
    column = variant_ids % var_width
    owner_marks = (holder[..., None] == jnp.arange(var_count, dtype=jnp.int32)).astype(jnp.int32)
    before = jnp.cumsum(owner_marks, axis=-2) - owner_marks
    serial = jnp.sum(before * owner_marks, -1)
    return (holder, column, serial)


def block_update(gradient, coeffs, inverse):
    phenos, fit_width = gradient.shape
    blocks, block_size = (inverse.shape[0], inverse.shape[1])
    inner_term = (gradient - penalty * coeffs).reshape(phenos, blocks, block_size)
    direction = jnp.einsum("bij,pbj->pbi", inverse, inner_term, precision=lax.Precision.HIGHEST)
    return direction.reshape(phenos, fit_width).astype(jnp.bfloat16)


def on_device(
    geno, scale_index, scale_table, residual, beta_active, block_inverse, active_ids, admit_ids
):
    var_count = lax.axis_size(VAR)
    var_rank = lax.axis_index(VAR)
    samp_rows, var_width = geno.shape
    inv_root = 1.0 / math.sqrt(samp_rows * lax.axis_size("samp"))
    phenos = residual.shape[0]
    local_ids = jnp.concatenate([active_ids, admit_ids])
    fit_width = local_ids.shape[0]
    capacity = 2 * fit_width // var_count
    dequant = dequantize(geno, scale_index, scale_table)
    resid_low = residual.astype(jnp.bfloat16)
    screened = (
        over_copies(jnp.dot(resid_low, dequant, preferred_element_type=jnp.float32), "samp")
        * inv_root
    )
    all_ids = collect(local_ids, VAR, 0).reshape(var_count, fit_width)
    holder, column, serial = slot_layout(all_ids, var_width, var_count)
    held_here = holder == var_rank
    wanted = held_here[:, None, :] & (
        serial[:, None, :] == jnp.arange(capacity, dtype=jnp.int32)[None, :, None]
    )
    source_column = jnp.sum(jnp.where(wanted, column[:, None, :], 0), -1).reshape(-1)
    present = jnp.any(wanted, -1).reshape(-1)
    selected = jnp.where(
        present[None, :], jnp.take(dequant, source_column, axis=1), jnp.zeros((), jnp.bfloat16)
    )
    position = lax.dynamic_index_in_dim(holder * capacity + serial, var_rank, 0, keepdims=False)
    coeffs = jnp.concatenate([beta_active, jnp.zeros((phenos, admit_ids.shape[0]), jnp.float32)], 1)
    current = residual
    received = exchange_by_chip(selected, (("var_0", "var_1"), "var_2"), (1, 0), 1, 1)
    fitting = jnp.take(received, position, axis=1)
    for pass_index in range(PASSES):
        gradient = (
            over_copies(jnp.dot(resid_low, fitting, preferred_element_type=jnp.float32), "samp")
            * inv_root
        )
        direction = block_update(gradient, coeffs, block_inverse)
        partial_update = jnp.einsum(
            "pc,sc->ps", direction, fitting, preferred_element_type=jnp.float32
        )
        update = over_copies(partial_update, VAR) * inv_root
        cross_sum, square = together(
            (jnp.sum(current * update, 1), jnp.sum(update * update, 1)), "samp"
        )
        factor = (cross_sum / (square + epsilon))[:, None]
        current = current - factor * update
        coeffs = coeffs + factor * direction.astype(jnp.float32)
        if pass_index + 1 < PASSES:
            resid_low = current.astype(jnp.bfloat16)
    return (screened, coeffs, current)


def solution(mesh):
    torus = Mesh(
        mesh.devices.reshape(2, 4, 2, mesh.shape["samp"]), ("var_0", "var_1", "var_2", "samp")
    )
    placed = (
        P("samp", VAR),
        P("samp", VAR),
        P(),
        P(None, "samp"),
        P(None, VAR),
        P(VAR, None, None),
        P(VAR),
        P(VAR),
    )
    return jax.shard_map(
        on_device,
        mesh=torus,
        in_specs=placed,
        out_specs=(P(None, VAR), P(None, VAR), P(None, "samp")),
        check_vma=False,
    )
```

profile of v0, /device:TPU:0, one launch (start us, length us, event | category | flops | bytes accessed | tf_op | source)
XLA Modules:
  0.0 302.6 jit_solution(2310565305567362694)
XLA Ops:
  2.1 6.5 %all-to-all-start.1 = ((s32[16,1,512]{2,1,0:T(1,128)}), s32[16,1,512]{2,1,0:T(1,128)S(1)}, u32[]{:S(2)}, u32[]{:S(2)}) async-start(s32[16,1,512]{2,1,0:T(1,128)} %broadcast_in_dim.93), calls=%async_computation.1 | async-start | bytes 65536 | tf_op jit(solution)/shard_map/all_to_all | solution.py:19
  10.6 12.3 %copy.40 = bf16[2048,2048]{0,1:T(8,128)(2,1)} copy(bf16[2048,2048]{1,0:T(8,128)(2,1)} %param.8) | data formatting | bytes 16777216 | tf_op args[0]
  22.9 4.6 %mul.130 = f32[16,128,2048]{1,0,2:T(8,128)S(1)} broadcast(f32[16,2048]{0,1:T(8,128)S(1)} %bitcast.108), dimensions={0,2} | broadcast | bytes 16908288 | tf_op jit(solution)/shard_map/mul | solution.py:71
  27.5 9.2 %fusion = bf16[2048,2048]{0,1:T(8,128)(2,1)} fusion(f32[256,8,16,128]{3,2,1,0:T(8,128)S(1)} %bitcast.105, bf16[2048,2048]{0,1:T(8,128)(2,1)S(1)} %copy-done.1), kind=kLoop, calls=%fused_computation.3 | loop fusion | flops 12582912 | bytes 33554432 | tf_op jit(solution)/shard_map/convert_element_type | solution.py:74
  36.8 18.1 %reduce-window.6 = s32[16,16,4,128]{3,1,2,0:T(8,128)S(1)} reduce-window(s32[16,16,4,128]{3,1,2,0:T(8,128)S(1)} %fusion.8, s32[]{:T(128)} %constant.80.clone.1), window={size=1x1x1x128 pad=0_0x0_0x0_0x127_0}, to_apply=%region_1.2 | reduce-window | flops 16646144 | bytes 1048580 | tf_op jit(solution)/shard_map/reduce-window
  57.2 13.3 %gather_fusion = bf16[1024,2048]{1,0:T(8,128)(2,1)} fusion(bf16[2048,2048]{0,1:T(8,128)(2,1)} %fusion, s32[1024]{0:T(1024)S(1)} %broadcast_clamp_fusion), kind=kCustom, calls=%fused_computation | custom fusion | bytes 8392704 | tf_op jit(solution)/shard_map/jit(_take)/gather | solution.py:120
  73.6 7.1 %all_to_all.75 = bf16[8,2,2048,64]{2,3,0,1:T(8,128)(2,1)S(1)} all-to-all(bf16[8,2,2048,64]{2,3,0,1:T(8,128)(2,1)S(1)} %copy.48), channel_id=1, replica_groups=mesh['var_0'=2,'var_1'=4,'var_2'=2,'samp'=8] {'var_2'}, dimensions={1} | all-to-all | bytes 8388608 | tf_op jit(solution)/shard_map/all_to_all | solution.py:46
  83.0 5.6 %all-to-all-start.3 = ((bf16[8,2,2048,64]{2,3,1,0:T(8,128)(2,1)}), bf16[8,2,2048,64]{2,3,1,0:T(8,128)(2,1)}, u32[]{:S(2)}, u32[]{:S(2)}) async-start(bf16[8,2,2048,64]{2,3,1,0:T(8,128)(2,1)} %copy.49), calls=%async_computation.3 | async-start | bytes 8388608 | tf_op jit(solution)/shard_map/all_to_all | solution.py:46
  88.6 48.9 %all-to-all-done.3 = bf16[8,2,2048,64]{2,3,1,0:T(8,128)(2,1)} async-done(((bf16[8,2,2048,64]{2,3,1,0:T(8,128)(2,1)}), bf16[8,2,2048,64]{2,3,1,0:T(8,128)(2,1)}, u32[]{:S(2)}, u32[]{:S(2)}) %all-to-all-start.3) | async-done | bytes 4194336 | tf_op jit(solution)/shard_map/all_to_all | solution.py:46
  137.5 8.0 %gather_fusion.1 = bf16[512,2048]{1,0:T(8,128)(2,1)} fusion(bf16[2048,1024]{0,1:T(8,128)(2,1)} %bitcast.16, s32[1024]{0:T(1024)S(1)} %pad_clamp_fusion), kind=kCustom, calls=%fused_computation.1 | custom fusion | bytes 4196352 | tf_op jit(solution)/shard_map/jit(_take)/gather | solution.py:126
  148.0 14.5 %all_to_all.76 = f32[8,8,512]{2,1,0:T(8,128)S(1)} all-to-all(f32[8,8,512]{2,1,0:T(8,128)S(1)} %broadcast_in_dim.103), channel_id=1, replica_groups=mesh['var_0'=2,'var_1'=4,'var_2'=2,'samp'=8] {'samp'}, dimensions={0} | all-to-all | bytes 262144 | tf_op jit(solution)/shard_map/all_to_all | solution.py:19
  163.6 19.8 %all_to_all.77 = f32[16,8,2048]{2,1,0:T(8,128)} all-to-all(f32[16,8,2048]{2,1,0:T(8,128)S(1)} %broadcast_in_dim.104), channel_id=1, replica_groups=mesh['var_0'=2,'var_1'=4,'var_2'=2,'samp'=8] {'var_0','var_1','var_2'}, dimensions={0} | all-to-all | bytes 2097152 | tf_op jit(solution)/shard_map/all_to_all | solution.py:19
  184.9 10.5 %all_to_all.78 = f32[8,1,16]{2,1,0:T(1,128)S(1)} all-to-all(f32[8,1,16]{2,1,0:T(1,128)S(1)} %broadcast_in_dim.105), channel_id=1, replica_groups=mesh['var_0'=2,'var_1'=4,'var_2'=2,'samp'=8] {'samp'}, dimensions={0} | all-to-all | bytes 1024 | tf_op jit(solution)/shard_map/all_to_all | solution.py:19
  196.3 10.5 %all_to_all.79 = f32[8,8,512]{2,1,0:T(8,128)S(1)} all-to-all(f32[8,8,512]{2,1,0:T(8,128)S(1)} %broadcast_in_dim.106), channel_id=1, replica_groups=mesh['var_0'=2,'var_1'=4,'var_2'=2,'samp'=8] {'samp'}, dimensions={0} | all-to-all | bytes 262144 | tf_op jit(solution)/shard_map/all_to_all | solution.py:19
  207.9 19.8 %all_to_all.80 = f32[16,8,2048]{2,1,0:T(8,128)} all-to-all(f32[16,8,2048]{2,1,0:T(8,128)S(1)} %broadcast_in_dim.107), channel_id=1, replica_groups=mesh['var_0'=2,'var_1'=4,'var_2'=2,'samp'=8] {'var_0','var_1','var_2'}, dimensions={0} | all-to-all | bytes 2097152 | tf_op jit(solution)/shard_map/all_to_all | solution.py:19
  229.2 10.2 %all_to_all.81 = f32[8,1,16]{2,1,0:T(1,128)S(1)} all-to-all(f32[8,1,16]{2,1,0:T(1,128)S(1)} %broadcast_in_dim.108), channel_id=1, replica_groups=mesh['var_0'=2,'var_1'=4,'var_2'=2,'samp'=8] {'samp'}, dimensions={0} | all-to-all | bytes 1024 | tf_op jit(solution)/shard_map/all_to_all | solution.py:19
  240.9 3.4 %all-to-all-start.10 = ((f32[8,8,512]{2,1,0:T(8,128)}), f32[8,8,512]{2,1,0:T(8,128)S(1)}, u32[]{:S(2)}, u32[]{:S(2)}) async-start(f32[8,8,512]{2,1,0:T(8,128)} %broadcast_in_dim.109), calls=%async_computation.10 | async-start | bytes 262144 | tf_op jit(solution)/shard_map/all_to_all | solution.py:19
  244.3 5.6 %convolution_bitcast_fusion = f32[8,2048]{1,0:T(8,128)S(1)} fusion(bf16[2048,2048]{0,1:T(8,128)(2,1)} %fusion, f32[8,2048]{1,0:T(8,128)S(1)} %copy-done.2), kind=kOutput, calls=%fused_computation.5 | convolution fusion | flops 67125248 | bytes 8519680 | tf_op jit(solution)/shard_map/dot_general | solution.py:108
  253.1 4.8 %all-to-all-start = ((f32[8,8,2048]{2,1,0:T(8,128)}), f32[8,8,2048]{2,1,0:T(8,128)S(1)}, u32[]{:S(2)}, u32[]{:S(2)}) async-start(f32[8,8,2048]{2,1,0:T(8,128)} %broadcast_in_dim.92), calls=%async_computation | async-start | bytes 1048576 | tf_op jit(solution)/shard_map/all_to_all | solution.py:19
  258.9 9.2 %all-to-all-done = f32[8,8,2048]{2,1,0:T(8,128)S(1)} async-done(((f32[8,8,2048]{2,1,0:T(8,128)}), f32[8,8,2048]{2,1,0:T(8,128)S(1)}, u32[]{:S(2)}, u32[]{:S(2)}) %all-to-all-start) | async-done | bytes 524320 | tf_op jit(solution)/shard_map/all_to_all | solution.py:19
  269.2 3.7 %all-to-all-start.11 = ((f32[16,8,2048]{2,1,0:T(8,128)}), f32[16,8,2048]{2,1,0:T(8,128)S(1)}, u32[]{:S(2)}, u32[]{:S(2)}) async-start(f32[16,8,2048]{2,1,0:T(8,128)} %broadcast_in_dim.110), calls=%async_computation.11 | async-start | bytes 2097152 | tf_op jit(solution)/shard_map/all_to_all | solution.py:19
  272.9 16.5 %all-to-all-done.11 = f32[16,8,2048]{2,1,0:T(8,128)S(1)} async-done(((f32[16,8,2048]{2,1,0:T(8,128)}), f32[16,8,2048]{2,1,0:T(8,128)S(1)}, u32[]{:S(2)}, u32[]{:S(2)}) %all-to-all-start.11) | async-done | bytes 1048608 | tf_op jit(solution)/shard_map/all_to_all | solution.py:19
  290.3 3.3 %all-to-all-start.12 = ((f32[8,1,16]{2,1,0:T(1,128)}), f32[8,1,16]{2,1,0:T(1,128)S(1)}, u32[]{:S(2)}, u32[]{:S(2)}) async-start(f32[8,1,16]{2,1,0:T(1,128)} %broadcast_in_dim.111), calls=%async_computation.12 | async-start | bytes 8192 | tf_op jit(solution)/shard_map/all_to_all | solution.py:19
  294.3 6.9 %all-to-all-done.12 = f32[8,1,16]{2,1,0:T(1,128)S(1)} async-done(((f32[8,1,16]{2,1,0:T(1,128)}), f32[8,1,16]{2,1,0:T(1,128)S(1)}, u32[]{:S(2)}, u32[]{:S(2)}) %all-to-all-start.12) | async-done | bytes 544 | tf_op jit(solution)/shard_map/all_to_all | solution.py:19
  (84 shorter events, 29.5 us)
Async XLA Ops:
  0.6 162.0 %copy-start = (f32[2,256,256]{2,1,0:T(8,128)S(1)}, f32[2,256,256]{2,1,0:T(8,128)}, u32[]{:S(2)}) copy-start(f32[2,256,256]{2,1,0:T(8,128)} %param.13) | copy-start | bytes 1572868
  2.1 34.6 %all-to-all-start.1 = ((s32[16,1,512]{2,1,0:T(1,128)}), s32[16,1,512]{2,1,0:T(1,128)S(1)}, u32[]{:S(2)}, u32[]{:S(2)}) async-start(s32[16,1,512]{2,1,0:T(1,128)} %broadcast_in_dim.93), calls=%async_computation.1 | async-start | bytes 65536 | tf_op jit(solution)/shard_map/all_to_all | solution.py:19
  22.9 4.6 %copy-start.1 = (bf16[2048,2048]{0,1:T(8,128)(2,1)S(1)}, bf16[2048,2048]{0,1:T(8,128)(2,1)}, u32[]{:S(2)}) copy-start(bf16[2048,2048]{0,1:T(8,128)(2,1)} %copy.40) | copy-start | bytes 25165828
  83.0 54.5 %all-to-all-start.3 = ((bf16[8,2,2048,64]{2,3,1,0:T(8,128)(2,1)}), bf16[8,2,2048,64]{2,3,1,0:T(8,128)(2,1)}, u32[]{:S(2)}, u32[]{:S(2)}) async-start(bf16[8,2,2048,64]{2,3,1,0:T(8,128)(2,1)} %copy.49), calls=%async_computation.3 | async-start | bytes 8388608 | tf_op jit(solution)/shard_map/all_to_all | solution.py:46
  145.4 1.9 copy-start.2
  147.3 15.2 %copy-start.3 = (f32[8,448]{1,0:T(8,128)S(1)}, f32[8,448]{1,0:T(8,128)}, u32[]{:S(2)}) copy-start(f32[8,448]{1,0:T(8,128)} %param.12) | copy-start | bytes 43012
  240.9 11.4 %all-to-all-start.10 = ((f32[8,8,512]{2,1,0:T(8,128)}), f32[8,8,512]{2,1,0:T(8,128)S(1)}, u32[]{:S(2)}, u32[]{:S(2)}) async-start(f32[8,8,512]{2,1,0:T(8,128)} %broadcast_in_dim.109), calls=%async_computation.10 | async-start | bytes 262144 | tf_op jit(solution)/shard_map/all_to_all | solution.py:19
  253.1 15.0 %all-to-all-start = ((f32[8,8,2048]{2,1,0:T(8,128)}), f32[8,8,2048]{2,1,0:T(8,128)S(1)}, u32[]{:S(2)}, u32[]{:S(2)}) async-start(f32[8,8,2048]{2,1,0:T(8,128)} %broadcast_in_dim.92), calls=%async_computation | async-start | bytes 1048576 | tf_op jit(solution)/shard_map/all_to_all | solution.py:19
  269.2 20.2 %all-to-all-start.11 = ((f32[16,8,2048]{2,1,0:T(8,128)}), f32[16,8,2048]{2,1,0:T(8,128)S(1)}, u32[]{:S(2)}, u32[]{:S(2)}) async-start(f32[16,8,2048]{2,1,0:T(8,128)} %broadcast_in_dim.110), calls=%async_computation.11 | async-start | bytes 2097152 | tf_op jit(solution)/shard_map/all_to_all | solution.py:19
  290.3 10.8 %all-to-all-start.12 = ((f32[8,1,16]{2,1,0:T(1,128)}), f32[8,1,16]{2,1,0:T(1,128)S(1)}, u32[]{:S(2)}, u32[]{:S(2)}) async-start(f32[8,1,16]{2,1,0:T(1,128)} %broadcast_in_dim.111), calls=%async_computation.12 | async-start | bytes 8192 | tf_op jit(solution)/shard_map/all_to_all | solution.py:19
where the time goes:
time: 304 us; the launch traced here: 303 us
  blocking collectives  92.4 us (30%)
  waiting for transfers between devices  83.8 us (28%)
  local copies, waits for them, and re-layouts  46.2 us (15%)
  other arithmetic  40.1 us (13%)
  starting transfers between devices  27.2 us (9%)
  matrix products  11.9 us (4%)
    all_to_all x6, blocking collectives, copy_for_each(): return lax.all_to_all(copies, axis, split_axis=0, concat_axis=0, tiled=True)  85.3 us
    all_to_all x1, waiting for transfers between devices, moved_by_axis(): lax.all_to_all(tiles, axes[k], split_axis=k, concat_axis=k, tiled=True)  48.9 us
    all_to_all x5, waiting for transfers between devices, copy_for_each(): return lax.all_to_all(copies, axis, split_axis=0, concat_axis=0, tiled=True)  35 us
    all_to_all x5, starting transfers between devices, copy_for_each(): return lax.all_to_all(copies, axis, split_axis=0, concat_axis=0, tiled=True)  21.6 us
    another operation x2, other arithmetic  18.3 us
    gather x1, local copies, waits for them, and re-layouts, on_device(): jnp.take(dequant, source_column, axis=1)  13.3 us
    unnamed x9, local copies, waits for them, and re-layouts  12.4 us
    convert_element_type x1, other arithmetic, dequantize(): return widened.reshape(values.shape).astype(jnp.bfloat16)  9.16 us
  transfers between devices with their start and end apart: 6, of which 5 were waited for; matrix products, arithmetic and copies ran while one was open for 12% of the time, Pallas kernels for 0%

commit v1 on v0

v1 whole, which is shorter than its diff:
```python
import functools
import math

import jax
import jax.numpy as jnp
from jax import lax
from jax.experimental import pallas as pl
from jax.experimental.pallas import tpu as pltpu
from jax.sharding import Mesh
from jax.sharding import PartitionSpec as P

PASSES = 3
VAR = ("y_lo", "z", "core")
SAMP = ("y_hi", "x")
CHIPS = ("y_lo", "z")

CAP = 64
LANES = 128
ROWS = 256
HALF = 4

penalty = 0.5
epsilon = 1e-06
LIMIT = pltpu.CompilerParams(vmem_limit_bytes=48 * 1024 * 1024)
f32 = jnp.float32
bf16 = jnp.bfloat16


def iota(shape, dim):
    return lax.broadcasted_iota(jnp.int32, shape, dim)


def dot(a, b, **kw):
    return jnp.dot(a, b, preferred_element_type=f32, **kw)


def dot_t(a, b, **kw):
    return lax.dot_general(a, b, (((1,), (1,)), ((), ())), preferred_element_type=f32, **kw)


def thirds(x):
    high = x.astype(bf16)
    rest = x - high.astype(f32)
    mid = rest.astype(bf16)
    return high, mid, (rest - mid.astype(f32)).astype(bf16)


def swapped(x):
    here = (iota(x.shape, 0) // HALF) == (iota(x.shape, 1) // CAP)
    return jnp.where(here, x, pltpu.roll(pltpu.roll(x, HALF, 0), CAP, 1))


def column_row(packed):
    low = iota((1, LANES), 1) < CAP
    return jnp.concatenate(
        [
            jnp.where(low, packed[t : t + 1], packed[t + 1 : t + 2])
            for t in range(0, packed.shape[0], 2)
        ],
        1,
    )


def slot_maps(serial, holder, holders):
    fit = serial.shape[1]
    serial2 = jnp.concatenate([serial, serial], 1)
    holder2 = jnp.concatenate([holder, holder], 1)
    shape = (2 * CAP, 2 * fit)
    rows, cols = iota(shape, 0), iota(shape, 1)
    spread = ((rows // CAP) == (cols // fit)) & ((rows % CAP) == serial2)
    mask = (iota((holders * HALF, 2 * fit), 0) // HALF) == holder2
    return spread.astype(f32).astype(bf16), mask.astype(f32)


def layout_kernel(holder_ref, column_ref, serial_ref, packed_ref):
    holders = packed_ref.shape[0]
    fit = holder_ref.shape[1]
    holder = holder_ref[...]
    marks = (iota((holders, fit), 0) == holder).astype(f32)
    earlier = (iota((fit, fit), 0) < iota((fit, fit), 1)).astype(f32).astype(bf16)
    before = dot(marks.astype(bf16), earlier)
    serial = jnp.sum(before * marks, 0, keepdims=True).astype(jnp.int32)
    serial_ref[...] = serial
    spread, _ = slot_maps(serial, holder, holders)
    marks2 = jnp.concatenate([marks, marks], 1)
    column = column_ref[...] + 1
    parts = []
    for piece in (column // LANES, column % LANES):
        row = piece.astype(f32)
        row = jnp.concatenate([row, row], 1)
        parts.append(dot_t((marks2 * row).astype(bf16), spread))
    packed_ref[...] = (parts[0] * LANES + parts[1]).astype(jnp.int32)


def layout(holder, column, holders):
    return pl.pallas_call(
        layout_kernel,
        out_shape=(
            jax.ShapeDtypeStruct(holder.shape, jnp.int32),
            jax.ShapeDtypeStruct((holders, LANES), jnp.int32),
        ),
        compiler_params=LIMIT,
        name="layout",
    )(holder, column)


def look_up(table_ref, index_ref, scales_ref):
    index = index_ref[...]
    scales = jnp.full(index.shape, table_ref[0], f32)
    for level in range(1, table_ref.shape[0]):
        scales = jnp.where(index == level, table_ref[level], scales)
    scales_ref[...] = scales


def dequantized(geno_ref, scales_ref, step):
    rows = geno_ref.shape[0]
    group = 128
    out = []
    for g in range(rows // group):
        scale = scales_ref[pl.ds(step * (rows // group) + g, 1), :]
        wide = geno_ref[g * group : (g + 1) * group, :].astype(f32) * scale
        out.append(wide.astype(bf16))
    return jnp.concatenate(out, 0)


def screen_kernel(table_ref, geno_ref, index_ref, resid_ref, out_ref, scales_ref):
    step = pl.program_id(0)

    @pl.when(step == 0)
    def _():
        look_up(table_ref, index_ref, scales_ref)
        out_ref[...] = jnp.zeros_like(out_ref)

    out_ref[...] += dot(resid_ref[...].astype(bf16), dequantized(geno_ref, scales_ref, step))


def screen(table, geno, index, resid):
    samples, width = geno.shape
    phenos = resid.shape[0]
    return pl.pallas_call(
        screen_kernel,
        grid=(samples // ROWS,),
        in_specs=[
            pl.BlockSpec(memory_space=pltpu.SMEM),
            pl.BlockSpec((ROWS, width), lambda i: (i, 0)),
            pl.BlockSpec(index.shape, lambda i: (0, 0)),
            pl.BlockSpec((phenos, ROWS), lambda i: (0, i)),
        ],
        out_specs=pl.BlockSpec((phenos, width), lambda i: (0, 0)),
        out_shape=jax.ShapeDtypeStruct((phenos, width), f32),
        scratch_shapes=[pltpu.VMEM(index.shape, f32)],
        compiler_params=LIMIT,
        cost_estimate=pl.CostEstimate(
            flops=2 * phenos * samples * width, bytes_accessed=2 * samples * width, transcendentals=0
        ),
        name="screen",
    )(table, geno, index, resid)


def select_kernel(table_ref, packed_ref, geno_ref, index_ref, out_ref, scales_ref, pick_ref):
    step = pl.program_id(0)

    @pl.when(step == 0)
    def _():
        look_up(table_ref, index_ref, scales_ref)
        wanted = column_row(packed_ref[...])

        @pl.loop(0, pick_ref.shape[0], step=ROWS)
        def _(at):
            here = iota((ROWS, pick_ref.shape[1]), 0) + (at + 1) == wanted
            pick_ref[pl.ds(pl.multiple_of(at, ROWS), ROWS), :] = here.astype(f32).astype(bf16)

    out_ref[...] = dot(dequantized(geno_ref, scales_ref, step), pick_ref[...]).astype(bf16)


def select(table, packed, geno, index):
    samples, width = geno.shape
    held = packed.shape[0] * CAP
    return pl.pallas_call(
        select_kernel,
        grid=(samples // ROWS,),
        in_specs=[
            pl.BlockSpec(memory_space=pltpu.SMEM),
            pl.BlockSpec(packed.shape, lambda i: (0, 0)),
            pl.BlockSpec((ROWS, width), lambda i: (i, 0)),
            pl.BlockSpec(index.shape, lambda i: (0, 0)),
        ],
        out_specs=pl.BlockSpec((ROWS, held), lambda i: (i, 0)),
        out_shape=jax.ShapeDtypeStruct((samples, held), bf16),
        scratch_shapes=[pltpu.VMEM(index.shape, f32), pltpu.VMEM((width, held), bf16)],
        compiler_params=LIMIT,
        cost_estimate=pl.CostEstimate(
            flops=2 * samples * width * held, bytes_accessed=2 * samples * width, transcendentals=0
        ),
        name="select",
    )(table, packed, geno, index)


def pick_kernel(inv_root, parts_ref, packed_ref, scores_ref, pay_ref):
    scores = parts_ref[0]
    for j in range(1, parts_ref.shape[0]):
        scores = scores + parts_ref[j]
    scores = scores * inv_root
    scores_ref[...] = scores
    wanted = column_row(packed_ref[...])
    stacked = jnp.concatenate(thirds(scores), 0)
    phenos, width = scores.shape
    total = jnp.zeros((stacked.shape[0], wanted.shape[1]), f32)
    for at in range(0, width, ROWS):
        here = iota((ROWS, wanted.shape[1]), 0) + (at + 1) == wanted
        total += dot(stacked[:, at : at + ROWS], here.astype(f32).astype(bf16))
    held = total[:phenos] + total[phenos : 2 * phenos] + total[2 * phenos :]
    for t in range(wanted.shape[1] // LANES):
        pay_ref[8 * t : 8 * t + 8, :] = swapped(held[:, t * LANES : (t + 1) * LANES])


def pick(parts, packed, inv_root):
    return pl.pallas_call(
        functools.partial(pick_kernel, inv_root),
        out_shape=(
            jax.ShapeDtypeStruct(parts.shape[1:], f32),
            jax.ShapeDtypeStruct((packed.shape[0] * HALF, LANES), f32),
        ),
        compiler_params=LIMIT,
        name="pick",
    )(parts, packed)


def direction_step(data, serial_ref, holder_ref, inverse_ref, advance, wide_ref, d_ref, pay_ref):
    fit = serial_ref.shape[1]
    holders = data.shape[0] // HALF
    spread, mask = slot_maps(serial_ref[...], holder_ref[...], holders)
    high, mid, low = thirds(data)
    placed = (dot(high, spread) + dot(mid, spread) + dot(low, spread)) * mask
    placed = jnp.sum(placed.reshape(-1, 2 * HALF, 2 * fit), 0)
    arrived = placed[:HALF] + placed[HALF:]
    inner = advance(arrived)
    wide_ref[:HALF, :] = inner[:, :fit]
    wide_ref[HALF:, :] = inner[:, fit:]
    blocks, size = inverse_ref.shape[0], inverse_ref.shape[1]
    for b in range(blocks):
        moved = dot_t(
            wide_ref[:, b * size : (b + 1) * size], inverse_ref[b], precision=lax.Precision.HIGHEST
        )
        moved = moved.astype(bf16).astype(f32)
        d_ref[:, b * size : (b + 1) * size] = moved[:HALF]
        d_ref[:, fit + b * size : fit + (b + 1) * size] = moved[HALF:]
    d = d_ref[...]
    d = jnp.concatenate([d, d], 0)
    d = jnp.broadcast_to(d[None], (holders * HALF // d.shape[0], *d.shape)).reshape(mask.shape)
    pay_ref[...] = dot_t((d * mask).astype(bf16), spread)


def first_owner_kernel(
    data_ref, serial_ref, holder_ref, inverse_ref, beta_ref, pay_ref, g_ref, b_ref, d_ref, wide_ref
):
    fit = serial_ref.shape[1]
    active = beta_ref.shape[1]
    b_ref[...] = jnp.zeros_like(b_ref)
    b_ref[:, :active] = beta_ref[:HALF]
    b_ref[:, fit : fit + active] = beta_ref[HALF:]

    def advance(arrived):
        g_ref[...] = arrived
        return arrived - penalty * b_ref[...]

    direction_step(
        data_ref[...], serial_ref, holder_ref, inverse_ref, advance, wide_ref, d_ref, pay_ref
    )


def owner_kernel(
    data_ref,
    serial_ref,
    holder_ref,
    inverse_ref,
    g_in,
    b_in,
    d_in,
    pay_ref,
    g_ref,
    b_ref,
    d_ref,
    factor_ref,
    wide_ref,
    sum_ref,
    rows_ref,
    scalar_ref,
):
    fit = serial_ref.shape[1]
    chunk = sum_ref.shape[0]
    total = data_ref[:chunk, :]
    for at in range(chunk, data_ref.shape[0], chunk):
        total = total + data_ref[at : at + chunk, :]
    sum_ref[...] = total
    for k in range(chunk // (HALF + 1)):
        at = k * (HALF + 1)
        rows_ref[k * HALF : (k + 1) * HALF, :] = sum_ref[at : at + HALF, :]
        if k < scalar_ref.shape[0]:
            scalar_ref[k : k + 1, :] = sum_ref[at + HALF : at + HALF + 1, :]
    factor = scalar_ref[:, :1] / (scalar_ref[:, CAP : CAP + 1] + epsilon)
    factor_ref[...] = jnp.broadcast_to(factor, factor_ref.shape)
    low = iota((HALF, 2 * fit), 1) < fit
    factor = jnp.where(low, factor[:HALF], factor[HALF:])

    def advance(arrived):
        g_ref[...] = g_in[...] - factor * arrived
        b_ref[...] = b_in[...] + factor * d_in[...]
        return g_ref[...] - penalty * b_ref[...]

    direction_step(
        rows_ref[...], serial_ref, holder_ref, inverse_ref, advance, wide_ref, d_ref, pay_ref
    )


def owner(data, serial, holder, inverse, state):
    fit = serial.shape[1]
    phenos = 2 * HALF
    held = jax.ShapeDtypeStruct((HALF, 2 * fit), f32)
    wide = pltpu.VMEM((phenos, fit), f32)
    if len(state) == 1:
        return pl.pallas_call(
            first_owner_kernel,
            out_shape=(jax.ShapeDtypeStruct(data.shape, f32), held, held, held),
            scratch_shapes=[wide],
            compiler_params=LIMIT,
            name="owner_first",
        )(data, serial, holder, inverse, *state)
    holders = lax.axis_size(VAR)
    return pl.pallas_call(
        owner_kernel,
        out_shape=(
            jax.ShapeDtypeStruct((holders * HALF, LANES), f32),
            held,
            held,
            held,
            jax.ShapeDtypeStruct((phenos, LANES), f32),
        ),
        scratch_shapes=[
            wide,
            pltpu.VMEM((holders * (HALF + 1), LANES), f32),
            pltpu.VMEM((holders * HALF, LANES), f32),
            pltpu.VMEM((phenos, LANES), f32),
        ],
        compiler_params=LIMIT,
        name="owner_next",
    )(data, serial, holder, inverse, *state)


def update_kernel(pay_ref, columns_ref, out_ref):
    packed = jnp.concatenate(
        [swapped(pay_ref[at : at + 8, :]) for at in range(0, pay_ref.shape[0], 8)], 1
    )
    out_ref[...] = dot_t(packed.astype(bf16), columns_ref[...])


def partial_update(pay, columns):
    samples, held = columns.shape
    rows = 2 * ROWS
    return pl.pallas_call(
        update_kernel,
        grid=(samples // rows,),
        in_specs=[
            pl.BlockSpec(pay.shape, lambda i: (0, 0)),
            pl.BlockSpec((rows, held), lambda i: (i, 0)),
        ],
        out_specs=pl.BlockSpec((2 * HALF, rows), lambda i: (0, i)),
        out_shape=jax.ShapeDtypeStruct((2 * HALF, samples), f32),
        compiler_params=LIMIT,
        name="update",
    )(pay, columns)


def descent_kernel(inv_root, rank_ref, update_ref, resid_ref, columns_ref, out_ref, acc_ref, dots_ref):
    step = pl.program_id(0)
    phenos = update_ref.shape[0]

    @pl.when(step == 0)
    def _():
        acc_ref[...] = jnp.zeros_like(acc_ref)
        dots_ref[...] = jnp.zeros_like(dots_ref)

    update = update_ref[...]
    high = update.astype(bf16)
    low = (update - high.astype(f32)).astype(bf16)
    acc_ref[...] += dot(jnp.concatenate([high, low], 0), columns_ref[...])
    dots_ref[0] += resid_ref[...] * update
    dots_ref[1] += update * update

    @pl.when(step == pl.num_programs(0) - 1)
    def _():
        grad = (acc_ref[:phenos, :] + acc_ref[phenos:, :]) * inv_root
        cross = jnp.sum(dots_ref[0], 1, keepdims=True)
        square = jnp.sum(dots_ref[1], 1, keepdims=True)
        shape = (phenos, LANES)
        both = jnp.where(iota(shape, 1) < CAP, cross, square)
        mine = iota(shape, 0) == lax.rem(rank_ref[0], phenos)
        row = jnp.sum(jnp.where(mine, both, 0.0), 0, keepdims=True)
        chunk = HALF + 1
        owners = grad.shape[1] // CAP
        copies = out_ref.shape[0] // (chunk * owners)
        for t in range(owners // 2):
            pair = swapped(grad[:, t * LANES : (t + 1) * LANES])
            for n in range(copies):
                at = (n * owners + 2 * t) * chunk
                out_ref[at : at + HALF, :] = pair[:HALF]
                out_ref[at + HALF : at + HALF + 1, :] = row
                out_ref[at + chunk : at + chunk + HALF, :] = pair[HALF:]
                out_ref[at + chunk + HALF : at + 2 * chunk, :] = row


def descent(rank, update, resid, columns, inv_root, copies):
    samples, held = columns.shape
    phenos = update.shape[0]
    rows = 2 * ROWS
    out = (copies * (held // CAP) * (HALF + 1), LANES)
    return pl.pallas_call(
        functools.partial(descent_kernel, inv_root),
        grid=(samples // rows,),
        in_specs=[
            pl.BlockSpec(memory_space=pltpu.SMEM),
            pl.BlockSpec((phenos, rows), lambda i: (0, i)),
            pl.BlockSpec((phenos, rows), lambda i: (0, i)),
            pl.BlockSpec((rows, held), lambda i: (i, 0)),
        ],
        out_specs=pl.BlockSpec(out, lambda i: (0, 0)),
        out_shape=jax.ShapeDtypeStruct(out, f32),
        scratch_shapes=[
            pltpu.VMEM((2 * phenos, held), f32),
            pltpu.VMEM((2, phenos, rows), f32),
        ],
        compiler_params=LIMIT,
        name="descent",
    )(rank, update, resid, columns)


def to_all(x, axes):
    copies = jnp.broadcast_to(x[None], (lax.axis_size(axes), *x.shape))
    return lax.all_to_all(copies, axes, split_axis=0, concat_axis=0, tiled=True)


def exchange(pay, axes):
    count = lax.axis_size(axes)
    rows = pay.shape[0] // count
    shape = (count, rows, LANES) if rows == HALF else (count, 1, rows * LANES)
    return lax.all_to_all(
        pay.reshape(shape), axes, split_axis=0, concat_axis=0, tiled=True
    ).reshape(pay.shape)


def other_core(x):
    return lax.ppermute(x, "core", [(0, 1), (1, 0)])


def sum_over_var(part):
    first = lax.axis_index("core") == 0
    half = part.shape[1] // 2
    a, b = part[:, :half], part[:, half:]
    mine = jnp.where(first, a, b) + other_core(jnp.where(first, b, a))
    mine = jnp.sum(to_all(mine, CHIPS), 0)
    other = other_core(mine)
    return jnp.concatenate([jnp.where(first, mine, other), jnp.where(first, other, mine)], 1)


def on_device(
    geno, scale_index, scale_table, residual, beta_active, block_inverse, active_ids, admit_ids
):
    holders = lax.axis_size(VAR)
    rank = lax.axis_index(VAR).astype(jnp.int32).reshape(1)
    samples, width = geno.shape
    copies = lax.axis_size(SAMP)
    inv_root = 1.0 / math.sqrt(samples * copies)

    ids = jnp.concatenate([active_ids, admit_ids])[None]
    holder = ids // width
    serial, packed = layout(holder, ids % width, holders)
    packed = lax.all_to_all(
        packed.reshape(holders, 1, LANES), VAR, split_axis=0, concat_axis=0, tiled=True
    ).reshape(holders, LANES)

    parts = screen(scale_table, geno, scale_index, residual)
    columns = select(scale_table, packed, geno, scale_index)
    scores, pay = pick(to_all(parts, SAMP), packed, inv_root)

    pay, *state = owner(exchange(pay, VAR), serial, holder, block_inverse, (beta_active,))
    current = residual
    for pass_index in range(PASSES):
        update = sum_over_var(partial_update(exchange(pay, VAR), columns)) * inv_root
        if pass_index + 1 == PASSES:
            break
        data = descent(rank, update, current, columns, inv_root, copies)
        pay, *state, factor = owner(
            exchange(data, SAMP + VAR), serial, holder, block_inverse, state
        )
        current = current - factor[:, :1] * update

    _, coeffs, direction = state
    sums = jnp.concatenate([jnp.sum(current * update, 1), jnp.sum(update * update, 1)])
    sums = jnp.sum(to_all(sums[None], SAMP), (0, 1))
    phenos = residual.shape[0]
    factor = (sums[:phenos] / (sums[phenos:] + epsilon))[:, None]
    fit = serial.shape[1]
    both = lambda x: jnp.concatenate([x[:, :fit], x[:, fit:]], 0)
    return (scores, both(coeffs) + factor * both(direction), current - factor * update)


def solution(mesh):
    torus = Mesh(mesh.devices.reshape(2, 4, 2, 2, 4), VAR + SAMP)
    placed = (
        P(SAMP, VAR),
        P(SAMP, VAR),
        P(),
        P(None, SAMP),
        P(None, VAR),
        P(VAR, None, None),
        P(VAR),
        P(VAR),
    )
    return jax.shard_map(
        on_device,
        mesh=torus,
        in_specs=placed,
        out_specs=(P(None, VAR), P(None, VAR), P(None, SAMP)),
        check_vma=False,
    )
```

time: 304 us -> 192 us (0.63)
  waiting for transfers between devices: 83.8 us -> 27.8 us
  other arithmetic: 40.1 us -> 3.82 us
  local copies, waits for them, and re-layouts: 46.2 us -> 12.3 us
  Pallas kernels: 0 us -> 32.8 us
  matrix products: 11.9 us -> 0 us
  starting transfers between devices: 27.2 us -> 22.8 us
    all_to_all x6 -> x5, waiting for transfers between devices: 83.8 us -> 21.3 us  [the longest x2 15.2 us: to_all(): return lax.all_to_all(copies, axes, split_axis=0, concat_axis=0, tiled=True)]
    pallas_call x0 -> x12, Pallas kernels: none -> 32.8 us  [the longest x1 12.4 us: select(): pl.pallas_call(select_kernel, grid=(samples // ROWS,), in_specs=[pl.Block...]
    gather x2 -> x0, local copies, waits for them, and re-layouts: 21.2 us -> none  [the longest x1 13.3 us: on_device(): jnp.take(dequant, source_column, axis=1)]
    another operation x2 -> x0, other arithmetic: 18.3 us -> none
    dot_general x11 -> x0, matrix products: 11.9 us -> none  [the longest x1 5.64 us: on_device(): jnp.dot(resid_low, dequant, preferred_element_type=jnp.float32)]
    convert_element_type x2 -> x0, other arithmetic: 9.21 us -> none  [the longest x1 9.16 us: dequantize(): return widened.reshape(values.shape).astype(jnp.bfloat16)]
    ppermute x0 -> x6, waiting for transfers between devices: none -> 6.45 us  [other_core(): return lax.ppermute(x, 'core', [(0, 1), (1, 0)])]
    all_to_all x6 -> x5, starting transfers between devices: 27.2 us -> 21.9 us  [the longest x2 8.32 us: exchange(): lax.all_to_all(pay.reshape(shape), axes, split_axis=0, concat_axis=0, til...]
  transfers between devices with their start and end apart: 6 -> 11, of which waited for: 5 -> 9; matrix products, arithmetic and copies ran while one was open for 12% -> 0% of each run, Pallas kernels for 0% -> 10%
where the time goes in v1:
time: 192 us; the launch traced here: 191 us
  blocking collectives  90.6 us (47%)
  Pallas kernels  32.8 us (17%)
  waiting for transfers between devices  27.8 us (14%)
  starting transfers between devices  22.8 us (12%)
  local copies, waits for them, and re-layouts  12.3 us (6%)
  other arithmetic  3.82 us (2%)
    all_to_all x4, blocking collectives, exchange(): lax.all_to_all(pay.reshape(shape), axes, split_axis=0, concat_axis=0, til...  48.9 us
    all_to_all x3, blocking collectives, to_all(): return lax.all_to_all(copies, axes, split_axis=0, concat_axis=0, tiled=True)  41.6 us
    all_to_all x2, waiting for transfers between devices, to_all(): return lax.all_to_all(copies, axes, split_axis=0, concat_axis=0, tiled=True)  15.2 us
    pallas_call x1, Pallas kernels, select(): pl.pallas_call(select_kernel, grid=(samples // ROWS,), in_specs=[pl.Block...  12.4 us
    unnamed x28, local copies, waits for them, and re-layouts  10.9 us
    all_to_all x2, starting transfers between devices, exchange(): lax.all_to_all(pay.reshape(shape), axes, split_axis=0, concat_axis=0, til...  8.32 us
    all_to_all x2, starting transfers between devices, to_all(): return lax.all_to_all(copies, axes, split_axis=0, concat_axis=0, tiled=True)  7.02 us
    pallas_call x1, Pallas kernels, screen(): pl.pallas_call(screen_kernel, grid=(samples // ROWS,), in_specs=[pl.Block...  6.84 us
  transfers between devices with their start and end apart: 11, of which 9 were waited for; matrix products, arithmetic and copies ran while one was open for 0% of the time, Pallas kernels for 10%

profile of v1, /device:TPU:0, one launch (start us, length us, event | category | flops | bytes accessed | tf_op | source)
XLA Modules:
  0.0 190.9 jit_solution(7168958159126055927)
XLA Ops:
  3.3 6.5 %all-to-all-start.1 = ((s32[16,1,128]{2,1,0:T(1,128)}), s32[16,1,128]{2,1,0:T(1,128)S(1)}, u32[]{:S(2)}, u32[]{:S(2)}) async-start(s32[16,1,128]{2,1,0:T(1,128)} %bitcast.3), calls=%async_computation.1 | async-start | bytes 16384 | tf_op jit(solution)/shard_map/all_to_all | solution.py:477
  12.2 6.8 %screen.1 = f32[8,2048]{1,0:T(8,128)S(1)} custom-call(f32[16]{0:T(128)S(1)} %copy-done.12, bf16[2048,2048]{1,0:T(8,128)(2,1)} %geno_ref.3, s32[16,2048]{1,0:T(8,128)S(1)} %copy-done.9, f32[8,2048]{1,0:T(8,128)S(1)} %copy-done.7), custom_call_target="tpu_custom_call" | custom-call | flops 67108864 | bytes 8388608 | tf_op jit(solution)/shard_map/screen/pallas_call | solution.py:140
  19.1 18.6 %all_to_all.60.parts_ref = f32[8,8,2048]{2,1,0:T(8,128)S(1)} all-to-all(f32[8,8,2048]{2,1,0:T(8,128)S(1)} %broadcast_in_dim.10), channel_id=1, replica_groups=mesh['y_lo'=2,'z'=4,'core'=2,'y_hi'=2,'x'=4] {'y_hi','x'}, dimensions={0} | all-to-all | bytes 1048576 | tf_op jit(solution)/shard_map/all_to_all | solution.py:439
  39.2 4.8 %all-to-all-start.2 = ((f32[16,4,128]{2,1,0:T(4,128)}), f32[16,4,128]{2,1,0:T(4,128)S(1)}, u32[]{:S(2)}, u32[]{:S(2)}) async-start(f32[16,4,128]{2,1,0:T(4,128)} %bitcast.6), calls=%async_computation.2 | async-start | bytes 65536 | tf_op jit(solution)/shard_map/all_to_all | solution.py:446
  44.1 6.1 %all-to-all-done.2 = f32[16,4,128]{2,1,0:T(4,128)S(1)} async-done(((f32[16,4,128]{2,1,0:T(4,128)}), f32[16,4,128]{2,1,0:T(4,128)S(1)}, u32[]{:S(2)}, u32[]{:S(2)}) %all-to-all-start.2) | async-done | bytes 32800 | tf_op jit(solution)/shard_map/all_to_all | solution.py:446
  50.2 1.6 owner_first.1
  51.8 3.5 %all-to-all-start.3 = ((f32[16,4,128]{2,1,0:T(4,128)}), f32[16,4,128]{2,1,0:T(4,128)S(1)}, u32[]{:S(2)}, u32[]{:S(2)}) async-start(f32[16,4,128]{2,1,0:T(4,128)} %bitcast.8), calls=%async_computation.3 | async-start | bytes 65536 | tf_op jit(solution)/shard_map/all_to_all | solution.py:446
  55.3 12.4 %select.41.columns_ref = bf16[2048,1024]{1,0:T(8,128)(2,1)S(1)} custom-call(f32[16]{0:T(128)S(1)} %copy-done.13, s32[16,128]{1,0:T(8,128)S(1)} %bitcast.29, bf16[2048,2048]{1,0:T(8,128)(2,1)} %geno_ref.3, s32[16,2048]{1,0:T(8,128)S(1)} %copy-done.10), custom_call_target="tpu_custom_call" | custom-call | flops 8589934592 | bytes 8388608 | tf_op jit(solution)/shard_map/select/pallas_call | solution.py:179
  67.7 1.9 %copy-done = bf16[2048,1024]{1,0:T(8,128)(2,1)} copy-done((bf16[2048,1024]{1,0:T(8,128)(2,1)}, bf16[2048,1024]{1,0:T(8,128)(2,1)S(1)}, u32[]{:S(2)}) %copy-start) | copy-done | bytes 4194328
  69.7 2.2 %copy-done.1 = bf16[2048,1024]{1,0:T(8,128)(2,1)S(1)} copy-done((bf16[2048,1024]{1,0:T(8,128)(2,1)S(1)}, bf16[2048,1024]{1,0:T(8,128)(2,1)}, u32[]{:S(2)}) %copy-start.1) | copy-done | bytes 4194328
  74.7 12.9 %all_to_all.61 = f32[8,8,1024]{2,1,0:T(8,128)S(1)} all-to-all(f32[8,8,1024]{2,1,0:T(8,128)S(1)} %broadcast_in_dim.11), channel_id=1, replica_groups=mesh['y_lo'=2,'z'=4,'core'=2,'y_hi'=2,'x'=4] {'y_lo','z'}, dimensions={0} | all-to-all | bytes 524288 | tf_op jit(solution)/shard_map/all_to_all | solution.py:439
  89.0 2.2 %copy-done.2 = bf16[2048,1024]{1,0:T(8,128)(2,1)S(1)} copy-done((bf16[2048,1024]{1,0:T(8,128)(2,1)S(1)}, bf16[2048,1024]{1,0:T(8,128)(2,1)}, u32[]{:S(2)}) %copy-start.2) | copy-done | bytes 4194328
  92.3 15.6 %all_to_all.62 = f32[128,1,640]{2,1,0:T(1,128)S(1)} all-to-all(f32[128,1,640]{2,1,0:T(1,128)S(1)} %bitcast.21), channel_id=1, replica_groups=mesh['y_lo'=2,'z'=4,'core'=2,'y_hi'=2,'x'=4] {'y_hi','x','y_lo','z','core'}, dimensions={0} | all-to-all | bytes 655360 | tf_op jit(solution)/shard_map/all_to_all | solution.py:446
  108.9 8.7 %all_to_all.63 = f32[16,4,128]{2,1,0:T(4,128)S(1)} all-to-all(f32[16,4,128]{2,1,0:T(4,128)S(1)} %bitcast.31), channel_id=1, replica_groups=mesh['y_lo'=2,'z'=4,'core'=2,'y_hi'=2,'x'=4] {'y_lo','z','core'}, dimensions={0} | all-to-all | bytes 65536 | tf_op jit(solution)/shard_map/all_to_all | solution.py:446
  117.6 1.6 update.4
  120.5 10.1 %all_to_all.64 = f32[8,8,1024]{2,1,0:T(8,128)S(1)} all-to-all(f32[8,8,1024]{2,1,0:T(8,128)S(1)} %broadcast_in_dim.12), channel_id=1, replica_groups=mesh['y_lo'=2,'z'=4,'core'=2,'y_hi'=2,'x'=4] {'y_lo','z'}, dimensions={0} | all-to-all | bytes 524288 | tf_op jit(solution)/shard_map/all_to_all | solution.py:439
  132.0 2.2 %copy-done.4 = bf16[2048,1024]{1,0:T(8,128)(2,1)S(1)} copy-done((bf16[2048,1024]{1,0:T(8,128)(2,1)S(1)}, bf16[2048,1024]{1,0:T(8,128)(2,1)}, u32[]{:S(2)}) %copy-start.4) | copy-done | bytes 4194328
  135.3 16.0 %all_to_all.65 = f32[128,1,640]{2,1,0:T(1,128)S(1)} all-to-all(f32[128,1,640]{2,1,0:T(1,128)S(1)} %bitcast.20), channel_id=1, replica_groups=mesh['y_lo'=2,'z'=4,'core'=2,'y_hi'=2,'x'=4] {'y_hi','x','y_lo','z','core'}, dimensions={0} | all-to-all | bytes 655360 | tf_op jit(solution)/shard_map/all_to_all | solution.py:446
  152.7 8.6 %all_to_all.66 = f32[16,4,128]{2,1,0:T(4,128)S(1)} all-to-all(f32[16,4,128]{2,1,0:T(4,128)S(1)} %bitcast.30), channel_id=1, replica_groups=mesh['y_lo'=2,'z'=4,'core'=2,'y_hi'=2,'x'=4] {'y_lo','z','core'}, dimensions={0} | all-to-all | bytes 65536 | tf_op jit(solution)/shard_map/all_to_all | solution.py:446
  161.4 1.6 update.5
  165.0 3.4 %all-to-all-start.10 = ((f32[8,8,1024]{2,1,0:T(8,128)}), f32[8,8,1024]{2,1,0:T(8,128)S(1)}, u32[]{:S(2)}, u32[]{:S(2)}) async-start(f32[8,8,1024]{2,1,0:T(8,128)} %broadcast_in_dim.13), calls=%async_computation.10 | async-start | bytes 524288 | tf_op jit(solution)/shard_map/all_to_all | solution.py:439
  168.4 7.6 %all-to-all-done.10 = f32[8,8,1024]{2,1,0:T(8,128)S(1)} async-done(((f32[8,8,1024]{2,1,0:T(8,128)}), f32[8,8,1024]{2,1,0:T(8,128)S(1)}, u32[]{:S(2)}, u32[]{:S(2)}) %all-to-all-start.10) | async-done | bytes 262176 | tf_op jit(solution)/shard_map/all_to_all | solution.py:439
  178.2 3.6 %all-to-all-start.11 = ((f32[8,1,16]{2,1,0:T(1,128)}), f32[8,1,16]{2,1,0:T(1,128)S(1)}, u32[]{:S(2)}, u32[]{:S(2)}) async-start(f32[8,1,16]{2,1,0:T(1,128)} %broadcast_in_dim.14), calls=%async_computation.11 | async-start | bytes 8192 | tf_op jit(solution)/shard_map/all_to_all | solution.py:439
  181.8 7.6 %all-to-all-done.11 = f32[8,1,16]{2,1,0:T(1,128)S(1)} async-done(((f32[8,1,16]{2,1,0:T(1,128)}), f32[8,1,16]{2,1,0:T(1,128)S(1)}, u32[]{:S(2)}, u32[]{:S(2)}) %all-to-all-start.11) | async-done | bytes 544 | tf_op jit(solution)/shard_map/all_to_all | solution.py:439
  (76 shorter events, 23.9 us)
Async XLA Ops:
  0.6 49.5 %copy-start.6 = (f32[2,256,256]{2,1,0:T(8,128)S(1)}, f32[2,256,256]{2,1,0:T(8,128)}, u32[]{:S(2)}) copy-start(f32[2,256,256]{2,1,0:T(8,128)} %inverse_ref.5) | copy-start | bytes 1572868
  3.3 15.8 %all-to-all-start.1 = ((s32[16,1,128]{2,1,0:T(1,128)}), s32[16,1,128]{2,1,0:T(1,128)S(1)}, u32[]{:S(2)}, u32[]{:S(2)}) async-start(s32[16,1,128]{2,1,0:T(1,128)} %bitcast.3), calls=%async_computation.1 | async-start | bytes 16384 | tf_op jit(solution)/shard_map/all_to_all | solution.py:477
  9.8 0.8 copy-start.7
  10.6 0.9 copy-start.9
  12.2 38.0 %copy-start.11 = (f32[8,448]{1,0:T(8,128)S(1)}, f32[8,448]{1,0:T(8,128)}, u32[]{:S(2)}) copy-start(f32[8,448]{1,0:T(8,128)} %beta_ref.1) | copy-start | bytes 43012
  12.2 43.1 %copy-start.10 = (s32[16,2048]{1,0:T(8,128)S(1)}, s32[16,2048]{1,0:T(8,128)}, u32[]{:S(2)}) copy-start(s32[16,2048]{1,0:T(8,128)} %index_ref.3) | copy-start | bytes 393220
  12.2 43.1 %copy-start.13 = (f32[16]{0:T(128)S(1)}, f32[16]{0:T(128)}, u32[]{:S(2)}) copy-start(f32[16]{0:T(128)} %table_ref.3) | copy-start | bytes 196
  39.2 10.9 %all-to-all-start.2 = ((f32[16,4,128]{2,1,0:T(4,128)}), f32[16,4,128]{2,1,0:T(4,128)S(1)}, u32[]{:S(2)}, u32[]{:S(2)}) async-start(f32[16,4,128]{2,1,0:T(4,128)} %bitcast.6), calls=%async_computation.2 | async-start | bytes 65536 | tf_op jit(solution)/shard_map/all_to_all | solution.py:446
  51.8 17.9 %all-to-all-start.3 = ((f32[16,4,128]{2,1,0:T(4,128)}), f32[16,4,128]{2,1,0:T(4,128)S(1)}, u32[]{:S(2)}, u32[]{:S(2)}) async-start(f32[16,4,128]{2,1,0:T(4,128)} %bitcast.8), calls=%async_computation.3 | async-start | bytes 65536 | tf_op jit(solution)/shard_map/all_to_all | solution.py:446
  55.3 33.6 %copy-start.8 = (f32[8,2048]{1,0:T(8,128)S(1)}, f32[8,2048]{1,0:T(8,128)}, u32[]{:S(2)}) copy-start(f32[8,2048]{1,0:T(8,128)} %resid_ref.3) | copy-start | bytes 196612
  67.7 1.9 %copy-start = (bf16[2048,1024]{1,0:T(8,128)(2,1)}, bf16[2048,1024]{1,0:T(8,128)(2,1)S(1)}, u32[]{:S(2)}) copy-start(bf16[2048,1024]{1,0:T(8,128)(2,1)S(1)} %select.41.columns_ref) | copy-start | bytes 12582916
  69.7 2.2 %copy-start.1 = (bf16[2048,1024]{1,0:T(8,128)(2,1)S(1)}, bf16[2048,1024]{1,0:T(8,128)(2,1)}, u32[]{:S(2)}) copy-start(bf16[2048,1024]{1,0:T(8,128)(2,1)} %copy-done) | copy-start | bytes 12582916
  73.4 1.3 collective-permute-start
  87.7 1.3 collective-permute-start.1
  89.0 2.2 %copy-start.2 = (bf16[2048,1024]{1,0:T(8,128)(2,1)S(1)}, bf16[2048,1024]{1,0:T(8,128)(2,1)}, u32[]{:S(2)}) copy-start(bf16[2048,1024]{1,0:T(8,128)(2,1)} %copy-done) | copy-start | bytes 12582916
  91.2 26.4 %copy-start.3 = (bf16[2048,1024]{1,0:T(8,128)(2,1)S(1)}, bf16[2048,1024]{1,0:T(8,128)(2,1)}, u32[]{:S(2)}) copy-start(bf16[2048,1024]{1,0:T(8,128)(2,1)} %copy-done) | copy-start | bytes 12582916
  119.2 1.3 collective-permute-start.2
  130.6 1.3 collective-permute-start.3
  132.0 2.2 %copy-start.4 = (bf16[2048,1024]{1,0:T(8,128)(2,1)S(1)}, bf16[2048,1024]{1,0:T(8,128)(2,1)}, u32[]{:S(2)}) copy-start(bf16[2048,1024]{1,0:T(8,128)(2,1)} %copy-done) | copy-start | bytes 12582916
  134.2 27.2 %copy-start.5 = (bf16[2048,1024]{1,0:T(8,128)(2,1)S(1)}, bf16[2048,1024]{1,0:T(8,128)(2,1)}, u32[]{:S(2)}) copy-start(bf16[2048,1024]{1,0:T(8,128)(2,1)} %copy-done) | copy-start | bytes 12582916
  163.0 1.3 collective-permute-start.4
  165.0 11.1 %all-to-all-start.10 = ((f32[8,8,1024]{2,1,0:T(8,128)}), f32[8,8,1024]{2,1,0:T(8,128)S(1)}, u32[]{:S(2)}, u32[]{:S(2)}) async-start(f32[8,8,1024]{2,1,0:T(8,128)} %broadcast_in_dim.13), calls=%async_computation.10 | async-start | bytes 524288 | tf_op jit(solution)/shard_map/all_to_all | solution.py:439
  176.1 1.3 collective-permute-start.5
  178.2 11.2 %all-to-all-start.11 = ((f32[8,1,16]{2,1,0:T(1,128)}), f32[8,1,16]{2,1,0:T(1,128)S(1)}, u32[]{:S(2)}, u32[]{:S(2)}) async-start(f32[8,1,16]{2,1,0:T(1,128)} %broadcast_in_dim.14), calls=%async_computation.11 | async-start | bytes 8192 | tf_op jit(solution)/shard_map/all_to_all | solution.py:439
  (1 other events, 0.7 us)

commit v2 on v1

v2 whole, which is shorter than its diff:
```python
import functools
import math

import jax
import jax.numpy as jnp
from jax import lax
from jax.experimental import pallas as pl
from jax.experimental.pallas import tpu as pltpu
from jax.sharding import Mesh
from jax.sharding import PartitionSpec as P

PASSES = 3
VAR = ("y_lo", "z", "core")
SAMP = ("y_hi", "x")
CHIPS = ("y_lo", "z")

CAP = 64
LANES = 128
ROWS = 256
HALF = 4

penalty = 0.5
epsilon = 1e-06
SMALL = pltpu.CompilerParams(vmem_limit_bytes=12 * 1024 * 1024)
MEDIUM = pltpu.CompilerParams(vmem_limit_bytes=46 * 1024 * 1024)
LARGE = pltpu.CompilerParams(vmem_limit_bytes=60 * 1024 * 1024)
f32 = jnp.float32
bf16 = jnp.bfloat16


def iota(shape, dim):
    return lax.broadcasted_iota(jnp.int32, shape, dim)


def dot(a, b, **kw):
    return jnp.dot(a, b, preferred_element_type=f32, **kw)


def dot_t(a, b, **kw):
    return lax.dot_general(a, b, (((1,), (1,)), ((), ())), preferred_element_type=f32, **kw)


def thirds(x):
    high = x.astype(bf16)
    rest = x - high.astype(f32)
    mid = rest.astype(bf16)
    return high, mid, (rest - mid.astype(f32)).astype(bf16)


def swapped(x):
    here = (iota(x.shape, 0) // HALF) == (iota(x.shape, 1) // CAP)
    return jnp.where(here, x, pltpu.roll(pltpu.roll(x, HALF, 0), CAP, 1))


def column_row(packed):
    low = iota((1, LANES), 1) < CAP
    return jnp.concatenate(
        [
            jnp.where(low, packed[t : t + 1], packed[t + 1 : t + 2])
            for t in range(0, packed.shape[0], 2)
        ],
        1,
    )


def slot_maps(serial, holder, holders):
    fit = serial.shape[1]
    serial2 = jnp.concatenate([serial, serial], 1)
    holder2 = jnp.concatenate([holder, holder], 1)
    shape = (2 * CAP, 2 * fit)
    rows, cols = iota(shape, 0), iota(shape, 1)
    spread = ((rows // CAP) == (cols // fit)) & ((rows % CAP) == serial2)
    mask = (iota((holders * HALF, 2 * fit), 0) // HALF) == holder2
    return spread.astype(f32).astype(bf16), mask.astype(f32)


def layout_kernel(
    width,
    place_ref,
    active_ref,
    admit_ref,
    holder_ref,
    serial_ref,
    packed_ref,
    rank_ref,
    core_ref,
    ids_ref,
):
    rank_ref[...] = jnp.full(rank_ref.shape, place_ref[0], jnp.int32)
    core_ref[...] = jnp.full(core_ref.shape, place_ref[1], jnp.int32)
    holders = packed_ref.shape[0]
    fit = holder_ref.shape[1]
    active = active_ref.shape[1]
    ids_ref[:, :active] = active_ref[...]
    ids_ref[:, active:] = admit_ref[...]
    ids = ids_ref[...]
    holder = ids // width
    holder_ref[...] = holder
    marks = (iota((holders, fit), 0) == holder).astype(f32)
    earlier = (iota((fit, fit), 0) < iota((fit, fit), 1)).astype(f32).astype(bf16)
    before = dot(marks.astype(bf16), earlier)
    serial = jnp.sum(before * marks, 0, keepdims=True).astype(jnp.int32)
    serial_ref[...] = serial
    spread, _ = slot_maps(serial, holder, holders)
    marks2 = jnp.concatenate([marks, marks], 1)
    column = ids - holder * width + 1
    parts = []
    for piece in (column // LANES, column % LANES):
        row = piece.astype(f32)
        row = jnp.concatenate([row, row], 1)
        parts.append(dot_t((marks2 * row).astype(bf16), spread))
    packed_ref[...] = (parts[0] * LANES + parts[1]).astype(jnp.int32)


def layout(place, active_ids, admit_ids, width, holders):
    row = jax.ShapeDtypeStruct((1, active_ids.size + admit_ids.size), jnp.int32)
    tile = jax.ShapeDtypeStruct((2 * HALF, LANES), jnp.int32)
    vmem = pl.BlockSpec(memory_space=pltpu.VMEM)
    return pl.pallas_call(
        functools.partial(layout_kernel, width),
        in_specs=[pl.BlockSpec(memory_space=pltpu.SMEM), vmem, vmem],
        out_shape=(row, row, jax.ShapeDtypeStruct((holders, LANES), jnp.int32), tile, tile),
        scratch_shapes=[pltpu.VMEM(row.shape, jnp.int32)],
        compiler_params=LARGE,
        name="layout",
    )(place, active_ids[None], admit_ids[None])


def look_up(table_ref, index_ref, scales_ref):
    index = index_ref[...]
    scales = jnp.full(index.shape, table_ref[0], f32)
    for level in range(1, table_ref.shape[0]):
        scales = jnp.where(index == level, table_ref[level], scales)
    scales_ref[...] = scales


def dequantized(geno_ref, scales_ref, step):
    rows = geno_ref.shape[0]
    group = 128
    out = []
    for g in range(rows // group):
        scale = scales_ref[pl.ds(step * (rows // group) + g, 1), :]
        wide = geno_ref[g * group : (g + 1) * group, :].astype(f32) * scale
        out.append(wide.astype(bf16))
    return jnp.concatenate(out, 0)


def screen_kernel(table_ref, geno_ref, index_ref, resid_ref, out_ref, scales_ref, acc_ref):
    step = pl.program_id(0)

    @pl.when(step == 0)
    def _():
        look_up(table_ref, index_ref, scales_ref)
        acc_ref[...] = jnp.zeros_like(acc_ref)

    acc_ref[...] += dot(resid_ref[...].astype(bf16), dequantized(geno_ref, scales_ref, step))

    @pl.when(step == pl.num_programs(0) - 1)
    def _():
        out_ref[...] = jnp.broadcast_to(acc_ref[...][None], out_ref.shape)


def screen(table, geno, index, resid, copies):
    samples, width = geno.shape
    phenos = resid.shape[0]
    return pl.pallas_call(
        screen_kernel,
        grid=(samples // ROWS,),
        in_specs=[
            pl.BlockSpec(memory_space=pltpu.SMEM),
            pl.BlockSpec((ROWS, width), lambda i: (i, 0)),
            pl.BlockSpec(index.shape, lambda i: (0, 0)),
            pl.BlockSpec((phenos, ROWS), lambda i: (0, i)),
        ],
        out_specs=pl.BlockSpec((copies, phenos, width), lambda i: (0, 0, 0)),
        out_shape=jax.ShapeDtypeStruct((copies, phenos, width), f32),
        scratch_shapes=[pltpu.VMEM(index.shape, f32), pltpu.VMEM((phenos, width), f32)],
        compiler_params=LARGE,
        cost_estimate=pl.CostEstimate(
            flops=2 * phenos * samples * width, bytes_accessed=2 * samples * width, transcendentals=0
        ),
        name="screen",
    )(table, geno, index, resid)


def select_kernel(table_ref, packed_ref, geno_ref, index_ref, out_ref, scales_ref, pick_ref):
    step = pl.program_id(0)

    @pl.when(step == 0)
    def _():
        look_up(table_ref, index_ref, scales_ref)
        wanted = column_row(packed_ref[...])

        @pl.loop(0, pick_ref.shape[0], step=ROWS)
        def _(at):
            here = iota((ROWS, pick_ref.shape[1]), 0) + (at + 1) == wanted
            pick_ref[pl.ds(pl.multiple_of(at, ROWS), ROWS), :] = here.astype(f32).astype(bf16)

    out_ref[...] = dot(dequantized(geno_ref, scales_ref, step), pick_ref[...]).astype(bf16)


def select(table, packed, geno, index):
    samples, width = geno.shape
    held = packed.shape[0] * CAP
    rows = 2 * ROWS
    return pl.pallas_call(
        select_kernel,
        grid=(samples // rows,),
        in_specs=[
            pl.BlockSpec(memory_space=pltpu.SMEM),
            pl.BlockSpec(packed.shape, lambda i: (0, 0)),
            pl.BlockSpec((rows, width), lambda i: (i, 0)),
            pl.BlockSpec(index.shape, lambda i: (0, 0)),
        ],
        out_specs=pl.BlockSpec((rows, held), lambda i: (i, 0)),
        out_shape=jax.ShapeDtypeStruct((samples, held), bf16),
        scratch_shapes=[pltpu.VMEM(index.shape, f32), pltpu.VMEM((width, held), bf16)],
        compiler_params=LARGE,
        cost_estimate=pl.CostEstimate(
            flops=2 * samples * width * held, bytes_accessed=2 * samples * width, transcendentals=0
        ),
        name="select",
    )(table, packed, geno, index)


def pick_kernel(inv_root, parts_ref, packed_hbm, scores_ref, pay_ref, packed_ref, sem):
    copy = pltpu.make_async_copy(packed_hbm, packed_ref, sem)
    copy.start()
    scores = parts_ref[0]
    for j in range(1, parts_ref.shape[0]):
        scores = scores + parts_ref[j]
    scores = scores * inv_root
    scores_ref[...] = scores
    copy.wait()
    wanted = column_row(packed_ref[...])
    stacked = jnp.concatenate(thirds(scores), 0)
    phenos, width = scores.shape
    total = jnp.zeros((stacked.shape[0], wanted.shape[1]), f32)
    for at in range(0, width, ROWS):
        here = iota((ROWS, wanted.shape[1]), 0) + (at + 1) == wanted
        total += dot(stacked[:, at : at + ROWS], here.astype(f32).astype(bf16))
    held = total[:phenos] + total[phenos : 2 * phenos] + total[2 * phenos :]
    for t in range(wanted.shape[1] // LANES):
        pay_ref[8 * t : 8 * t + 8, :] = swapped(held[:, t * LANES : (t + 1) * LANES])


def pick(parts, packed, inv_root):
    return pl.pallas_call(
        functools.partial(pick_kernel, inv_root),
        in_specs=[pl.BlockSpec(memory_space=pltpu.VMEM), pl.BlockSpec(memory_space=pltpu.HBM)],
        scratch_shapes=[pltpu.VMEM(packed.shape, packed.dtype), pltpu.SemaphoreType.DMA],
        out_shape=(
            jax.ShapeDtypeStruct(parts.shape[1:], f32),
            jax.ShapeDtypeStruct((packed.shape[0] * HALF, LANES), f32),
        ),
        compiler_params=SMALL,
        name="pick",
    )(parts, packed)


def direction_step(data, serial_ref, holder_ref, inverse_ref, advance, wide_ref, d_ref, pay_ref):
    fit = serial_ref.shape[1]
    holders = data.shape[0] // HALF
    spread, mask = slot_maps(serial_ref[...], holder_ref[...], holders)
    high, mid, low = thirds(data)
    placed = (dot(high, spread) + dot(mid, spread) + dot(low, spread)) * mask
    placed = jnp.sum(placed.reshape(-1, 2 * HALF, 2 * fit), 0)
    arrived = placed[:HALF] + placed[HALF:]
    inner = advance(arrived)
    wide_ref[:HALF, :] = inner[:, :fit]
    wide_ref[HALF:, :] = inner[:, fit:]
    blocks, size = inverse_ref.shape[0], inverse_ref.shape[1]
    for b in range(blocks):
        moved = dot_t(
            wide_ref[:, b * size : (b + 1) * size], inverse_ref[b], precision=lax.Precision.HIGHEST
        )
        moved = moved.astype(bf16).astype(f32)
        d_ref[:, b * size : (b + 1) * size] = moved[:HALF]
        d_ref[:, fit + b * size : fit + (b + 1) * size] = moved[HALF:]
    d = d_ref[...]
    d = jnp.concatenate([d, d], 0)
    d = jnp.broadcast_to(d[None], (holders * HALF // d.shape[0], *d.shape)).reshape(mask.shape)
    pay_ref[...] = dot_t((d * mask).astype(bf16), spread)


def first_owner_kernel(
    data_ref,
    serial_ref,
    holder_ref,
    inverse_ref,
    beta_ref,
    columns_hbm,
    pay_ref,
    g_ref,
    b_ref,
    d_ref,
    columns_ref,
    wide_ref,
    sem,
):
    copy = pltpu.make_async_copy(columns_hbm, columns_ref, sem)
    copy.start()
    fit = serial_ref.shape[1]
    active = beta_ref.shape[1]
    b_ref[...] = jnp.zeros_like(b_ref)
    b_ref[:, :active] = beta_ref[:HALF]
    b_ref[:, fit : fit + active] = beta_ref[HALF:]

    def advance(arrived):
        g_ref[...] = arrived
        return arrived - penalty * b_ref[...]

    direction_step(
        data_ref[...], serial_ref, holder_ref, inverse_ref, advance, wide_ref, d_ref, pay_ref
    )
    copy.wait()


def owner_kernel(
    data_ref,
    serial_ref,
    holder_ref,
    inverse_ref,
    g_in,
    b_in,
    d_in,
    resid_in,
    update_ref,
    pay_ref,
    g_ref,
    b_ref,
    d_ref,
    resid_ref,
    wide_ref,
    sum_ref,
    rows_ref,
    scalar_ref,
):
    fit = serial_ref.shape[1]
    chunk = sum_ref.shape[0]
    total = data_ref[:chunk, :]
    for at in range(chunk, data_ref.shape[0], chunk):
        total = total + data_ref[at : at + chunk, :]
    sum_ref[...] = total
    for k in range(chunk // (HALF + 1)):
        at = k * (HALF + 1)
        rows_ref[k * HALF : (k + 1) * HALF, :] = sum_ref[at : at + HALF, :]
        if k < scalar_ref.shape[0]:
            scalar_ref[k : k + 1, :] = sum_ref[at + HALF : at + HALF + 1, :]
    factor = scalar_ref[:, :1] / (scalar_ref[:, CAP : CAP + 1] + epsilon)
    resid_ref[...] = resid_in[...] - factor * update_ref[...]
    low = iota((HALF, 2 * fit), 1) < fit
    factor = jnp.where(low, factor[:HALF], factor[HALF:])

    def advance(arrived):
        g_ref[...] = g_in[...] - factor * arrived
        b_ref[...] = b_in[...] + factor * d_in[...]
        return g_ref[...] - penalty * b_ref[...]

    direction_step(
        rows_ref[...], serial_ref, holder_ref, inverse_ref, advance, wide_ref, d_ref, pay_ref
    )


def owner(data, serial, holder, inverse, state):
    fit = serial.shape[1]
    phenos = 2 * HALF
    held = jax.ShapeDtypeStruct((HALF, 2 * fit), f32)
    wide = pltpu.VMEM((phenos, fit), f32)
    if len(state) == 2:
        vmem = pl.BlockSpec(memory_space=pltpu.VMEM)
        columns = state[1]
        return pl.pallas_call(
            first_owner_kernel,
            in_specs=[vmem] * 5 + [pl.BlockSpec(memory_space=pltpu.HBM)],
            out_specs=(vmem,) * 5,
            out_shape=(
                jax.ShapeDtypeStruct(data.shape, f32),
                held,
                held,
                held,
                jax.ShapeDtypeStruct(columns.shape, columns.dtype),
            ),
            scratch_shapes=[wide, pltpu.SemaphoreType.DMA],
            compiler_params=MEDIUM,
            name="owner_first",
        )(data, serial, holder, inverse, *state)
    holders = lax.axis_size(VAR)
    return pl.pallas_call(
        owner_kernel,
        out_shape=(
            jax.ShapeDtypeStruct((holders * HALF, LANES), f32),
            held,
            held,
            held,
            jax.ShapeDtypeStruct(state[3].shape, f32),
        ),
        scratch_shapes=[
            wide,
            pltpu.VMEM((holders * (HALF + 1), LANES), f32),
            pltpu.VMEM((holders * HALF, LANES), f32),
            pltpu.VMEM((phenos, LANES), f32),
        ],
        compiler_params=SMALL,
        name="owner_next",
    )(data, serial, holder, inverse, *state)


def update_kernel(core_ref, pay_ref, columns_ref, keep_ref, send_ref):
    packed = jnp.concatenate(
        [swapped(pay_ref[at : at + 8, :]) for at in range(0, pay_ref.shape[0], 8)], 1
    ).astype(bf16)
    first = core_ref[:, :1] == 0
    half = keep_ref.shape[1]
    for at in range(0, half, ROWS):
        a = dot_t(packed, columns_ref[at : at + ROWS, :])
        b = dot_t(packed, columns_ref[half + at : half + at + ROWS, :])
        keep_ref[:, at : at + ROWS] = jnp.where(first, a, b)
        send_ref[:, at : at + ROWS] = jnp.where(first, b, a)


def partial_update(core, pay, columns):
    half = jax.ShapeDtypeStruct((2 * HALF, columns.shape[0] // 2), f32)
    return pl.pallas_call(
        update_kernel,
        out_shape=(half, half),
        compiler_params=SMALL,
        name="update",
    )(core, pay, columns)


def spread_kernel(keep_ref, arrived_ref, out_ref):
    out_ref[...] = jnp.broadcast_to((keep_ref[...] + arrived_ref[...])[None], out_ref.shape)


def spread(keep, arrived, copies):
    return pl.pallas_call(
        spread_kernel,
        out_shape=jax.ShapeDtypeStruct((copies, *keep.shape), f32),
        compiler_params=SMALL,
        name="spread",
    )(keep, arrived)


def total_kernel(parts_ref, out_ref):
    total = parts_ref[0]
    for n in range(1, parts_ref.shape[0]):
        total = total + parts_ref[n]
    out_ref[...] = total


def total(parts):
    return pl.pallas_call(
        total_kernel,
        out_shape=jax.ShapeDtypeStruct(parts.shape[1:], f32),
        compiler_params=SMALL,
        name="total",
    )(parts)


def whole_update(inv_root, core_ref, mine_ref, other_ref):
    first = core_ref[:, :1] == 0
    mine, other = mine_ref[...] * inv_root, other_ref[...] * inv_root
    return jnp.concatenate([jnp.where(first, mine, other), jnp.where(first, other, mine)], 1)


def step_sums(resid, update):
    cross = jnp.sum(resid * update, 1, keepdims=True)
    square = jnp.sum(update * update, 1, keepdims=True)
    return jnp.where(iota((update.shape[0], LANES), 1) < CAP, cross, square)


def descent_kernel(
    inv_root, rank_ref, core_ref, mine_ref, other_ref, resid_ref, columns_ref, out_ref, update_ref
):
    update = whole_update(inv_root, core_ref, mine_ref, other_ref)
    update_ref[...] = update
    phenos = update.shape[0]
    high = update.astype(bf16)
    low = (update - high.astype(f32)).astype(bf16)
    grad = dot(jnp.concatenate([high, low], 0), columns_ref[...])
    grad = (grad[:phenos] + grad[phenos:]) * inv_root
    both = step_sums(resid_ref[...], update)
    mine = iota(both.shape, 0) == lax.rem(rank_ref[...], phenos)
    row = jnp.sum(jnp.where(mine, both, 0.0), 0, keepdims=True)
    chunk = HALF + 1
    owners = grad.shape[1] // CAP
    copies = out_ref.shape[0] // (chunk * owners)
    for t in range(owners // 2):
        pair = swapped(grad[:, t * LANES : (t + 1) * LANES])
        for n in range(copies):
            at = (n * owners + 2 * t) * chunk
            out_ref[at : at + HALF, :] = pair[:HALF]
            out_ref[at + HALF : at + HALF + 1, :] = row
            out_ref[at + chunk : at + chunk + HALF, :] = pair[HALF:]
            out_ref[at + chunk + HALF : at + 2 * chunk, :] = row


def descent(rank, core, mine, other, resid, columns, inv_root, copies):
    out = (copies * (columns.shape[1] // CAP) * (HALF + 1), LANES)
    return pl.pallas_call(
        functools.partial(descent_kernel, inv_root),
        out_shape=(jax.ShapeDtypeStruct(out, f32), jax.ShapeDtypeStruct(resid.shape, f32)),
        compiler_params=SMALL,
        name="descent",
    )(rank, core, mine, other, resid, columns)


def settle_kernel(inv_root, core_ref, mine_ref, other_ref, resid_ref, sums_ref, update_ref):
    update = whole_update(inv_root, core_ref, mine_ref, other_ref)
    update_ref[...] = update
    sums_ref[...] = jnp.broadcast_to(step_sums(resid_ref[...], update)[None], sums_ref.shape)


def settle(core, mine, other, resid, inv_root, copies):
    return pl.pallas_call(
        functools.partial(settle_kernel, inv_root),
        out_shape=(
            jax.ShapeDtypeStruct((copies, resid.shape[0], LANES), f32),
            jax.ShapeDtypeStruct(resid.shape, f32),
        ),
        compiler_params=SMALL,
        name="settle",
    )(core, mine, other, resid)


def last_kernel(sums_ref, b_ref, d_ref, resid_ref, update_ref, coeffs_ref, out_ref):
    phenos, fit = coeffs_ref.shape
    total = sums_ref[0]
    for j in range(1, sums_ref.shape[0]):
        total = total + sums_ref[j]
    factor = total[:, :1] / (total[:, CAP : CAP + 1] + epsilon)
    for half in range(2):
        rows = slice(half * HALF, (half + 1) * HALF)
        cols = slice(half * fit, (half + 1) * fit)
        coeffs_ref[rows, :] = b_ref[:, cols] + factor[rows] * d_ref[:, cols]
    out_ref[...] = resid_ref[...] - factor * update_ref[...]


def last(sums, coeffs, direction, resid, update):
    phenos = resid.shape[0]
    return pl.pallas_call(
        last_kernel,
        out_shape=(
            jax.ShapeDtypeStruct((phenos, coeffs.shape[1] // 2), f32),
            jax.ShapeDtypeStruct(resid.shape, f32),
        ),
        compiler_params=SMALL,
        name="last",
    )(sums, coeffs, direction, resid, update)


def exchange(pay, axes):
    count = lax.axis_size(axes)
    rows = pay.shape[0] // count
    shape = (count, rows, LANES) if rows == HALF else (count, 1, rows * LANES)
    return lax.all_to_all(
        pay.reshape(shape), axes, split_axis=0, concat_axis=0, tiled=True
    ).reshape(pay.shape)


def other_core(x):
    return lax.ppermute(x, "core", [(0, 1), (1, 0)])


def on_device(
    geno, scale_index, scale_table, residual, beta_active, block_inverse, active_ids, admit_ids
):
    holders = lax.axis_size(VAR)
    place = jnp.stack([lax.axis_index(VAR), lax.axis_index("core")]).astype(jnp.int32)
    samples, width = geno.shape
    copies = lax.axis_size(SAMP)
    inv_root = 1.0 / math.sqrt(samples * copies)

    holder, serial, packed, rank, core = layout(place, active_ids, admit_ids, width, holders)
    packed = lax.all_to_all(
        packed.reshape(holders, 1, LANES), VAR, split_axis=0, concat_axis=0, tiled=True
    ).reshape(holders, LANES)

    parts = screen(scale_table, geno, scale_index, residual, copies)
    parts = lax.all_to_all(parts, SAMP, split_axis=0, concat_axis=0, tiled=True)
    columns = select(scale_table, packed, geno, scale_index)
    parts, columns = lax.optimization_barrier((parts, columns))
    scores, pay = pick(parts, packed, inv_root)

    pay, *state, columns = owner(
        exchange(pay, VAR), serial, holder, block_inverse, (beta_active, columns)
    )
    current = residual
    for pass_index in range(PASSES):
        keep, send = partial_update(core, exchange(pay, VAR), columns)
        mine = spread(keep, other_core(send), lax.axis_size(CHIPS))
        mine = total(lax.all_to_all(mine, CHIPS, split_axis=0, concat_axis=0, tiled=True))
        other = other_core(mine)
        if pass_index + 1 == PASSES:
            break
        data, update = descent(rank, core, mine, other, current, columns, inv_root, copies)
        pay, *state, current = owner(
            exchange(data, SAMP + VAR), serial, holder, block_inverse, (*state, current, update)
        )

    _, coeffs, direction = state
    sums, update = settle(core, mine, other, current, inv_root, copies)
    sums = lax.all_to_all(sums, SAMP, split_axis=0, concat_axis=0, tiled=True)
    return (scores, *last(sums, coeffs, direction, current, update))


def solution(mesh):
    torus = Mesh(mesh.devices.reshape(2, 4, 2, 2, 4), VAR + SAMP)
    placed = (
        P(SAMP, VAR),
        P(SAMP, VAR),
        P(),
        P(None, SAMP),
        P(None, VAR),
        P(VAR, None, None),
        P(VAR),
        P(VAR),
    )
    return jax.shard_map(
        on_device,
        mesh=torus,
        in_specs=placed,
        out_specs=(P(None, VAR), P(None, VAR), P(None, SAMP)),
        check_vma=False,
    )
```

time: 192 us -> 173 us (0.901)
  blocking collectives: 90.6 us -> 115 us
  waiting for transfers between devices: 27.8 us -> 6.86 us
  local copies, waits for them, and re-layouts: 12.3 us -> 0.73 us
  starting transfers between devices: 22.8 us -> 13.8 us
  other arithmetic: 3.82 us -> 0.59 us
    all_to_all x4 -> x6, blocking collectives: 48.9 us -> 73.1 us  [exchange(): lax.all_to_all(pay.reshape(shape), axes, split_axis=0, concat_axis=0, til...]
    all_to_all x4 -> x1, waiting for transfers between devices: 21.3 us -> 0.01 us  [on_device(): parts = lax.all_to_all(parts, SAMP, split_axis=0, concat_axis=0, tiled=True)]
    unnamed x28 -> x18, local copies, waits for them, and re-layouts: 10.9 us -> 0.73 us
    all_to_all x4 -> x1, starting transfers between devices: 15.3 us -> 6.65 us  [on_device(): parts = lax.all_to_all(parts, SAMP, split_axis=0, concat_axis=0, tiled=True)]
    pallas_call x9 -> x17, Pallas kernels: 23.5 us -> 24.2 us  [the longest x1 13 us: select(): pl.pallas_call(select_kernel, grid=(samples // rows,), in_specs=[pl.Block...]
    all_to_all x3 -> x4, blocking collectives: 41.6 us -> 41.5 us  [the longest x3 30.4 us: on_device(): lax.all_to_all(mine, CHIPS, split_axis=0, concat_axis=0, tiled=True)]
  transfers between devices with their start and end apart: 11 -> 8, of which waited for: 9 -> 6; matrix products, arithmetic and copies ran while one was open for 0% -> 0% of each run, Pallas kernels for 10% -> 12%
where the time goes in v2:
time: 173 us; the launch traced here: 172 us
  blocking collectives  115 us (66%)
  Pallas kernels  34.3 us (20%)
  starting transfers between devices  13.8 us (8%)
  waiting for transfers between devices  6.86 us (4%)
    all_to_all x6, blocking collectives, exchange(): lax.all_to_all(pay.reshape(shape), axes, split_axis=0, concat_axis=0, til...  73.1 us
    all_to_all x3, blocking collectives, on_device(): lax.all_to_all(mine, CHIPS, split_axis=0, concat_axis=0, tiled=True)  30.4 us
    pallas_call x1, Pallas kernels, select(): pl.pallas_call(select_kernel, grid=(samples // rows,), in_specs=[pl.Block...  13 us
    all_to_all x1, blocking collectives, on_device(): sums = lax.all_to_all(sums, SAMP, split_axis=0, concat_axis=0, tiled=True)  11.2 us
    pallas_call x1, Pallas kernels, screen(): pl.pallas_call(screen_kernel, grid=(samples // ROWS,), in_specs=[pl.Block...  7.69 us
    ppermute x6, waiting for transfers between devices, other_core(): return lax.ppermute(x, 'core', [(0, 1), (1, 0)])  6.86 us
    all_to_all x1, starting transfers between devices, on_device(): parts = lax.all_to_all(parts, SAMP, split_axis=0, concat_axis=0, tiled=True)  6.65 us
    all_to_all x1, starting transfers between devices, on_device(): lax.all_to_all(packed.reshape(holders, 1, LANES), VAR, split_axis=0, conc...  6.51 us
  transfers between devices with their start and end apart: 8, of which 6 were waited for; matrix products, arithmetic and copies ran while one was open for 0% of the time, Pallas kernels for 12%

profile of v2, /device:TPU:0, one launch (start us, length us, event | category | flops | bytes accessed | tf_op | source)
XLA Modules:
  0.0 171.8 jit_solution(7156524327215135556)
XLA Ops:
  1.2 1.8 %layout.1 = (s32[1,512]{1,0:T(1,128)}, s32[1,512]{1,0:T(1,128)}, s32[16,128]{1,0:T(8,128)}, s32[8,128]{1,0:T(8,128)}, s32[8,128]{1,0:T(8,128)}) custom-call(s32[2]{0:T(128)} %pad_add_fusion.place_ref, s32[1,448]{1,0:T(1,128)} %bitcast.35, s32[1,64]{1,0:T(1,128)} %bitcast.36), custom_call_target="tpu_custom_call" | custom-call | tf_op jit(solution)/shard_map/layout/pallas_call | solution.py:119
  3.0 6.5 %all-to-all-start.1 = ((s32[16,1,128]{2,1,0:T(1,128)}), s32[16,1,128]{2,1,0:T(1,128)S(1)}, u32[]{:S(2)}, u32[]{:S(2)}) async-start(s32[16,1,128]{2,1,0:T(1,128)} %bitcast.34), calls=%async_computation.1 | async-start | bytes 16384 | tf_op jit(solution)/shard_map/all_to_all | solution.py:576
  9.5 7.7 %screen.1 = f32[8,8,2048]{2,1,0:T(8,128)} custom-call(f32[16]{0:T(128)} %table_ref.3, bf16[2048,2048]{1,0:T(8,128)(2,1)} %geno_ref.3, s32[16,2048]{1,0:T(8,128)} %index_ref.3, f32[8,2048]{1,0:T(8,128)} %resid_in.1), custom_call_target="tpu_custom_call" | custom-call | flops 67108864 | bytes 8388608 | tf_op jit(solution)/shard_map/screen/pallas_call | solution.py:166
  17.2 6.6 %all-to-all-start = ((f32[8,8,2048]{2,1,0:T(8,128)}), f32[8,8,2048]{2,1,0:T(8,128)S(1)}, u32[]{:S(2)}, u32[]{:S(2)}) async-start(f32[8,8,2048]{2,1,0:T(8,128)} %screen.1), calls=%async_computation | async-start | bytes 1048576 | tf_op jit(solution)/shard_map/all_to_all | solution.py:581
  23.9 13.0 %select.1.columns_hbm = bf16[2048,1024]{1,0:T(8,128)(2,1)} custom-call(f32[16]{0:T(128)} %table_ref.3, s32[16,128]{1,0:T(8,128)} %bitcast.28, bf16[2048,2048]{1,0:T(8,128)(2,1)} %geno_ref.3, s32[16,2048]{1,0:T(8,128)} %index_ref.3), custom_call_target="tpu_custom_call" | custom-call | flops 8589934592 | bytes 8388608 | tf_op jit(solution)/shard_map/select/pallas_call | solution.py:206
  38.6 11.0 %all_to_all.60 = f32[16,4,128]{2,1,0:T(4,128)S(1)} all-to-all(f32[16,4,128]{2,1,0:T(4,128)S(1)} %bitcast.33), channel_id=1, replica_groups=mesh['y_lo'=2,'z'=4,'core'=2,'y_hi'=2,'x'=4] {'y_lo','z','core'}, dimensions={0} | all-to-all | bytes 65536 | tf_op jit(solution)/shard_map/all_to_all | solution.py:557
  49.6 2.2 %owner_first.1 = (f32[64,128]{1,0:T(8,128)S(1)}, f32[4,1024]{1,0:T(4,128)S(1)}, f32[4,1024]{1,0:T(4,128)S(1)}, f32[4,1024]{1,0:T(4,128)S(1)}, bf16[2048,1024]{1,0:T(8,128)(2,1)S(1)}) custom-call(f32[64,128]{1,0:T(8,128)S(1)} %bitcast.24, s32[1,512]{1,0:T(1,128)S(1)} %copy-done.6, s32[1,512]{1,0:T(1,128)S(1)} %copy-done.5, f32[2,256,256]{2,1,0:T(8,128)S(1)} %copy-done, ...), custom_call_target="tpu_custom_call" | custom-call | tf_op jit(solution)/shard_map/owner_first/pallas_call | solution.py:373
  51.9 8.7 %all_to_all.61 = f32[16,4,128]{2,1,0:T(4,128)S(1)} all-to-all(f32[16,4,128]{2,1,0:T(4,128)S(1)} %bitcast.32), channel_id=1, replica_groups=mesh['y_lo'=2,'z'=4,'core'=2,'y_hi'=2,'x'=4] {'y_lo','z','core'}, dimensions={0} | all-to-all | bytes 65536 | tf_op jit(solution)/shard_map/all_to_all | solution.py:557
  60.5 1.2 update.3
  61.9 1.1 collective-permute-done.arrived_ref
  63.0 10.1 %all_to_all.62.parts_ref = f32[8,8,1024]{2,1,0:T(8,128)S(1)} all-to-all(f32[8,8,1024]{2,1,0:T(8,128)S(1)} %spread.3), channel_id=1, replica_groups=mesh['y_lo'=2,'z'=4,'core'=2,'y_hi'=2,'x'=4] {'y_lo','z'}, dimensions={0} | all-to-all | bytes 524288 | tf_op jit(solution)/shard_map/all_to_all | solution.py:593
  73.2 1.2 collective-permute-done.1.other_ref
  75.2 20.2 %all_to_all.63 = f32[128,1,640]{2,1,0:T(1,128)S(1)} all-to-all(f32[128,1,640]{2,1,0:T(1,128)S(1)} %bitcast.23), channel_id=1, replica_groups=mesh['y_lo'=2,'z'=4,'core'=2,'y_hi'=2,'x'=4] {'y_hi','x','y_lo','z','core'}, dimensions={0} | all-to-all | bytes 655360 | tf_op jit(solution)/shard_map/all_to_all | solution.py:557
  96.4 8.7 %all_to_all.64 = f32[16,4,128]{2,1,0:T(4,128)S(1)} all-to-all(f32[16,4,128]{2,1,0:T(4,128)S(1)} %bitcast.31), channel_id=1, replica_groups=mesh['y_lo'=2,'z'=4,'core'=2,'y_hi'=2,'x'=4] {'y_lo','z','core'}, dimensions={0} | all-to-all | bytes 65536 | tf_op jit(solution)/shard_map/all_to_all | solution.py:557
  105.1 1.2 update.4
  107.5 10.1 %all_to_all.65.parts_ref = f32[8,8,1024]{2,1,0:T(8,128)S(1)} all-to-all(f32[8,8,1024]{2,1,0:T(8,128)S(1)} %spread.4), channel_id=1, replica_groups=mesh['y_lo'=2,'z'=4,'core'=2,'y_hi'=2,'x'=4] {'y_lo','z'}, dimensions={0} | all-to-all | bytes 524288 | tf_op jit(solution)/shard_map/all_to_all | solution.py:593
  117.7 1.2 collective-permute-done.3.other_ref
  119.7 16.0 %all_to_all.66 = f32[128,1,640]{2,1,0:T(1,128)S(1)} all-to-all(f32[128,1,640]{2,1,0:T(1,128)S(1)} %bitcast.22), channel_id=1, replica_groups=mesh['y_lo'=2,'z'=4,'core'=2,'y_hi'=2,'x'=4] {'y_hi','x','y_lo','z','core'}, dimensions={0} | all-to-all | bytes 655360 | tf_op jit(solution)/shard_map/all_to_all | solution.py:557
  135.7 1.4 owner_next.3
  137.2 8.6 %all_to_all.67 = f32[16,4,128]{2,1,0:T(4,128)S(1)} all-to-all(f32[16,4,128]{2,1,0:T(4,128)S(1)} %bitcast.30), channel_id=1, replica_groups=mesh['y_lo'=2,'z'=4,'core'=2,'y_hi'=2,'x'=4] {'y_lo','z','core'}, dimensions={0} | all-to-all | bytes 65536 | tf_op jit(solution)/shard_map/all_to_all | solution.py:557
  145.8 1.2 update.5
  148.3 10.1 %all_to_all.68.parts_ref = f32[8,8,1024]{2,1,0:T(8,128)S(1)} all-to-all(f32[8,8,1024]{2,1,0:T(8,128)S(1)} %spread.5), channel_id=1, replica_groups=mesh['y_lo'=2,'z'=4,'core'=2,'y_hi'=2,'x'=4] {'y_lo','z'}, dimensions={0} | all-to-all | bytes 524288 | tf_op jit(solution)/shard_map/all_to_all | solution.py:593
  158.5 1.2 collective-permute-done.5.other_ref
  159.9 11.2 %all_to_all.69.sums_ref = f32[8,8,128]{2,1,0:T(8,128)S(1)} all-to-all(f32[8,8,128]{2,1,0:T(8,128)S(1)} %get-tuple-element.71), channel_id=1, replica_groups=mesh['y_lo'=2,'z'=4,'core'=2,'y_hi'=2,'x'=4] {'y_hi','x'}, dimensions={0} | all-to-all | bytes 65536 | tf_op jit(solution)/shard_map/all_to_all | solution.py:604
  (41 shorter events, 8.8 us)
Async XLA Ops:
  3.0 14.2 %all-to-all-start.1 = ((s32[16,1,128]{2,1,0:T(1,128)}), s32[16,1,128]{2,1,0:T(1,128)S(1)}, u32[]{:S(2)}, u32[]{:S(2)}) async-start(s32[16,1,128]{2,1,0:T(1,128)} %bitcast.34), calls=%async_computation.1 | async-start | bytes 16384 | tf_op jit(solution)/shard_map/all_to_all | solution.py:576
  17.2 6.7 %copy-start.3 = (s32[16,1,128]{2,1,0:T(1,128)}, s32[16,1,128]{2,1,0:T(1,128)S(1)}, u32[]{:S(2)}) copy-start(s32[16,1,128]{2,1,0:T(1,128)S(1)} %all-to-all-done.1) | copy-start | bytes 24580
  17.2 19.7 %all-to-all-start = ((f32[8,8,2048]{2,1,0:T(8,128)}), f32[8,8,2048]{2,1,0:T(8,128)S(1)}, u32[]{:S(2)}, u32[]{:S(2)}) async-start(f32[8,8,2048]{2,1,0:T(8,128)} %screen.1), calls=%async_computation | async-start | bytes 1048576 | tf_op jit(solution)/shard_map/all_to_all | solution.py:581
  23.9 25.7 %copy-start = (f32[2,256,256]{2,1,0:T(8,128)S(1)}, f32[2,256,256]{2,1,0:T(8,128)}, u32[]{:S(2)}) copy-start(f32[2,256,256]{2,1,0:T(8,128)} %inverse_ref.5) | copy-start | bytes 1572868
  23.9 25.7 %copy-start.5 = (s32[1,512]{1,0:T(1,128)S(1)}, s32[1,512]{1,0:T(1,128)}, u32[]{:S(2)}) copy-start(s32[1,512]{1,0:T(1,128)} %get-tuple-element.47.holder_ref) | copy-start | bytes 6148
  23.9 25.7 %copy-start.6 = (s32[1,512]{1,0:T(1,128)S(1)}, s32[1,512]{1,0:T(1,128)}, u32[]{:S(2)}) copy-start(s32[1,512]{1,0:T(1,128)} %get-tuple-element.46.serial_ref) | copy-start | bytes 6148
  23.9 25.7 %copy-start.7 = (f32[8,448]{1,0:T(8,128)S(1)}, f32[8,448]{1,0:T(8,128)}, u32[]{:S(2)}) copy-start(f32[8,448]{1,0:T(8,128)} %beta_ref.1) | copy-start | bytes 43012
  36.9 23.6 %copy-start.2 = (s32[8,128]{1,0:T(8,128)S(1)}, s32[8,128]{1,0:T(8,128)}, u32[]{:S(2)}) copy-start(s32[8,128]{1,0:T(8,128)} %get-tuple-element.43.core_ref) | copy-start | bytes 12292
  36.9 0.7 copy-start.4
  49.6 24.8 %copy-start.1 = (f32[8,2048]{1,0:T(8,128)S(1)}, f32[8,2048]{1,0:T(8,128)}, u32[]{:S(2)}) copy-start(f32[8,2048]{1,0:T(8,128)} %resid_in.1) | copy-start | bytes 196612
  49.6 24.8 %copy-start.8 = (s32[8,128]{1,0:T(8,128)S(1)}, s32[8,128]{1,0:T(8,128)}, u32[]{:S(2)}) copy-start(s32[8,128]{1,0:T(8,128)} %get-tuple-element.44.rank_ref) | copy-start | bytes 12292
  61.7 1.2 collective-permute-start
  73.1 1.3 collective-permute-start.1
  106.2 1.2 collective-permute-start.2
  117.7 1.3 collective-permute-start.3
  147.0 1.2 collective-permute-start.4
  158.4 1.3 collective-permute-start.5

commit v3 on v2

--- a/solution.py
+++ b/solution.py
@@ -76,7 +76,6 @@
 
 def layout_kernel(
     width,
-    place_ref,
     active_ref,
     admit_ref,
     holder_ref,
@@ -86,8 +85,8 @@
     core_ref,
     ids_ref,
 ):
-    rank_ref[...] = jnp.full(rank_ref.shape, place_ref[0], jnp.int32)
-    core_ref[...] = jnp.full(core_ref.shape, place_ref[1], jnp.int32)
+    rank_ref[...] = jnp.full(rank_ref.shape, lax.axis_index(VAR), jnp.int32)
+    core_ref[...] = jnp.full(core_ref.shape, lax.axis_index("core"), jnp.int32)
     holders = packed_ref.shape[0]
     fit = holder_ref.shape[1]
     active = active_ref.shape[1]
@@ -112,18 +111,18 @@
     packed_ref[...] = (parts[0] * LANES + parts[1]).astype(jnp.int32)
 
 
-def layout(place, active_ids, admit_ids, width, holders):
+def layout(active_ids, admit_ids, width, holders):
     row = jax.ShapeDtypeStruct((1, active_ids.size + admit_ids.size), jnp.int32)
     tile = jax.ShapeDtypeStruct((2 * HALF, LANES), jnp.int32)
     vmem = pl.BlockSpec(memory_space=pltpu.VMEM)
     return pl.pallas_call(
         functools.partial(layout_kernel, width),
-        in_specs=[pl.BlockSpec(memory_space=pltpu.SMEM), vmem, vmem],
+        in_specs=[vmem, vmem],
         out_shape=(row, row, jax.ShapeDtypeStruct((holders, LANES), jnp.int32), tile, tile),
         scratch_shapes=[pltpu.VMEM(row.shape, jnp.int32)],
         compiler_params=LARGE,
         name="layout",
-    )(place, active_ids[None], admit_ids[None])
+    )(active_ids[None], admit_ids[None])
 
 
 def look_up(table_ref, index_ref, scales_ref):
@@ -145,7 +144,7 @@
     return jnp.concatenate(out, 0)
 
 
-def screen_kernel(table_ref, geno_ref, index_ref, resid_ref, out_ref, scales_ref, acc_ref):
+def screen_kernel(table_ref, geno_ref, index_ref, resid_ref, out_ref, x_ref, scales_ref, acc_ref):
     step = pl.program_id(0)
 
     @pl.when(step == 0)
@@ -153,14 +152,16 @@
         look_up(table_ref, index_ref, scales_ref)
         acc_ref[...] = jnp.zeros_like(acc_ref)
 
-    acc_ref[...] += dot(resid_ref[...].astype(bf16), dequantized(geno_ref, scales_ref, step))
+    x = dequantized(geno_ref, scales_ref, step)
+    x_ref[...] = x
+    acc_ref[...] += dot(resid_ref[...].astype(bf16), x)
 
     @pl.when(step == pl.num_programs(0) - 1)
     def _():
-        out_ref[...] = jnp.broadcast_to(acc_ref[...][None], out_ref.shape)
-
-
-def screen(table, geno, index, resid, copies):
+        out_ref[...] = acc_ref[...]
+
+
+def screen(table, geno, index, resid):
     samples, width = geno.shape
     phenos = resid.shape[0]
     return pl.pallas_call(
@@ -172,8 +173,14 @@
             pl.BlockSpec(index.shape, lambda i: (0, 0)),
             pl.BlockSpec((phenos, ROWS), lambda i: (0, i)),
         ],
-        out_specs=pl.BlockSpec((copies, phenos, width), lambda i: (0, 0, 0)),
-        out_shape=jax.ShapeDtypeStruct((copies, phenos, width), f32),
+        out_specs=(
+            pl.BlockSpec((phenos, width), lambda i: (0, 0)),
+            pl.BlockSpec((ROWS, width), lambda i: (i, 0)),
+        ),
+        out_shape=(
+            jax.ShapeDtypeStruct((phenos, width), f32),
+            jax.ShapeDtypeStruct((samples, width), bf16),
+        ),
         scratch_shapes=[pltpu.VMEM(index.shape, f32), pltpu.VMEM((phenos, width), f32)],
         compiler_params=LARGE,
         cost_estimate=pl.CostEstimate(
@@ -183,12 +190,9 @@
     )(table, geno, index, resid)
 
 
-def select_kernel(table_ref, packed_ref, geno_ref, index_ref, out_ref, scales_ref, pick_ref):
-    step = pl.program_id(0)
-
-    @pl.when(step == 0)
+def select_kernel(packed_ref, x_ref, out_ref, pick_ref):
+    @pl.when(pl.program_id(0) == 0)
     def _():
-        look_up(table_ref, index_ref, scales_ref)
         wanted = column_row(packed_ref[...])
 
         @pl.loop(0, pick_ref.shape[0], step=ROWS)
@@ -196,40 +200,37 @@
             here = iota((ROWS, pick_ref.shape[1]), 0) + (at + 1) == wanted
             pick_ref[pl.ds(pl.multiple_of(at, ROWS), ROWS), :] = here.astype(f32).astype(bf16)
 
-    out_ref[...] = dot(dequantized(geno_ref, scales_ref, step), pick_ref[...]).astype(bf16)
-
-
-def select(table, packed, geno, index):
-    samples, width = geno.shape
+    out_ref[...] = dot(x_ref[...], pick_ref[...]).astype(bf16)
+
+
+def select(packed, x):
+    samples, width = x.shape
     held = packed.shape[0] * CAP
     rows = 2 * ROWS
     return pl.pallas_call(
         select_kernel,
         grid=(samples // rows,),
         in_specs=[
-            pl.BlockSpec(memory_space=pltpu.SMEM),
             pl.BlockSpec(packed.shape, lambda i: (0, 0)),
             pl.BlockSpec((rows, width), lambda i: (i, 0)),
-            pl.BlockSpec(index.shape, lambda i: (0, 0)),
         ],
         out_specs=pl.BlockSpec((rows, held), lambda i: (i, 0)),
         out_shape=jax.ShapeDtypeStruct((samples, held), bf16),
-        scratch_shapes=[pltpu.VMEM(index.shape, f32), pltpu.VMEM((width, held), bf16)],
+        scratch_shapes=[pltpu.VMEM((width, held), bf16)],
         compiler_params=LARGE,
         cost_estimate=pl.CostEstimate(
             flops=2 * samples * width * held, bytes_accessed=2 * samples * width, transcendentals=0
         ),
         name="select",
-    )(table, packed, geno, index)
-
-
-def pick_kernel(inv_root, parts_ref, packed_hbm, scores_ref, pay_ref, packed_ref, sem):
+    )(packed, x)
+
+
+def pick_kernel(
+    inv_root, own_ref, one_ref, two_ref, three_ref, packed_hbm, scores_ref, pay_ref, packed_ref, sem
+):
     copy = pltpu.make_async_copy(packed_hbm, packed_ref, sem)
     copy.start()
-    scores = parts_ref[0]
-    for j in range(1, parts_ref.shape[0]):
-        scores = scores + parts_ref[j]
-    scores = scores * inv_root
+    scores = ((own_ref[...] + two_ref[...]) + (one_ref[...] + three_ref[...])) * inv_root
     scores_ref[...] = scores
     copy.wait()
     wanted = column_row(packed_ref[...])
@@ -247,15 +248,16 @@
 def pick(parts, packed, inv_root):
     return pl.pallas_call(
         functools.partial(pick_kernel, inv_root),
-        in_specs=[pl.BlockSpec(memory_space=pltpu.VMEM), pl.BlockSpec(memory_space=pltpu.HBM)],
+        in_specs=[pl.BlockSpec(memory_space=pltpu.VMEM)] * 4
+        + [pl.BlockSpec(memory_space=pltpu.HBM)],
         scratch_shapes=[pltpu.VMEM(packed.shape, packed.dtype), pltpu.SemaphoreType.DMA],
         out_shape=(
-            jax.ShapeDtypeStruct(parts.shape[1:], f32),
+            jax.ShapeDtypeStruct(parts[0].shape, f32),
             jax.ShapeDtypeStruct((packed.shape[0] * HALF, LANES), f32),
         ),
         compiler_params=SMALL,
         name="pick",
-    )(parts, packed)
+    )(*parts, packed)
 
 
 def direction_step(data, serial_ref, holder_ref, inverse_ref, advance, wide_ref, d_ref, pay_ref):
@@ -559,39 +561,41 @@
     ).reshape(pay.shape)
 
 
-def other_core(x):
-    return lax.ppermute(x, "core", [(0, 1), (1, 0)])
+def shifted(x, axis, by=1):
+    size = lax.axis_size(axis)
+    return lax.ppermute(x, axis, [(i, (i + by) % size) for i in range(size)])
 
 
 def on_device(
     geno, scale_index, scale_table, residual, beta_active, block_inverse, active_ids, admit_ids
 ):
     holders = lax.axis_size(VAR)
-    place = jnp.stack([lax.axis_index(VAR), lax.axis_index("core")]).astype(jnp.int32)
     samples, width = geno.shape
     copies = lax.axis_size(SAMP)
     inv_root = 1.0 / math.sqrt(samples * copies)
 
-    holder, serial, packed, rank, core = layout(place, active_ids, admit_ids, width, holders)
+    part, x = screen(scale_table, geno, scale_index, residual)
+    part, active_ids = lax.optimization_barrier((part, active_ids))
+    part = part + shifted(part, "y_hi")
+    parts = [part] + [shifted(part, "x", n) for n in range(1, lax.axis_size("x"))]
+
+    holder, serial, packed, rank, core = layout(active_ids, admit_ids, width, holders)
     packed = lax.all_to_all(
         packed.reshape(holders, 1, LANES), VAR, split_axis=0, concat_axis=0, tiled=True
     ).reshape(holders, LANES)
 
-    parts = screen(scale_table, geno, scale_index, residual, copies)
-    parts = lax.all_to_all(parts, SAMP, split_axis=0, concat_axis=0, tiled=True)
-    columns = select(scale_table, packed, geno, scale_index)
+    columns = select(packed, x)
     parts, columns = lax.optimization_barrier((parts, columns))
     scores, pay = pick(parts, packed, inv_root)
-
     pay, *state, columns = owner(
         exchange(pay, VAR), serial, holder, block_inverse, (beta_active, columns)
     )
     current = residual
     for pass_index in range(PASSES):
         keep, send = partial_update(core, exchange(pay, VAR), columns)
-        mine = spread(keep, other_core(send), lax.axis_size(CHIPS))
+        mine = spread(keep, shifted(send, "core"), lax.axis_size(CHIPS))
         mine = total(lax.all_to_all(mine, CHIPS, split_axis=0, concat_axis=0, tiled=True))
-        other = other_core(mine)
+        other = shifted(mine, "core")
         if pass_index + 1 == PASSES:
             break
         data, update = descent(rank, core, mine, other, current, columns, inv_root, copies)

time: 173 us -> 174 us (level)
  blocking collectives: 115 us -> 112 us
  Pallas kernels: 34.3 us -> 36.6 us
    ppermute x6 -> x10, starting transfers between devices: 0.66 us -> 8.45 us  [shifted(): return lax.ppermute(x, axis, [(i, (i + by) % size) for i in range(size)])]
    all_to_all x1 -> x0, starting transfers between devices: 6.65 us -> none  [on_device(): parts = lax.all_to_all(parts, SAMP, split_axis=0, concat_axis=0, tiled=True)]
    all_to_all x6, blocking collectives: 73.1 us -> 70.3 us  [exchange(): lax.all_to_all(pay.reshape(shape), axes, split_axis=0, concat_axis=0, til...]
    pallas_call x1, Pallas kernels: 7.69 us -> 10.2 us  [screen(): pl.pallas_call(screen_kernel, grid=(samples // ROWS,), in_specs=[pl.Block...]
    ppermute x6 -> x10, waiting for transfers between devices: 6.86 us -> 6.87 us  [shifted(): return lax.ppermute(x, axis, [(i, (i + by) % size) for i in range(size)])]
  transfers between devices with their start and end apart: 8 -> 11, of which waited for: 6 -> 7; matrix products, arithmetic and copies ran while one was open for 0% -> 0% of each run, Pallas kernels for 12% -> 8%
where the time goes in v3:
time: 174 us; the launch traced here: 173 us
  blocking collectives  112 us (64%)
  Pallas kernels  36.6 us (21%)
  starting transfers between devices  14 us (8%)
  waiting for transfers between devices  7.47 us (4%)
    all_to_all x6, blocking collectives, exchange(): lax.all_to_all(pay.reshape(shape), axes, split_axis=0, concat_axis=0, til...  70.3 us
    all_to_all x3, blocking collectives, on_device(): lax.all_to_all(mine, CHIPS, split_axis=0, concat_axis=0, tiled=True)  30.4 us
    pallas_call x1, Pallas kernels, select(): pl.pallas_call(select_kernel, grid=(samples // rows,), in_specs=[pl.Block...  12.8 us
    all_to_all x1, blocking collectives, on_device(): sums = lax.all_to_all(sums, SAMP, split_axis=0, concat_axis=0, tiled=True)  11.2 us
    pallas_call x1, Pallas kernels, screen(): pl.pallas_call(screen_kernel, grid=(samples // ROWS,), in_specs=[pl.Block...  10.2 us
    ppermute x10, starting transfers between devices, shifted(): return lax.ppermute(x, axis, [(i, (i + by) % size) for i in range(size)])  8.45 us
    ppermute x10, waiting for transfers between devices, shifted(): return lax.ppermute(x, axis, [(i, (i + by) % size) for i in range(size)])  6.87 us
    all_to_all x1, starting transfers between devices, on_device(): lax.all_to_all(packed.reshape(holders, 1, LANES), VAR, split_axis=0, conc...  5.53 us
  transfers between devices with their start and end apart: 11, of which 7 were waited for; matrix products, arithmetic and copies ran while one was open for 0% of the time, Pallas kernels for 8%

profile of v3, /device:TPU:0, one launch (start us, length us, event | category | flops | bytes accessed | tf_op | source)
XLA Modules:
  0.0 172.9 jit_solution(9608488130031591622)
XLA Ops:
  0.6 10.2 %screen.1 = (f32[8,2048]{1,0:T(8,128)}, bf16[2048,2048]{1,0:T(8,128)(2,1)}) custom-call(f32[16]{0:T(128)} %table_ref.1, bf16[2048,2048]{1,0:T(8,128)(2,1)} %geno_ref.1, s32[16,2048]{1,0:T(8,128)} %index_ref.1, f32[8,2048]{1,0:T(8,128)} %resid_in.1), custom_call_target="tpu_custom_call" | custom-call | flops 67108864 | bytes 8388608 | tf_op jit(solution)/shard_map/screen/pallas_call | solution.py:167
  10.9 3.3 %collective-permute-start = (f32[8,2048]{1,0:T(8,128)}, f32[8,2048]{1,0:T(8,128)S(1)}, u32[]{:S(2)}, u32[]{:S(2)}) collective-permute-start(f32[8,2048]{1,0:T(8,128)} %get-tuple-element.48), channel_id=1, source_target_pairs={{0,4},{4,0},{1,5},{5,1},{2,6},{6,2},{3,7},{7,3},{8,12},{12,8},{9,1... | collective-permute-start | bytes 196616 | tf_op jit(solution)/shard_map/ppermute | solution.py:566
  14.1 1.8 %layout.1 = (s32[1,512]{1,0:T(1,128)}, s32[1,512]{1,0:T(1,128)}, s32[16,128]{1,0:T(8,128)}, s32[8,128]{1,0:T(8,128)}, s32[8,128]{1,0:T(8,128)}) custom-call(s32[1,448]{1,0:T(1,128)} %bitcast.33, s32[1,64]{1,0:T(1,128)} %bitcast.34), custom_call_target="tpu_custom_call" | custom-call | tf_op jit(solution)/shard_map/layout/pallas_call | solution.py:118
  15.9 5.5 %all-to-all-start = ((s32[16,1,128]{2,1,0:T(1,128)}), s32[16,1,128]{2,1,0:T(1,128)S(1)}, u32[]{:S(2)}, u32[]{:S(2)}) async-start(s32[16,1,128]{2,1,0:T(1,128)} %bitcast.32), calls=%async_computation | async-start | bytes 16384 | tf_op jit(solution)/shard_map/all_to_all | solution.py:583
  22.3 2.8 %collective-permute-start.3 = (f32[8,2048]{1,0:T(8,128)S(1)}, f32[8,2048]{1,0:T(8,128)S(1)}, u32[]{:S(2)}, u32[]{:S(2)}) collective-permute-start(f32[8,2048]{1,0:T(8,128)S(1)} %add.3.own_ref), channel_id=1, source_target_pairs={{0,3},{1,0},{2,1},{3,2},{4,7},{5,4},{6,5},{7,6},{8,11},{9,8},{10,9... | collective-permute-start | bytes 196616 | tf_op jit(solution)/shard_map/ppermute | solution.py:566
  28.1 12.8 %select.1.columns_hbm = bf16[2048,1024]{1,0:T(8,128)(2,1)} custom-call(s32[16,128]{1,0:T(8,128)} %bitcast.26, bf16[2048,2048]{1,0:T(8,128)(2,1)} %get-tuple-element.51.x_ref), custom_call_target="tpu_custom_call" | custom-call | flops 8589934592 | bytes 8388608 | tf_op jit(solution)/shard_map/select/pallas_call | solution.py:210
  42.6 11.0 %all_to_all.55 = f32[16,4,128]{2,1,0:T(4,128)S(1)} all-to-all(f32[16,4,128]{2,1,0:T(4,128)S(1)} %bitcast.30), channel_id=1, replica_groups=mesh['y_lo'=2,'z'=4,'core'=2,'y_hi'=2,'x'=4] {'y_lo','z','core'}, dimensions={0} | all-to-all | bytes 65536 | tf_op jit(solution)/shard_map/all_to_all | solution.py:559
  53.6 2.2 %owner_first.1 = (f32[64,128]{1,0:T(8,128)S(1)}, f32[4,1024]{1,0:T(4,128)S(1)}, f32[4,1024]{1,0:T(4,128)S(1)}, f32[4,1024]{1,0:T(4,128)S(1)}, bf16[2048,1024]{1,0:T(8,128)(2,1)S(1)}) custom-call(f32[64,128]{1,0:T(8,128)S(1)} %bitcast.22, s32[1,512]{1,0:T(1,128)S(1)} %copy-done.6, s32[1,512]{1,0:T(1,128)S(1)} %copy-done.5, f32[2,256,256]{2,1,0:T(8,128)S(1)} %copy-done, ...), custom_call_target="tpu_custom_call" | custom-call | tf_op jit(solution)/shard_map/owner_first/pallas_call | solution.py:375
  55.8 8.7 %all_to_all.56 = f32[16,4,128]{2,1,0:T(4,128)S(1)} all-to-all(f32[16,4,128]{2,1,0:T(4,128)S(1)} %bitcast.31), channel_id=1, replica_groups=mesh['y_lo'=2,'z'=4,'core'=2,'y_hi'=2,'x'=4] {'y_lo','z','core'}, dimensions={0} | all-to-all | bytes 65536 | tf_op jit(solution)/shard_map/all_to_all | solution.py:559
  64.5 1.2 update.3
  66.9 10.1 %all_to_all.57.parts_ref = f32[8,8,1024]{2,1,0:T(8,128)S(1)} all-to-all(f32[8,8,1024]{2,1,0:T(8,128)S(1)} %spread.3), channel_id=1, replica_groups=mesh['y_lo'=2,'z'=4,'core'=2,'y_hi'=2,'x'=4] {'y_lo','z'}, dimensions={0} | all-to-all | bytes 524288 | tf_op jit(solution)/shard_map/all_to_all | solution.py:597
  77.2 1.2 collective-permute-done.5.other_ref
  79.2 17.3 %all_to_all.58 = f32[128,1,640]{2,1,0:T(1,128)S(1)} all-to-all(f32[128,1,640]{2,1,0:T(1,128)S(1)} %bitcast.21), channel_id=1, replica_groups=mesh['y_lo'=2,'z'=4,'core'=2,'y_hi'=2,'x'=4] {'y_hi','x','y_lo','z','core'}, dimensions={0} | all-to-all | bytes 655360 | tf_op jit(solution)/shard_map/all_to_all | solution.py:559
  97.4 8.7 %all_to_all.59 = f32[16,4,128]{2,1,0:T(4,128)S(1)} all-to-all(f32[16,4,128]{2,1,0:T(4,128)S(1)} %bitcast.29), channel_id=1, replica_groups=mesh['y_lo'=2,'z'=4,'core'=2,'y_hi'=2,'x'=4] {'y_lo','z','core'}, dimensions={0} | all-to-all | bytes 65536 | tf_op jit(solution)/shard_map/all_to_all | solution.py:559
  106.1 1.2 update.4
  108.6 10.1 %all_to_all.60.parts_ref = f32[8,8,1024]{2,1,0:T(8,128)S(1)} all-to-all(f32[8,8,1024]{2,1,0:T(8,128)S(1)} %spread.4), channel_id=1, replica_groups=mesh['y_lo'=2,'z'=4,'core'=2,'y_hi'=2,'x'=4] {'y_lo','z'}, dimensions={0} | all-to-all | bytes 524288 | tf_op jit(solution)/shard_map/all_to_all | solution.py:597
  118.8 1.2 collective-permute-done.7.other_ref
  120.8 16.0 %all_to_all.61 = f32[128,1,640]{2,1,0:T(1,128)S(1)} all-to-all(f32[128,1,640]{2,1,0:T(1,128)S(1)} %bitcast.20), channel_id=1, replica_groups=mesh['y_lo'=2,'z'=4,'core'=2,'y_hi'=2,'x'=4] {'y_hi','x','y_lo','z','core'}, dimensions={0} | all-to-all | bytes 655360 | tf_op jit(solution)/shard_map/all_to_all | solution.py:559
  136.8 1.4 owner_next.3
  138.2 8.6 %all_to_all.62 = f32[16,4,128]{2,1,0:T(4,128)S(1)} all-to-all(f32[16,4,128]{2,1,0:T(4,128)S(1)} %bitcast.28), channel_id=1, replica_groups=mesh['y_lo'=2,'z'=4,'core'=2,'y_hi'=2,'x'=4] {'y_lo','z','core'}, dimensions={0} | all-to-all | bytes 65536 | tf_op jit(solution)/shard_map/all_to_all | solution.py:559
  146.9 1.2 update.5
  149.3 10.1 %all_to_all.63.parts_ref = f32[8,8,1024]{2,1,0:T(8,128)S(1)} all-to-all(f32[8,8,1024]{2,1,0:T(8,128)S(1)} %spread.5), channel_id=1, replica_groups=mesh['y_lo'=2,'z'=4,'core'=2,'y_hi'=2,'x'=4] {'y_lo','z'}, dimensions={0} | all-to-all | bytes 524288 | tf_op jit(solution)/shard_map/all_to_all | solution.py:597
  159.6 1.2 collective-permute-done.9.other_ref
  160.9 11.2 %all_to_all.64.sums_ref = f32[8,8,128]{2,1,0:T(8,128)S(1)} all-to-all(f32[8,8,128]{2,1,0:T(8,128)S(1)} %get-tuple-element.85), channel_id=1, replica_groups=mesh['y_lo'=2,'z'=4,'core'=2,'y_hi'=2,'x'=4] {'y_hi','x'}, dimensions={0} | all-to-all | bytes 65536 | tf_op jit(solution)/shard_map/all_to_all | solution.py:608
  (47 shorter events, 13.0 us)
Async XLA Ops:
  10.9 10.6 %collective-permute-start = (f32[8,2048]{1,0:T(8,128)}, f32[8,2048]{1,0:T(8,128)S(1)}, u32[]{:S(2)}, u32[]{:S(2)}) collective-permute-start(f32[8,2048]{1,0:T(8,128)} %get-tuple-element.48), channel_id=1, source_target_pairs={{0,4},{4,0},{1,5},{5,1},{2,6},{6,2},{3,7},{7,3},{8,12},{12,8},{9,1... | collective-permute-start | bytes 196616 | tf_op jit(solution)/shard_map/ppermute | solution.py:566
  15.9 11.5 %all-to-all-start = ((s32[16,1,128]{2,1,0:T(1,128)}), s32[16,1,128]{2,1,0:T(1,128)S(1)}, u32[]{:S(2)}, u32[]{:S(2)}) async-start(s32[16,1,128]{2,1,0:T(1,128)} %bitcast.32), calls=%async_computation | async-start | bytes 16384 | tf_op jit(solution)/shard_map/all_to_all | solution.py:583
  22.3 18.6 %collective-permute-start.3 = (f32[8,2048]{1,0:T(8,128)S(1)}, f32[8,2048]{1,0:T(8,128)S(1)}, u32[]{:S(2)}, u32[]{:S(2)}) collective-permute-start(f32[8,2048]{1,0:T(8,128)S(1)} %add.3.own_ref), channel_id=1, source_target_pairs={{0,3},{1,0},{2,1},{3,2},{4,7},{5,4},{6,5},{7,6},{8,11},{9,8},{10,9... | collective-permute-start | bytes 196616 | tf_op jit(solution)/shard_map/ppermute | solution.py:566
  25.1 15.8 %collective-permute-start.2 = (f32[8,2048]{1,0:T(8,128)S(1)}, f32[8,2048]{1,0:T(8,128)S(1)}, u32[]{:S(2)}, u32[]{:S(2)}) collective-permute-start(f32[8,2048]{1,0:T(8,128)S(1)} %add.3.own_ref), channel_id=1, source_target_pairs={{0,2},{1,3},{2,0},{3,1},{4,6},{5,7},{6,4},{7,5},{8,10},{9,11},{10,... | collective-permute-start | bytes 196616 | tf_op jit(solution)/shard_map/ppermute | solution.py:566
  25.9 15.0 %collective-permute-start.1 = (f32[8,2048]{1,0:T(8,128)S(1)}, f32[8,2048]{1,0:T(8,128)S(1)}, u32[]{:S(2)}, u32[]{:S(2)}) collective-permute-start(f32[8,2048]{1,0:T(8,128)S(1)} %add.3.own_ref), channel_id=1, source_target_pairs={{0,1},{1,2},{2,3},{3,0},{4,5},{5,6},{6,7},{7,4},{8,9},{9,10},{10,1... | collective-permute-start | bytes 196616 | tf_op jit(solution)/shard_map/ppermute | solution.py:566
  27.4 0.6 copy-start.3
  28.0 25.6 %copy-start = (f32[2,256,256]{2,1,0:T(8,128)S(1)}, f32[2,256,256]{2,1,0:T(8,128)}, u32[]{:S(2)}) copy-start(f32[2,256,256]{2,1,0:T(8,128)} %inverse_ref.5) | copy-start | bytes 1572868
  28.0 25.6 %copy-start.5 = (s32[1,512]{1,0:T(1,128)S(1)}, s32[1,512]{1,0:T(1,128)}, u32[]{:S(2)}) copy-start(s32[1,512]{1,0:T(1,128)} %get-tuple-element.61.holder_ref) | copy-start | bytes 6148
  28.0 25.6 %copy-start.6 = (s32[1,512]{1,0:T(1,128)S(1)}, s32[1,512]{1,0:T(1,128)}, u32[]{:S(2)}) copy-start(s32[1,512]{1,0:T(1,128)} %get-tuple-element.60.serial_ref) | copy-start | bytes 6148
  28.0 25.6 %copy-start.7 = (f32[8,448]{1,0:T(8,128)S(1)}, f32[8,448]{1,0:T(8,128)}, u32[]{:S(2)}) copy-start(f32[8,448]{1,0:T(8,128)} %beta_ref.1) | copy-start | bytes 43012
  28.0 36.4 %copy-start.2 = (s32[8,128]{1,0:T(8,128)S(1)}, s32[8,128]{1,0:T(8,128)}, u32[]{:S(2)}) copy-start(s32[8,128]{1,0:T(8,128)} %get-tuple-element.57.core_ref) | copy-start | bytes 12292
  28.1 50.3 %copy-start.8 = (s32[8,128]{1,0:T(8,128)S(1)}, s32[8,128]{1,0:T(8,128)}, u32[]{:S(2)}) copy-start(s32[8,128]{1,0:T(8,128)} %get-tuple-element.58.rank_ref) | copy-start | bytes 12292
  40.9 37.5 %copy-start.1 = (f32[8,2048]{1,0:T(8,128)S(1)}, f32[8,2048]{1,0:T(8,128)}, u32[]{:S(2)}) copy-start(f32[8,2048]{1,0:T(8,128)} %resid_in.1) | copy-start | bytes 196612
  40.9 0.7 copy-start.4
  65.7 1.2 collective-permute-start.4
  77.1 1.3 collective-permute-start.5
  107.3 1.2 collective-permute-start.6
  118.7 1.3 collective-permute-start.7
  148.1 1.2 collective-permute-start.8
  159.5 1.3 collective-permute-start.9

commit v4 on v3

--- a/solution.py
+++ b/solution.py
@@ -22,7 +22,7 @@
 penalty = 0.5
 epsilon = 1e-06
 SMALL = pltpu.CompilerParams(vmem_limit_bytes=12 * 1024 * 1024)
-MEDIUM = pltpu.CompilerParams(vmem_limit_bytes=46 * 1024 * 1024)
+MEDIUM = pltpu.CompilerParams(vmem_limit_bytes=50 * 1024 * 1024)
 LARGE = pltpu.CompilerParams(vmem_limit_bytes=60 * 1024 * 1024)
 f32 = jnp.float32
 bf16 = jnp.bfloat16
@@ -74,19 +74,7 @@
     return spread.astype(f32).astype(bf16), mask.astype(f32)
 
 
-def layout_kernel(
-    width,
-    active_ref,
-    admit_ref,
-    holder_ref,
-    serial_ref,
-    packed_ref,
-    rank_ref,
-    core_ref,
-    ids_ref,
-):
-    rank_ref[...] = jnp.full(rank_ref.shape, lax.axis_index(VAR), jnp.int32)
-    core_ref[...] = jnp.full(core_ref.shape, lax.axis_index("core"), jnp.int32)
+def lay_out(width, active_ref, admit_ref, holder_ref, serial_ref, packed_ref, ids_ref):
     holders = packed_ref.shape[0]
     fit = holder_ref.shape[1]
     active = active_ref.shape[1]
@@ -111,20 +99,6 @@
     packed_ref[...] = (parts[0] * LANES + parts[1]).astype(jnp.int32)
 
 
-def layout(active_ids, admit_ids, width, holders):
-    row = jax.ShapeDtypeStruct((1, active_ids.size + admit_ids.size), jnp.int32)
-    tile = jax.ShapeDtypeStruct((2 * HALF, LANES), jnp.int32)
-    vmem = pl.BlockSpec(memory_space=pltpu.VMEM)
-    return pl.pallas_call(
-        functools.partial(layout_kernel, width),
-        in_specs=[vmem, vmem],
-        out_shape=(row, row, jax.ShapeDtypeStruct((holders, LANES), jnp.int32), tile, tile),
-        scratch_shapes=[pltpu.VMEM(row.shape, jnp.int32)],
-        compiler_params=LARGE,
-        name="layout",
-    )(active_ids[None], admit_ids[None])
-
-
 def look_up(table_ref, index_ref, scales_ref):
     index = index_ref[...]
     scales = jnp.full(index.shape, table_ref[0], f32)
@@ -144,55 +118,72 @@
     return jnp.concatenate(out, 0)
 
 
-def screen_kernel(table_ref, geno_ref, index_ref, resid_ref, out_ref, x_ref, scales_ref, acc_ref):
+def screen_kernel(
+    table_ref,
+    geno_ref,
+    index_ref,
+    resid_ref,
+    active_ref,
+    admit_ref,
+    out_ref,
+    holder_ref,
+    serial_ref,
+    packed_ref,
+    rank_ref,
+    core_ref,
+    scales_ref,
+    ids_ref,
+):
     step = pl.program_id(0)
 
     @pl.when(step == 0)
     def _():
+        rank_ref[...] = jnp.full(rank_ref.shape, lax.axis_index(VAR), jnp.int32)
+        core_ref[...] = jnp.full(core_ref.shape, lax.axis_index("core"), jnp.int32)
+        width = geno_ref.shape[1]
+        lay_out(width, active_ref, admit_ref, holder_ref, serial_ref, packed_ref, ids_ref)
         look_up(table_ref, index_ref, scales_ref)
-        acc_ref[...] = jnp.zeros_like(acc_ref)
-
-    x = dequantized(geno_ref, scales_ref, step)
-    x_ref[...] = x
-    acc_ref[...] += dot(resid_ref[...].astype(bf16), x)
-
-    @pl.when(step == pl.num_programs(0) - 1)
-    def _():
-        out_ref[...] = acc_ref[...]
-
-
-def screen(table, geno, index, resid):
+        out_ref[...] = jnp.zeros_like(out_ref)
+
+    out_ref[...] += dot(resid_ref[...].astype(bf16), dequantized(geno_ref, scales_ref, step))
+
+
+def screen(table, geno, index, resid, active_ids, admit_ids):
     samples, width = geno.shape
     phenos = resid.shape[0]
+    active_ids, admit_ids = active_ids[None], admit_ids[None]
+    fit = active_ids.size + admit_ids.size
+    outs = [(phenos, width, f32), (1, fit, jnp.int32), (1, fit, jnp.int32)]
+    outs += [(lax.axis_size(VAR), LANES, jnp.int32)] + [(2 * HALF, LANES, jnp.int32)] * 2
+    whole = lambda shape: pl.BlockSpec(shape, lambda i: (0, 0))
     return pl.pallas_call(
         screen_kernel,
         grid=(samples // ROWS,),
         in_specs=[
             pl.BlockSpec(memory_space=pltpu.SMEM),
             pl.BlockSpec((ROWS, width), lambda i: (i, 0)),
-            pl.BlockSpec(index.shape, lambda i: (0, 0)),
+            whole(index.shape),
             pl.BlockSpec((phenos, ROWS), lambda i: (0, i)),
+            whole(active_ids.shape),
+            whole(admit_ids.shape),
         ],
-        out_specs=(
-            pl.BlockSpec((phenos, width), lambda i: (0, 0)),
-            pl.BlockSpec((ROWS, width), lambda i: (i, 0)),
-        ),
-        out_shape=(
-            jax.ShapeDtypeStruct((phenos, width), f32),
-            jax.ShapeDtypeStruct((samples, width), bf16),
-        ),
-        scratch_shapes=[pltpu.VMEM(index.shape, f32), pltpu.VMEM((phenos, width), f32)],
+        out_specs=[whole(out[:2]) for out in outs],
+        out_shape=[jax.ShapeDtypeStruct(out[:2], out[2]) for out in outs],
+        scratch_shapes=[pltpu.VMEM(index.shape, f32), pltpu.VMEM((1, fit), jnp.int32)],
         compiler_params=LARGE,
         cost_estimate=pl.CostEstimate(
             flops=2 * phenos * samples * width, bytes_accessed=2 * samples * width, transcendentals=0
         ),
         name="screen",
-    )(table, geno, index, resid)
-
-
-def select_kernel(packed_ref, x_ref, out_ref, pick_ref):
-    @pl.when(pl.program_id(0) == 0)
+    )(table, geno, index, resid, active_ids, admit_ids)
+
+
+def select_kernel(first, table_ref, packed_ref, geno_ref, index_ref, out_ref, scales_ref, pick_ref):
+    step = pl.program_id(0)
+
+    @pl.when(step == 0)
     def _():
+        look_up(table_ref, index_ref, scales_ref)
         wanted = column_row(packed_ref[...])
 
         @pl.loop(0, pick_ref.shape[0], step=ROWS)
@@ -200,29 +191,33 @@
             here = iota((ROWS, pick_ref.shape[1]), 0) + (at + 1) == wanted
             pick_ref[pl.ds(pl.multiple_of(at, ROWS), ROWS), :] = here.astype(f32).astype(bf16)
 
-    out_ref[...] = dot(x_ref[...], pick_ref[...]).astype(bf16)
-
-
-def select(packed, x):
-    samples, width = x.shape
+    x = dequantized(geno_ref, scales_ref, first + step)
+    out_ref[...] = dot(x, pick_ref[...]).astype(bf16)
+
+
+def select(half, table, packed, geno, index, params):
+    samples, width = geno.shape[0] // 2, geno.shape[1]
     held = packed.shape[0] * CAP
     rows = 2 * ROWS
-    return pl.pallas_call(
-        select_kernel,
+    first = half * (samples // rows)
+    return pl.pallas_call(
+        functools.partial(select_kernel, first),
         grid=(samples // rows,),
         in_specs=[
+            pl.BlockSpec(memory_space=pltpu.SMEM),
             pl.BlockSpec(packed.shape, lambda i: (0, 0)),
-            pl.BlockSpec((rows, width), lambda i: (i, 0)),
+            pl.BlockSpec((rows, width), lambda i: (i + first, 0)),
+            pl.BlockSpec(index.shape, lambda i: (0, 0)),
         ],
         out_specs=pl.BlockSpec((rows, held), lambda i: (i, 0)),
         out_shape=jax.ShapeDtypeStruct((samples, held), bf16),
-        scratch_shapes=[pltpu.VMEM((width, held), bf16)],
-        compiler_params=LARGE,
+        scratch_shapes=[pltpu.VMEM(index.shape, f32), pltpu.VMEM((width, held), bf16)],
+        compiler_params=params,
         cost_estimate=pl.CostEstimate(
             flops=2 * samples * width * held, bytes_accessed=2 * samples * width, transcendentals=0
         ),
         name="select",
-    )(packed, x)
+    )(table, packed, geno, index)
 
 
 def pick_kernel(
@@ -293,9 +288,9 @@
     beta_ref,
     columns_hbm,
     pay_ref,
-    g_ref,
     b_ref,
     d_ref,
+    g_ref,
     columns_ref,
     wide_ref,
     sem,
@@ -323,16 +318,16 @@
     serial_ref,
     holder_ref,
     inverse_ref,
-    g_in,
     b_in,
     d_in,
+    g_in,
     resid_in,
     update_ref,
     pay_ref,
-    g_ref,
     b_ref,
     d_ref,
     resid_ref,
+    g_ref,
     wide_ref,
     sum_ref,
     rows_ref,
@@ -364,71 +359,70 @@
     )
 
 
-def owner(data, serial, holder, inverse, state):
+def owner_first(data, serial, holder, inverse, beta, columns):
     fit = serial.shape[1]
-    phenos = 2 * HALF
     held = jax.ShapeDtypeStruct((HALF, 2 * fit), f32)
-    wide = pltpu.VMEM((phenos, fit), f32)
-    if len(state) == 2:
-        vmem = pl.BlockSpec(memory_space=pltpu.VMEM)
-        columns = state[1]
-        return pl.pallas_call(
-            first_owner_kernel,
-            in_specs=[vmem] * 5 + [pl.BlockSpec(memory_space=pltpu.HBM)],
-            out_specs=(vmem,) * 5,
-            out_shape=(
-                jax.ShapeDtypeStruct(data.shape, f32),
-                held,
-                held,
-                held,
-                jax.ShapeDtypeStruct(columns.shape, columns.dtype),
-            ),
-            scratch_shapes=[wide, pltpu.SemaphoreType.DMA],
-            compiler_params=MEDIUM,
-            name="owner_first",
-        )(data, serial, holder, inverse, *state)
-    holders = lax.axis_size(VAR)
-    return pl.pallas_call(
-        owner_kernel,
+    vmem = pl.BlockSpec(memory_space=pltpu.VMEM)
+    return pl.pallas_call(
+        first_owner_kernel,
+        in_specs=[vmem] * 5 + [pl.BlockSpec(memory_space=pltpu.HBM)],
+        out_specs=(vmem,) * 5,
         out_shape=(
-            jax.ShapeDtypeStruct((holders * HALF, LANES), f32),
+            jax.ShapeDtypeStruct(data.shape, f32),
             held,
             held,
             held,
-            jax.ShapeDtypeStruct(state[3].shape, f32),
+            jax.ShapeDtypeStruct(columns.shape, columns.dtype),
         ),
-        scratch_shapes=[
-            wide,
-            pltpu.VMEM((holders * (HALF + 1), LANES), f32),
-            pltpu.VMEM((holders * HALF, LANES), f32),
+        scratch_shapes=[pltpu.VMEM((2 * HALF, fit), f32), pltpu.SemaphoreType.DMA],
+        compiler_params=MEDIUM,
+        name="owner_first",
+    )(data, serial, holder, inverse, beta, columns)
+
+
+def owner_next(data, serial, holder, inverse, state, resid, update, final):
+    fit = serial.shape[1]
+    phenos = resid.shape[0]
+    held = jax.ShapeDtypeStruct((HALF, 2 * fit), f32)
+    rows = lax.axis_size(VAR) * HALF
+    pay = jax.ShapeDtypeStruct((rows, LANES), f32)
+    new_resid = jax.ShapeDtypeStruct(resid.shape, f32)
+    return pl.pallas_call(
+        owner_kernel,
+        out_shape=(pay, held, held, new_resid) + (() if final else (held,)),
+        scratch_shapes=([pltpu.VMEM(held.shape, f32)] if final else [])
+        + [
+            pltpu.VMEM((phenos, fit), f32),
+            pltpu.VMEM((rows // HALF * (HALF + 1), LANES), f32),
+            pltpu.VMEM((rows, LANES), f32),
             pltpu.VMEM((phenos, LANES), f32),
         ],
         compiler_params=SMALL,
         name="owner_next",
-    )(data, serial, holder, inverse, *state)
-
-
-def update_kernel(core_ref, pay_ref, columns_ref, keep_ref, send_ref):
+    )(data, serial, holder, inverse, *state, resid, update)
+
+
+def update_kernel(core_ref, pay_ref, first_ref, second_ref, keep_ref, send_ref):
     packed = jnp.concatenate(
         [swapped(pay_ref[at : at + 8, :]) for at in range(0, pay_ref.shape[0], 8)], 1
     ).astype(bf16)
     first = core_ref[:, :1] == 0
     half = keep_ref.shape[1]
     for at in range(0, half, ROWS):
-        a = dot_t(packed, columns_ref[at : at + ROWS, :])
-        b = dot_t(packed, columns_ref[half + at : half + at + ROWS, :])
+        a = dot_t(packed, first_ref[at : at + ROWS, :])
+        b = dot_t(packed, second_ref[at : at + ROWS, :])
         keep_ref[:, at : at + ROWS] = jnp.where(first, a, b)
         send_ref[:, at : at + ROWS] = jnp.where(first, b, a)
 
 
-def partial_update(core, pay, columns):
-    half = jax.ShapeDtypeStruct((2 * HALF, columns.shape[0] // 2), f32)
+def partial_update(core, pay, first, second):
+    half = jax.ShapeDtypeStruct((2 * HALF, first.shape[0]), f32)
     return pl.pallas_call(
         update_kernel,
         out_shape=(half, half),
         compiler_params=SMALL,
         name="update",
-    )(core, pay, columns)
+    )(core, pay, first, second)
 
 
 def spread_kernel(keep_ref, arrived_ref, out_ref):
@@ -473,14 +467,25 @@
 
 
 def descent_kernel(
-    inv_root, rank_ref, core_ref, mine_ref, other_ref, resid_ref, columns_ref, out_ref, update_ref
+    inv_root,
+    rank_ref,
+    core_ref,
+    mine_ref,
+    other_ref,
+    resid_ref,
+    first_ref,
+    second_ref,
+    out_ref,
+    update_ref,
 ):
     update = whole_update(inv_root, core_ref, mine_ref, other_ref)
     update_ref[...] = update
     phenos = update.shape[0]
     high = update.astype(bf16)
     low = (update - high.astype(f32)).astype(bf16)
-    grad = dot(jnp.concatenate([high, low], 0), columns_ref[...])
+    pair = jnp.concatenate([high, low], 0)
+    half = first_ref.shape[0]
+    grad = dot(pair[:, :half], first_ref[...]) + dot(pair[:, half:], second_ref[...])
     grad = (grad[:phenos] + grad[phenos:]) * inv_root
     both = step_sums(resid_ref[...], update)
     mine = iota(both.shape, 0) == lax.rem(rank_ref[...], phenos)
@@ -498,14 +503,14 @@
             out_ref[at + chunk + HALF : at + 2 * chunk, :] = row
 
 
-def descent(rank, core, mine, other, resid, columns, inv_root, copies):
-    out = (copies * (columns.shape[1] // CAP) * (HALF + 1), LANES)
+def descent(rank, core, mine, other, resid, first, second, inv_root, copies):
+    out = (copies * (first.shape[1] // CAP) * (HALF + 1), LANES)
     return pl.pallas_call(
         functools.partial(descent_kernel, inv_root),
         out_shape=(jax.ShapeDtypeStruct(out, f32), jax.ShapeDtypeStruct(resid.shape, f32)),
         compiler_params=SMALL,
         name="descent",
-    )(rank, core, mine, other, resid, columns)
+    )(rank, core, mine, other, resid, first, second)
 
 
 def settle_kernel(inv_root, core_ref, mine_ref, other_ref, resid_ref, sums_ref, update_ref):
@@ -574,36 +579,44 @@
     copies = lax.axis_size(SAMP)
     inv_root = 1.0 / math.sqrt(samples * copies)
 
-    part, x = screen(scale_table, geno, scale_index, residual)
-    part, active_ids = lax.optimization_barrier((part, active_ids))
+    part, holder, serial, packed, rank, core = screen(
+        scale_table, geno, scale_index, residual, active_ids, admit_ids
+    )
     part = part + shifted(part, "y_hi")
     parts = [part] + [shifted(part, "x", n) for n in range(1, lax.axis_size("x"))]
-
-    holder, serial, packed, rank, core = layout(active_ids, admit_ids, width, holders)
     packed = lax.all_to_all(
         packed.reshape(holders, 1, LANES), VAR, split_axis=0, concat_axis=0, tiled=True
     ).reshape(holders, LANES)
 
-    columns = select(packed, x)
-    parts, columns = lax.optimization_barrier((parts, columns))
+    first = select(0, scale_table, packed, geno, scale_index, MEDIUM)
+    parts, first = lax.optimization_barrier((parts, first))
     scores, pay = pick(parts, packed, inv_root)
-    pay, *state, columns = owner(
-        exchange(pay, VAR), serial, holder, block_inverse, (beta_active, columns)
+    pay, packed = lax.optimization_barrier((pay, packed))
+    second = select(1, scale_table, packed, geno, scale_index, LARGE)
+    pay, *state, second = owner_first(
+        exchange(pay, VAR), serial, holder, block_inverse, beta_active, second
     )
     current = residual
     for pass_index in range(PASSES):
-        keep, send = partial_update(core, exchange(pay, VAR), columns)
+        keep, send = partial_update(core, exchange(pay, VAR), first, second)
         mine = spread(keep, shifted(send, "core"), lax.axis_size(CHIPS))
         mine = total(lax.all_to_all(mine, CHIPS, split_axis=0, concat_axis=0, tiled=True))
         other = shifted(mine, "core")
         if pass_index + 1 == PASSES:
             break
-        data, update = descent(rank, core, mine, other, current, columns, inv_root, copies)
-        pay, *state, current = owner(
-            exchange(data, SAMP + VAR), serial, holder, block_inverse, (*state, current, update)
+        data, update = descent(rank, core, mine, other, current, first, second, inv_root, copies)
+        pay, coeffs, direction, current, *gradient = owner_next(
+            exchange(data, SAMP + VAR),
+            serial,
+            holder,
+            block_inverse,
+            state,
+            current,
+            update,
+            pass_index + 2 == PASSES,
         )
-
-    _, coeffs, direction = state
+        state = (coeffs, direction, *gradient)
+
     sums, update = settle(core, mine, other, current, inv_root, copies)
     sums = lax.all_to_all(sums, SAMP, split_axis=0, concat_axis=0, tiled=True)
     return (scores, *last(sums, coeffs, direction, current, update))

time: 174 us -> 168 us (0.966)
  blocking collectives: 112 us -> 104 us
  starting transfers between devices: 14 us -> 19.3 us
    all_to_all x6 -> x5, blocking collectives: 70.3 us -> 62.2 us  [exchange(): lax.all_to_all(pay.reshape(shape), axes, split_axis=0, concat_axis=0, til...]
    all_to_all x0 -> x1, starting transfers between devices: none -> 5.13 us  [exchange(): lax.all_to_all(pay.reshape(shape), axes, split_axis=0, concat_axis=0, til...]
    pallas_call x1, Pallas kernels: 10.2 us -> 8.05 us  [screen(): pl.pallas_call(screen_kernel, grid=(samples // ROWS,), in_specs=[pl.Block...]
  transfers between devices with their start and end apart: 11 -> 12, of which waited for: 7 -> 7; matrix products, arithmetic and copies ran while one was open for 0% -> 1% of each run, Pallas kernels for 8% -> 9%
where the time goes in v4:
time: 168 us; the launch traced here: 167 us
  blocking collectives  104 us (62%)
  Pallas kernels  34.9 us (21%)
  starting transfers between devices  19.3 us (11%)
  waiting for transfers between devices  7.48 us (4%)
    all_to_all x5, blocking collectives, exchange(): lax.all_to_all(pay.reshape(shape), axes, split_axis=0, concat_axis=0, til...  62.2 us
    all_to_all x3, blocking collectives, on_device(): lax.all_to_all(mine, CHIPS, split_axis=0, concat_axis=0, tiled=True)  30.4 us
    pallas_call x2, Pallas kernels, select(): pl.pallas_call(functools.partial(select_kernel, first), grid=(samples //...  15.5 us
    all_to_all x1, blocking collectives, on_device(): sums = lax.all_to_all(sums, SAMP, split_axis=0, concat_axis=0, tiled=True)  11.2 us
    ppermute x10, starting transfers between devices, shifted(): return lax.ppermute(x, axis, [(i, (i + by) % size) for i in range(size)])  8.67 us
    pallas_call x1, Pallas kernels, screen(): pl.pallas_call(screen_kernel, grid=(samples // ROWS,), in_specs=[pl.Block...  8.05 us
    ppermute x10, waiting for transfers between devices, shifted(): return lax.ppermute(x, axis, [(i, (i + by) % size) for i in range(size)])  6.87 us
    all_to_all x1, starting transfers between devices, on_device(): lax.all_to_all(packed.reshape(holders, 1, LANES), VAR, split_axis=0, conc...  5.53 us
  transfers between devices with their start and end apart: 12, of which 7 were waited for; matrix products, arithmetic and copies ran while one was open for 1% of the time, Pallas kernels for 9%

profile of v4, /device:TPU:0, one launch (start us, length us, event | category | flops | bytes accessed | tf_op | source)
XLA Modules:
  0.0 167.3 jit_solution(933940977327586035)
XLA Ops:
  0.7 8.0 %screen.1 = (f32[8,2048]{1,0:T(8,128)}, s32[1,512]{1,0:T(1,128)}, s32[1,512]{1,0:T(1,128)}, s32[16,128]{1,0:T(8,128)}, s32[8,128]{1,0:T(8,128)}, /*index=5*/s32[8,128]{1,0:T(8,128)}) custom-call(f32[16]{0:T(128)} %table_ref.5, bf16[2048,2048]{1,0:T(8,128)(2,1)} %geno_ref.5, s32[16,2048]{1,0:T(8,128)} %index_ref.5, f32[8,2048]{1,0:T(8,128)} %resid_in.1, ...), custom_call_target="tpu_custom_call" | custom-call | flops 67108864 | bytes 8388608 | tf_op jit(solution)/shard_map/screen/pallas_call | solution.py:159
  8.7 3.4 %collective-permute-start = (f32[8,2048]{1,0:T(8,128)}, f32[8,2048]{1,0:T(8,128)S(1)}, u32[]{:S(2)}, u32[]{:S(2)}) collective-permute-start(f32[8,2048]{1,0:T(8,128)} %get-tuple-element.46), channel_id=1, source_target_pairs={{0,4},{4,0},{1,5},{5,1},{2,6},{6,2},{3,7},{7,3},{8,12},{12,8},{9,1... | collective-permute-start | bytes 196616 | tf_op jit(solution)/shard_map/ppermute | solution.py:571
  12.1 5.5 %all-to-all-start = ((s32[16,1,128]{2,1,0:T(1,128)}), s32[16,1,128]{2,1,0:T(1,128)S(1)}, u32[]{:S(2)}, u32[]{:S(2)}) async-start(s32[16,1,128]{2,1,0:T(1,128)} %bitcast.32), calls=%async_computation | async-start | bytes 16384 | tf_op jit(solution)/shard_map/all_to_all | solution.py:587
  18.5 2.8 %collective-permute-start.3 = (f32[8,2048]{1,0:T(8,128)S(1)}, f32[8,2048]{1,0:T(8,128)S(1)}, u32[]{:S(2)}, u32[]{:S(2)}) collective-permute-start(f32[8,2048]{1,0:T(8,128)S(1)} %add.3.own_ref), channel_id=1, source_target_pairs={{0,3},{1,0},{2,1},{3,2},{4,7},{5,4},{6,5},{7,6},{8,11},{9,8},{10,9... | collective-permute-start | bytes 196616 | tf_op jit(solution)/shard_map/ppermute | solution.py:571
  23.6 7.2 %select.2.first_ref = bf16[1024,1024]{1,0:T(8,128)(2,1)S(1)} custom-call(f32[16]{0:T(128)S(1)} %copy-done.9, s32[16,128]{1,0:T(8,128)S(1)} %bitcast.26, bf16[2048,2048]{1,0:T(8,128)(2,1)} %geno_ref.5, s32[16,2048]{1,0:T(8,128)S(1)} %copy-done.3), custom_call_target="tpu_custom_call" | custom-call | flops 4294967296 | bytes 4194304 | tf_op jit(solution)/shard_map/select/pallas_call | solution.py:203
  30.9 1.6 pick.1
  32.4 5.1 %all-to-all-start.1 = ((f32[16,4,128]{2,1,0:T(4,128)}), f32[16,4,128]{2,1,0:T(4,128)S(1)}, u32[]{:S(2)}, u32[]{:S(2)}) async-start(f32[16,4,128]{2,1,0:T(4,128)} %bitcast.5), calls=%async_computation.1 | async-start | bytes 65536 | tf_op jit(solution)/shard_map/all_to_all | solution.py:564
  37.6 8.3 %select.3.columns_hbm = bf16[1024,1024]{1,0:T(8,128)(2,1)} custom-call(f32[16]{0:T(128)} %table_ref.5, s32[16,128]{1,0:T(8,128)} %bitcast.28, bf16[2048,2048]{1,0:T(8,128)(2,1)} %geno_ref.5, s32[16,2048]{1,0:T(8,128)} %index_ref.5), custom_call_target="tpu_custom_call" | custom-call | flops 4294967296 | bytes 4194304 | tf_op jit(solution)/shard_map/select/pallas_call | solution.py:203
  45.9 1.6 owner_first.1
  47.5 11.6 %all_to_all.55 = f32[16,4,128]{2,1,0:T(4,128)S(1)} all-to-all(f32[16,4,128]{2,1,0:T(4,128)S(1)} %bitcast.31), channel_id=1, replica_groups=mesh['y_lo'=2,'z'=4,'core'=2,'y_hi'=2,'x'=4] {'y_lo','z','core'}, dimensions={0} | all-to-all | bytes 65536 | tf_op jit(solution)/shard_map/all_to_all | solution.py:564
  59.1 1.2 update.3
  61.6 10.1 %all_to_all.56.parts_ref = f32[8,8,1024]{2,1,0:T(8,128)S(1)} all-to-all(f32[8,8,1024]{2,1,0:T(8,128)S(1)} %spread.3), channel_id=1, replica_groups=mesh['y_lo'=2,'z'=4,'core'=2,'y_hi'=2,'x'=4] {'y_lo','z'}, dimensions={0} | all-to-all | bytes 524288 | tf_op jit(solution)/shard_map/all_to_all | solution.py:603
  71.8 1.2 collective-permute-done.5.other_ref
  73.8 17.3 %all_to_all.57 = f32[128,1,640]{2,1,0:T(1,128)S(1)} all-to-all(f32[128,1,640]{2,1,0:T(1,128)S(1)} %bitcast.21), channel_id=1, replica_groups=mesh['y_lo'=2,'z'=4,'core'=2,'y_hi'=2,'x'=4] {'y_hi','x','y_lo','z','core'}, dimensions={0} | all-to-all | bytes 655360 | tf_op jit(solution)/shard_map/all_to_all | solution.py:564
  92.1 8.7 %all_to_all.58 = f32[16,4,128]{2,1,0:T(4,128)S(1)} all-to-all(f32[16,4,128]{2,1,0:T(4,128)S(1)} %bitcast.30), channel_id=1, replica_groups=mesh['y_lo'=2,'z'=4,'core'=2,'y_hi'=2,'x'=4] {'y_lo','z','core'}, dimensions={0} | all-to-all | bytes 65536 | tf_op jit(solution)/shard_map/all_to_all | solution.py:564
  100.8 1.2 update.4
  103.4 10.1 %all_to_all.59.parts_ref = f32[8,8,1024]{2,1,0:T(8,128)S(1)} all-to-all(f32[8,8,1024]{2,1,0:T(8,128)S(1)} %spread.4), channel_id=1, replica_groups=mesh['y_lo'=2,'z'=4,'core'=2,'y_hi'=2,'x'=4] {'y_lo','z'}, dimensions={0} | all-to-all | bytes 524288 | tf_op jit(solution)/shard_map/all_to_all | solution.py:603
  113.6 1.2 collective-permute-done.7.other_ref
  115.6 16.0 %all_to_all.60 = f32[128,1,640]{2,1,0:T(1,128)S(1)} all-to-all(f32[128,1,640]{2,1,0:T(1,128)S(1)} %bitcast.20), channel_id=1, replica_groups=mesh['y_lo'=2,'z'=4,'core'=2,'y_hi'=2,'x'=4] {'y_hi','x','y_lo','z','core'}, dimensions={0} | all-to-all | bytes 655360 | tf_op jit(solution)/shard_map/all_to_all | solution.py:564
  132.6 8.7 %all_to_all.61 = f32[16,4,128]{2,1,0:T(4,128)S(1)} all-to-all(f32[16,4,128]{2,1,0:T(4,128)S(1)} %bitcast.29), channel_id=1, replica_groups=mesh['y_lo'=2,'z'=4,'core'=2,'y_hi'=2,'x'=4] {'y_lo','z','core'}, dimensions={0} | all-to-all | bytes 65536 | tf_op jit(solution)/shard_map/all_to_all | solution.py:564
  141.3 1.2 update.5
  143.7 10.1 %all_to_all.62.parts_ref = f32[8,8,1024]{2,1,0:T(8,128)S(1)} all-to-all(f32[8,8,1024]{2,1,0:T(8,128)S(1)} %spread.5), channel_id=1, replica_groups=mesh['y_lo'=2,'z'=4,'core'=2,'y_hi'=2,'x'=4] {'y_lo','z'}, dimensions={0} | all-to-all | bytes 524288 | tf_op jit(solution)/shard_map/all_to_all | solution.py:603
  153.9 1.2 collective-permute-done.9.other_ref
  155.3 11.2 %all_to_all.63.sums_ref = f32[8,8,128]{2,1,0:T(8,128)S(1)} all-to-all(f32[8,8,128]{2,1,0:T(8,128)S(1)} %get-tuple-element.83), channel_id=1, replica_groups=mesh['y_lo'=2,'z'=4,'core'=2,'y_hi'=2,'x'=4] {'y_hi','x'}, dimensions={0} | all-to-all | bytes 65536 | tf_op jit(solution)/shard_map/all_to_all | solution.py:621
  (50 shorter events, 12.0 us)
Async XLA Ops:
  0.6 23.0 %copy-start.3 = (s32[16,2048]{1,0:T(8,128)S(1)}, s32[16,2048]{1,0:T(8,128)}, u32[]{:S(2)}) copy-start(s32[16,2048]{1,0:T(8,128)} %index_ref.5) | copy-start | bytes 393220
  0.6 22.9 %copy-start.9 = (f32[16]{0:T(128)S(1)}, f32[16]{0:T(128)}, u32[]{:S(2)}) copy-start(f32[16]{0:T(128)} %table_ref.5) | copy-start | bytes 196
  8.7 8.9 %collective-permute-start = (f32[8,2048]{1,0:T(8,128)}, f32[8,2048]{1,0:T(8,128)S(1)}, u32[]{:S(2)}, u32[]{:S(2)}) collective-permute-start(f32[8,2048]{1,0:T(8,128)} %get-tuple-element.46), channel_id=1, source_target_pairs={{0,4},{4,0},{1,5},{5,1},{2,6},{6,2},{3,7},{7,3},{8,12},{12,8},{9,1... | collective-permute-start | bytes 196616 | tf_op jit(solution)/shard_map/ppermute | solution.py:571
  12.1 11.5 %all-to-all-start = ((s32[16,1,128]{2,1,0:T(1,128)}), s32[16,1,128]{2,1,0:T(1,128)S(1)}, u32[]{:S(2)}, u32[]{:S(2)}) async-start(s32[16,1,128]{2,1,0:T(1,128)} %bitcast.32), calls=%async_computation | async-start | bytes 16384 | tf_op jit(solution)/shard_map/all_to_all | solution.py:587
  18.5 12.3 %collective-permute-start.3 = (f32[8,2048]{1,0:T(8,128)S(1)}, f32[8,2048]{1,0:T(8,128)S(1)}, u32[]{:S(2)}, u32[]{:S(2)}) collective-permute-start(f32[8,2048]{1,0:T(8,128)S(1)} %add.3.own_ref), channel_id=1, source_target_pairs={{0,3},{1,0},{2,1},{3,2},{4,7},{5,4},{6,5},{7,6},{8,11},{9,8},{10,9... | collective-permute-start | bytes 196616 | tf_op jit(solution)/shard_map/ppermute | solution.py:571
  21.3 9.5 %collective-permute-start.2 = (f32[8,2048]{1,0:T(8,128)S(1)}, f32[8,2048]{1,0:T(8,128)S(1)}, u32[]{:S(2)}, u32[]{:S(2)}) collective-permute-start(f32[8,2048]{1,0:T(8,128)S(1)} %add.3.own_ref), channel_id=1, source_target_pairs={{0,2},{1,3},{2,0},{3,1},{4,6},{5,7},{6,4},{7,5},{8,10},{9,11},{10,... | collective-permute-start | bytes 196616 | tf_op jit(solution)/shard_map/ppermute | solution.py:571
  22.1 8.7 %collective-permute-start.1 = (f32[8,2048]{1,0:T(8,128)S(1)}, f32[8,2048]{1,0:T(8,128)S(1)}, u32[]{:S(2)}, u32[]{:S(2)}) collective-permute-start(f32[8,2048]{1,0:T(8,128)S(1)} %add.3.own_ref), channel_id=1, source_target_pairs={{0,1},{1,2},{2,3},{3,0},{4,5},{5,6},{6,7},{7,4},{8,9},{9,10},{10,1... | collective-permute-start | bytes 196616 | tf_op jit(solution)/shard_map/ppermute | solution.py:571
  23.6 7.3 %copy-start.4 = (s32[16,1,128]{2,1,0:T(1,128)}, s32[16,1,128]{2,1,0:T(1,128)S(1)}, u32[]{:S(2)}) copy-start(s32[16,1,128]{2,1,0:T(1,128)S(1)} %all-to-all-done) | copy-start | bytes 24580
  32.4 13.4 %all-to-all-start.1 = ((f32[16,4,128]{2,1,0:T(4,128)}), f32[16,4,128]{2,1,0:T(4,128)S(1)}, u32[]{:S(2)}, u32[]{:S(2)}) async-start(f32[16,4,128]{2,1,0:T(4,128)} %bitcast.5), calls=%async_computation.1 | async-start | bytes 65536 | tf_op jit(solution)/shard_map/all_to_all | solution.py:564
  37.6 8.3 %copy-start = (f32[2,256,256]{2,1,0:T(8,128)S(1)}, f32[2,256,256]{2,1,0:T(8,128)}, u32[]{:S(2)}) copy-start(f32[2,256,256]{2,1,0:T(8,128)} %inverse_ref.5) | copy-start | bytes 1572868
  37.6 8.3 %copy-start.5 = (s32[1,512]{1,0:T(1,128)S(1)}, s32[1,512]{1,0:T(1,128)}, u32[]{:S(2)}) copy-start(s32[1,512]{1,0:T(1,128)} %get-tuple-element.58.holder_ref) | copy-start | bytes 6148
  37.6 8.3 %copy-start.6 = (s32[1,512]{1,0:T(1,128)S(1)}, s32[1,512]{1,0:T(1,128)}, u32[]{:S(2)}) copy-start(s32[1,512]{1,0:T(1,128)} %get-tuple-element.57.serial_ref) | copy-start | bytes 6148
  37.6 8.3 %copy-start.7 = (f32[8,448]{1,0:T(8,128)S(1)}, f32[8,448]{1,0:T(8,128)}, u32[]{:S(2)}) copy-start(f32[8,448]{1,0:T(8,128)} %beta_ref.1) | copy-start | bytes 43012
  45.9 13.3 %copy-start.2 = (s32[8,128]{1,0:T(8,128)S(1)}, s32[8,128]{1,0:T(8,128)}, u32[]{:S(2)}) copy-start(s32[8,128]{1,0:T(8,128)} %get-tuple-element.53.core_ref) | copy-start | bytes 12292
  59.1 13.9 %copy-start.1 = (f32[8,2048]{1,0:T(8,128)S(1)}, f32[8,2048]{1,0:T(8,128)}, u32[]{:S(2)}) copy-start(f32[8,2048]{1,0:T(8,128)} %resid_in.1) | copy-start | bytes 196612
  59.1 13.9 %copy-start.8 = (s32[8,128]{1,0:T(8,128)S(1)}, s32[8,128]{1,0:T(8,128)}, u32[]{:S(2)}) copy-start(s32[8,128]{1,0:T(8,128)} %get-tuple-element.54.rank_ref) | copy-start | bytes 12292
  60.3 1.2 collective-permute-start.4
  71.7 1.3 collective-permute-start.5
  102.0 1.4 collective-permute-start.6
  113.5 1.3 collective-permute-start.7
  142.4 1.2 collective-permute-start.8
  153.9 1.3 collective-permute-start.9

commit v5 on v4

--- a/solution.py
+++ b/solution.py
@@ -22,7 +22,7 @@
 penalty = 0.5
 epsilon = 1e-06
 SMALL = pltpu.CompilerParams(vmem_limit_bytes=12 * 1024 * 1024)
-MEDIUM = pltpu.CompilerParams(vmem_limit_bytes=50 * 1024 * 1024)
+MEDIUM = pltpu.CompilerParams(vmem_limit_bytes=48 * 1024 * 1024)
 LARGE = pltpu.CompilerParams(vmem_limit_bytes=60 * 1024 * 1024)
 f32 = jnp.float32
 bf16 = jnp.bfloat16
@@ -220,39 +220,43 @@
     )(table, packed, geno, index)
 
 
-def pick_kernel(
-    inv_root, own_ref, one_ref, two_ref, three_ref, packed_hbm, scores_ref, pay_ref, packed_ref, sem
-):
-    copy = pltpu.make_async_copy(packed_hbm, packed_ref, sem)
-    copy.start()
-    scores = ((own_ref[...] + two_ref[...]) + (one_ref[...] + three_ref[...])) * inv_root
-    scores_ref[...] = scores
-    copy.wait()
+def pick_kernel(inv_root, part_ref, packed_ref, pay_ref):
+    part = part_ref[...] * inv_root
     wanted = column_row(packed_ref[...])
-    stacked = jnp.concatenate(thirds(scores), 0)
-    phenos, width = scores.shape
+    stacked = jnp.concatenate(thirds(part), 0)
+    phenos, width = part.shape
     total = jnp.zeros((stacked.shape[0], wanted.shape[1]), f32)
     for at in range(0, width, ROWS):
         here = iota((ROWS, wanted.shape[1]), 0) + (at + 1) == wanted
         total += dot(stacked[:, at : at + ROWS], here.astype(f32).astype(bf16))
     held = total[:phenos] + total[phenos : 2 * phenos] + total[2 * phenos :]
+    rows = packed_ref.shape[0] * HALF
     for t in range(wanted.shape[1] // LANES):
-        pay_ref[8 * t : 8 * t + 8, :] = swapped(held[:, t * LANES : (t + 1) * LANES])
-
-
-def pick(parts, packed, inv_root):
+        pair = swapped(held[:, t * LANES : (t + 1) * LANES])
+        for at in range(8 * t, pay_ref.shape[0], rows):
+            pay_ref[at : at + 8, :] = pair
+
+
+def pick(part, packed, inv_root, copies):
     return pl.pallas_call(
         functools.partial(pick_kernel, inv_root),
-        in_specs=[pl.BlockSpec(memory_space=pltpu.VMEM)] * 4
-        + [pl.BlockSpec(memory_space=pltpu.HBM)],
-        scratch_shapes=[pltpu.VMEM(packed.shape, packed.dtype), pltpu.SemaphoreType.DMA],
-        out_shape=(
-            jax.ShapeDtypeStruct(parts[0].shape, f32),
-            jax.ShapeDtypeStruct((packed.shape[0] * HALF, LANES), f32),
-        ),
+        out_shape=jax.ShapeDtypeStruct((copies * packed.shape[0] * HALF, LANES), f32),
         compiler_params=SMALL,
         name="pick",
-    )(*parts, packed)
+    )(part, packed)
+
+
+def tally_kernel(inv_root, own_ref, one_ref, two_ref, three_ref, scores_ref):
+    scores_ref[...] = ((own_ref[...] + two_ref[...]) + (one_ref[...] + three_ref[...])) * inv_root
+
+
+def tally(parts, inv_root):
+    return pl.pallas_call(
+        functools.partial(tally_kernel, inv_root),
+        out_shape=jax.ShapeDtypeStruct(parts[0].shape, f32),
+        compiler_params=SMALL,
+        name="tally",
+    )(*parts)
 
 
 def direction_step(data, serial_ref, holder_ref, inverse_ref, advance, wide_ref, d_ref, pay_ref):
@@ -286,17 +290,16 @@
     holder_ref,
     inverse_ref,
     beta_ref,
-    columns_hbm,
     pay_ref,
     b_ref,
     d_ref,
     g_ref,
-    columns_ref,
     wide_ref,
-    sem,
 ):
-    copy = pltpu.make_async_copy(columns_hbm, columns_ref, sem)
-    copy.start()
+    rows = pay_ref.shape[0]
+    data = data_ref[:rows, :]
+    for at in range(rows, data_ref.shape[0], rows):
+        data = data + data_ref[at : at + rows, :]
     fit = serial_ref.shape[1]
     active = beta_ref.shape[1]
     b_ref[...] = jnp.zeros_like(b_ref)
@@ -307,10 +310,7 @@
         g_ref[...] = arrived
         return arrived - penalty * b_ref[...]
 
-    direction_step(
-        data_ref[...], serial_ref, holder_ref, inverse_ref, advance, wide_ref, d_ref, pay_ref
-    )
-    copy.wait()
+    direction_step(data, serial_ref, holder_ref, inverse_ref, advance, wide_ref, d_ref, pay_ref)
 
 
 def owner_kernel(
@@ -359,25 +359,17 @@
     )
 
 
-def owner_first(data, serial, holder, inverse, beta, columns):
+def owner_first(data, serial, holder, inverse, beta):
     fit = serial.shape[1]
     held = jax.ShapeDtypeStruct((HALF, 2 * fit), f32)
-    vmem = pl.BlockSpec(memory_space=pltpu.VMEM)
+    pay = jax.ShapeDtypeStruct((lax.axis_size(VAR) * HALF, LANES), f32)
     return pl.pallas_call(
         first_owner_kernel,
-        in_specs=[vmem] * 5 + [pl.BlockSpec(memory_space=pltpu.HBM)],
-        out_specs=(vmem,) * 5,
-        out_shape=(
-            jax.ShapeDtypeStruct(data.shape, f32),
-            held,
-            held,
-            held,
-            jax.ShapeDtypeStruct(columns.shape, columns.dtype),
-        ),
-        scratch_shapes=[pltpu.VMEM((2 * HALF, fit), f32), pltpu.SemaphoreType.DMA],
-        compiler_params=MEDIUM,
+        out_shape=(pay, held, held, held),
+        scratch_shapes=[pltpu.VMEM((2 * HALF, fit), f32)],
+        compiler_params=SMALL,
         name="owner_first",
-    )(data, serial, holder, inverse, beta, columns)
+    )(data, serial, holder, inverse, beta)
 
 
 def owner_next(data, serial, holder, inverse, state, resid, update, final):
@@ -402,17 +394,19 @@
     )(data, serial, holder, inverse, *state, resid, update)
 
 
-def update_kernel(core_ref, pay_ref, first_ref, second_ref, keep_ref, send_ref):
+def update_kernel(core_ref, pay_ref, first_ref, second_ref, keep_ref, send_ref, ready=None):
     packed = jnp.concatenate(
         [swapped(pay_ref[at : at + 8, :]) for at in range(0, pay_ref.shape[0], 8)], 1
     ).astype(bf16)
-    first = core_ref[:, :1] == 0
-    half = keep_ref.shape[1]
-    for at in range(0, half, ROWS):
-        a = dot_t(packed, first_ref[at : at + ROWS, :])
+    mine = core_ref[:, :1] == 0
+    blocks = range(0, keep_ref.shape[1], ROWS)
+    early = [dot_t(packed, first_ref[at : at + ROWS, :]) for at in blocks]
+    if ready is not None:
+        ready()
+    for a, at in zip(early, blocks):
         b = dot_t(packed, second_ref[at : at + ROWS, :])
-        keep_ref[:, at : at + ROWS] = jnp.where(first, a, b)
-        send_ref[:, at : at + ROWS] = jnp.where(first, b, a)
+        keep_ref[:, at : at + ROWS] = jnp.where(mine, a, b)
+        send_ref[:, at : at + ROWS] = jnp.where(mine, b, a)
 
 
 def partial_update(core, pay, first, second):
@@ -422,6 +416,28 @@
         out_shape=(half, half),
         compiler_params=SMALL,
         name="update",
+    )(core, pay, first, second)
+
+
+def fetching_kernel(
+    core_ref, pay_ref, first_ref, second_hbm, keep_ref, send_ref, second_ref, sem
+):
+    copy = pltpu.make_async_copy(second_hbm, second_ref, sem)
+    copy.start()
+    update_kernel(core_ref, pay_ref, first_ref, second_ref, keep_ref, send_ref, copy.wait)
+
+
+def first_update(core, pay, first, second):
+    half = jax.ShapeDtypeStruct((2 * HALF, first.shape[0]), f32)
+    vmem = pl.BlockSpec(memory_space=pltpu.VMEM)
+    return pl.pallas_call(
+        fetching_kernel,
+        in_specs=[vmem] * 3 + [pl.BlockSpec(memory_space=pltpu.HBM)],
+        out_specs=(vmem,) * 3,
+        out_shape=(half, half, jax.ShapeDtypeStruct(second.shape, second.dtype)),
+        scratch_shapes=[pltpu.SemaphoreType.DMA],
+        compiler_params=MEDIUM,
+        name="update_first",
     )(core, pay, first, second)
 
 
@@ -513,25 +529,25 @@
     )(rank, core, mine, other, resid, first, second)
 
 
-def settle_kernel(inv_root, core_ref, mine_ref, other_ref, resid_ref, sums_ref, update_ref):
-    update = whole_update(inv_root, core_ref, mine_ref, other_ref)
-    update_ref[...] = update
-    sums_ref[...] = jnp.broadcast_to(step_sums(resid_ref[...], update)[None], sums_ref.shape)
-
-
-def settle(core, mine, other, resid, inv_root, copies):
+def settle_kernel(inv_root, core_ref, mine_ref, resid_ref, sums_ref):
+    half = mine_ref.shape[1]
+    resid = jnp.where(core_ref[:, :1] == 0, resid_ref[:, :half], resid_ref[:, half:])
+    sums = step_sums(resid, mine_ref[...] * inv_root)
+    sums_ref[...] = jnp.broadcast_to(sums[None], sums_ref.shape)
+
+
+def settle(core, mine, resid, inv_root, copies):
     return pl.pallas_call(
         functools.partial(settle_kernel, inv_root),
-        out_shape=(
-            jax.ShapeDtypeStruct((copies, resid.shape[0], LANES), f32),
-            jax.ShapeDtypeStruct(resid.shape, f32),
-        ),
+        out_shape=jax.ShapeDtypeStruct((copies, resid.shape[0], LANES), f32),
         compiler_params=SMALL,
         name="settle",
-    )(core, mine, other, resid)
-
-
-def last_kernel(sums_ref, b_ref, d_ref, resid_ref, update_ref, coeffs_ref, out_ref):
+    )(core, mine, resid)
+
+
+def last_kernel(
+    inv_root, sums_ref, core_ref, mine_ref, other_ref, b_ref, d_ref, resid_ref, coeffs_ref, out_ref
+):
     phenos, fit = coeffs_ref.shape
     total = sums_ref[0]
     for j in range(1, sums_ref.shape[0]):
@@ -541,20 +557,21 @@
         rows = slice(half * HALF, (half + 1) * HALF)
         cols = slice(half * fit, (half + 1) * fit)
         coeffs_ref[rows, :] = b_ref[:, cols] + factor[rows] * d_ref[:, cols]
-    out_ref[...] = resid_ref[...] - factor * update_ref[...]
-
-
-def last(sums, coeffs, direction, resid, update):
+    update = whole_update(inv_root, core_ref, mine_ref, other_ref)
+    out_ref[...] = resid_ref[...] - factor * update
+
+
+def last(sums, core, mine, other, coeffs, direction, resid, inv_root):
     phenos = resid.shape[0]
     return pl.pallas_call(
-        last_kernel,
+        functools.partial(last_kernel, inv_root),
         out_shape=(
             jax.ShapeDtypeStruct((phenos, coeffs.shape[1] // 2), f32),
             jax.ShapeDtypeStruct(resid.shape, f32),
         ),
         compiler_params=SMALL,
         name="last",
-    )(sums, coeffs, direction, resid, update)
+    )(sums, core, mine, other, coeffs, direction, resid)
 
 
 def exchange(pay, axes):
@@ -582,23 +599,27 @@
     part, holder, serial, packed, rank, core = screen(
         scale_table, geno, scale_index, residual, active_ids, admit_ids
     )
-    part = part + shifted(part, "y_hi")
-    parts = [part] + [shifted(part, "x", n) for n in range(1, lax.axis_size("x"))]
     packed = lax.all_to_all(
         packed.reshape(holders, 1, LANES), VAR, split_axis=0, concat_axis=0, tiled=True
     ).reshape(holders, LANES)
 
+    pay = pick(part, packed, inv_root, copies)
+    pay, packed, part = lax.optimization_barrier((pay, packed, part))
+    part = part + shifted(part, "y_hi")
     first = select(0, scale_table, packed, geno, scale_index, MEDIUM)
-    parts, first = lax.optimization_barrier((parts, first))
-    scores, pay = pick(parts, packed, inv_root)
+    data, first, part = lax.optimization_barrier((exchange(pay, SAMP + VAR), first, part))
+    pay, *state = owner_first(data, serial, holder, block_inverse, beta_active)
+    parts = [part] + [shifted(part, "x", n) for n in range(1, lax.axis_size("x"))]
     pay, packed = lax.optimization_barrier((pay, packed))
     second = select(1, scale_table, packed, geno, scale_index, LARGE)
-    pay, *state, second = owner_first(
-        exchange(pay, VAR), serial, holder, block_inverse, beta_active, second
-    )
+    pay, second, parts = lax.optimization_barrier((exchange(pay, VAR), second, parts))
+    scores = tally(parts, inv_root)
     current = residual
     for pass_index in range(PASSES):
-        keep, send = partial_update(core, exchange(pay, VAR), first, second)
+        if pass_index == 0:
+            keep, send, second = first_update(core, pay, first, second)
+        else:
+            keep, send = partial_update(core, exchange(pay, VAR), first, second)
         mine = spread(keep, shifted(send, "core"), lax.axis_size(CHIPS))
         mine = total(lax.all_to_all(mine, CHIPS, split_axis=0, concat_axis=0, tiled=True))
         other = shifted(mine, "core")
@@ -617,9 +638,9 @@
         )
         state = (coeffs, direction, *gradient)
 
-    sums, update = settle(core, mine, other, current, inv_root, copies)
-    sums = lax.all_to_all(sums, SAMP, split_axis=0, concat_axis=0, tiled=True)
-    return (scores, *last(sums, coeffs, direction, current, update))
+    sums = settle(core, mine, current, inv_root, 2 * copies)
+    sums = lax.all_to_all(sums, ("core",) + SAMP, split_axis=0, concat_axis=0, tiled=True)
+    return (scores, *last(sums, core, mine, other, coeffs, direction, current, inv_root))
 
 
 def solution(mesh):

time: 168 us -> 175 us (1.042)
  blocking collectives: 104 us -> 96.3 us
  waiting for transfers between devices: 7.48 us -> 13 us
  starting transfers between devices: 19.3 us -> 24 us
  Pallas kernels: 34.9 us -> 37.8 us
    all_to_all x5 -> x4, blocking collectives: 62.2 us -> 50.6 us  [exchange(): lax.all_to_all(pay.reshape(shape), axes, split_axis=0, concat_axis=0, til...]
    all_to_all x1 -> x2, starting transfers between devices: 5.13 us -> 12.9 us  [exchange(): lax.all_to_all(pay.reshape(shape), axes, split_axis=0, concat_axis=0, til...]
    all_to_all x1, waiting for transfers between devices: 0.6 us -> 6.38 us  [on_device(): lax.all_to_all(sums, ('core',) + SAMP, split_axis=0, concat_axis=0, tiled...]
    pallas_call x4 -> x6, Pallas kernels: 4.12 us -> 8.25 us  [the longest x1 2.77 us: first_update(): pl.pallas_call(fetching_kernel, in_specs=[vmem] * 3 + [pl.BlockSpec(memor...]
    all_to_all x3, blocking collectives: 30.4 us -> 33.1 us  [on_device(): lax.all_to_all(mine, CHIPS, split_axis=0, concat_axis=0, tiled=True)]
    all_to_all x1, starting transfers between devices: 5.53 us -> 3.72 us  [on_device(): lax.all_to_all(sums, ('core',) + SAMP, split_axis=0, concat_axis=0, tiled...]
    pallas_call x3 -> x2, Pallas kernels: 3.55 us -> 2.37 us  [partial_update(): pl.pallas_call(update_kernel, out_shape=(half, half), compiler_params=SMA...]
  transfers between devices with their start and end apart: 12 -> 13, of which waited for: 7 -> 8; matrix products, arithmetic and copies ran while one was open for 1% -> 0% of each run, Pallas kernels for 9% -> 10%
where the time goes in v5:
time: 175 us; the launch traced here: 173 us
  blocking collectives  96.3 us (55%)
  Pallas kernels  37.8 us (22%)
  starting transfers between devices  24 us (14%)
  waiting for transfers between devices  13 us (7%)
    all_to_all x4, blocking collectives, exchange(): lax.all_to_all(pay.reshape(shape), axes, split_axis=0, concat_axis=0, til...  50.6 us
    all_to_all x3, blocking collectives, on_device(): lax.all_to_all(mine, CHIPS, split_axis=0, concat_axis=0, tiled=True)  33.1 us
    pallas_call x2, Pallas kernels, select(): pl.pallas_call(functools.partial(select_kernel, first), grid=(samples //...  15.4 us
    all_to_all x2, starting transfers between devices, exchange(): lax.all_to_all(pay.reshape(shape), axes, split_axis=0, concat_axis=0, til...  12.9 us
    all_to_all x1, blocking collectives, on_device(): lax.all_to_all(packed.reshape(holders, 1, LANES), VAR, split_axis=0, conc...  12.5 us
    pallas_call x1, Pallas kernels, screen(): pl.pallas_call(screen_kernel, grid=(samples // ROWS,), in_specs=[pl.Block...  8.05 us
    ppermute x10, starting transfers between devices, shifted(): return lax.ppermute(x, axis, [(i, (i + by) % size) for i in range(size)])  7.45 us
    all_to_all x1, waiting for transfers between devices, on_device(): lax.all_to_all(sums, ('core',) + SAMP, split_axis=0, concat_axis=0, tiled...  6.38 us
  transfers between devices with their start and end apart: 13, of which 8 were waited for; matrix products, arithmetic and copies ran while one was open for 0% of the time, Pallas kernels for 10%

profile of v5, /device:TPU:0, one launch (start us, length us, event | category | flops | bytes accessed | tf_op | source)
XLA Modules:
  0.0 172.9 jit_solution(13651650341329696171)
XLA Ops:
  0.7 8.0 %screen.1 = (f32[8,2048]{1,0:T(8,128)}, s32[1,512]{1,0:T(1,128)}, s32[1,512]{1,0:T(1,128)}, s32[16,128]{1,0:T(8,128)}, s32[8,128]{1,0:T(8,128)}, /*index=5*/s32[8,128]{1,0:T(8,128)}) custom-call(f32[16]{0:T(128)} %table_ref.5, bf16[2048,2048]{1,0:T(8,128)(2,1)} %geno_ref.5, s32[16,2048]{1,0:T(8,128)} %index_ref.5, f32[8,2048]{1,0:T(8,128)} %resid_in.1, ...), custom_call_target="tpu_custom_call" | custom-call | flops 67108864 | bytes 8388608 | tf_op jit(solution)/shard_map/screen/pallas_call | solution.py:159
  8.7 12.5 %all_to_all.55 = s32[16,1,128]{2,1,0:T(1,128)S(1)} all-to-all(s32[16,1,128]{2,1,0:T(1,128)} %bitcast.31), channel_id=1, replica_groups=mesh['y_lo'=2,'z'=4,'core'=2,'y_hi'=2,'x'=4] {'y_lo','z','core'}, dimensions={0} | all-to-all | bytes 16384 | tf_op jit(solution)/shard_map/all_to_all | solution.py:602
  22.1 1.6 pick.1
  23.7 7.9 %all-to-all-start.1 = ((f32[128,4,128]{2,1,0:T(4,128)}), f32[128,4,128]{2,1,0:T(4,128)S(1)}, u32[]{:S(2)}, u32[]{:S(2)}) async-start(f32[128,4,128]{2,1,0:T(4,128)} %bitcast.5), calls=%async_computation.1 | async-start | bytes 524288 | tf_op jit(solution)/shard_map/all_to_all | solution.py:581
  31.6 2.5 %collective-permute-start = (f32[8,2048]{1,0:T(8,128)}, f32[8,2048]{1,0:T(8,128)S(1)}, u32[]{:S(2)}, u32[]{:S(2)}) collective-permute-start(f32[8,2048]{1,0:T(8,128)} %get-tuple-element.53.part_ref), channel_id=1, source_target_pairs={{0,4},{4,0},{1,5},{5,1},{2,6},{6,2},{3,7},{7,3},{8,12},{12,8},{9,1... | collective-permute-start | bytes 196616 | tf_op jit(solution)/shard_map/ppermute | solution.py:588
  34.2 7.2 %select.2.first_ref = bf16[1024,1024]{1,0:T(8,128)(2,1)S(1)} custom-call(f32[16]{0:T(128)S(1)} %copy-done.11, s32[16,128]{1,0:T(8,128)S(1)} %bitcast.29, bf16[2048,2048]{1,0:T(8,128)(2,1)} %geno_ref.5, s32[16,2048]{1,0:T(8,128)S(1)} %copy-done.5), custom_call_target="tpu_custom_call" | custom-call | flops 4294967296 | bytes 4194304 | tf_op jit(solution)/shard_map/select/pallas_call | solution.py:203
  42.4 1.9 %collective-permute-start.3 = (f32[8,2048]{1,0:T(8,128)S(1)}, f32[8,2048]{1,0:T(8,128)S(1)}, u32[]{:S(2)}, u32[]{:S(2)}) collective-permute-start(f32[8,2048]{1,0:T(8,128)S(1)} %add.3.own_ref), channel_id=1, source_target_pairs={{0,3},{1,0},{2,1},{3,2},{4,7},{5,4},{6,5},{7,6},{8,11},{9,8},{10,9... | collective-permute-start | bytes 196616 | tf_op jit(solution)/shard_map/ppermute | solution.py:588
  45.9 1.6 owner_first.1
  47.6 5.0 %all-to-all-start.2 = ((f32[16,4,128]{2,1,0:T(4,128)}), f32[16,4,128]{2,1,0:T(4,128)S(1)}, u32[]{:S(2)}, u32[]{:S(2)}) async-start(f32[16,4,128]{2,1,0:T(4,128)} %bitcast.7), calls=%async_computation.2 | async-start | bytes 65536 | tf_op jit(solution)/shard_map/all_to_all | solution.py:581
  52.6 8.2 %select.3.second_hbm = bf16[1024,1024]{1,0:T(8,128)(2,1)} custom-call(f32[16]{0:T(128)} %table_ref.5, s32[16,128]{1,0:T(8,128)} %bitcast.30, bf16[2048,2048]{1,0:T(8,128)(2,1)} %geno_ref.5, s32[16,2048]{1,0:T(8,128)} %index_ref.5), custom_call_target="tpu_custom_call" | custom-call | flops 4294967296 | bytes 4194304 | tf_op jit(solution)/shard_map/select/pallas_call | solution.py:203
  60.8 2.8 %update_first.1 = (f32[8,1024]{1,0:T(8,128)S(1)}, f32[8,1024]{1,0:T(8,128)S(1)}, bf16[1024,1024]{1,0:T(8,128)(2,1)S(1)}) custom-call(s32[8,128]{1,0:T(8,128)S(1)} %copy-done.4, f32[64,128]{1,0:T(8,128)S(1)} %bitcast.23, bf16[1024,1024]{1,0:T(8,128)(2,1)S(1)} %select.2.first_ref, bf16[1024,1024]{1,0:T(8,128)(2,1)} %select.3.second_hbm), custom_call_target="tpu_custom_call" | custom-call | tf_op jit(solution)/shard_map/update_first/pallas_call | solution.py:433
  65.0 12.9 %all_to_all.56.parts_ref = f32[8,8,1024]{2,1,0:T(8,128)S(1)} all-to-all(f32[8,8,1024]{2,1,0:T(8,128)S(1)} %spread.3), channel_id=1, replica_groups=mesh['y_lo'=2,'z'=4,'core'=2,'y_hi'=2,'x'=4] {'y_lo','z'}, dimensions={0} | all-to-all | bytes 524288 | tf_op jit(solution)/shard_map/all_to_all | solution.py:624
  78.0 1.2 collective-permute-done.5.other_ref
  80.0 17.3 %all_to_all.57 = f32[128,1,640]{2,1,0:T(1,128)S(1)} all-to-all(f32[128,1,640]{2,1,0:T(1,128)S(1)} %bitcast.22), channel_id=1, replica_groups=mesh['y_lo'=2,'z'=4,'core'=2,'y_hi'=2,'x'=4] {'y_hi','x','y_lo','z','core'}, dimensions={0} | all-to-all | bytes 655360 | tf_op jit(solution)/shard_map/all_to_all | solution.py:581
  98.3 8.7 %all_to_all.58 = f32[16,4,128]{2,1,0:T(4,128)S(1)} all-to-all(f32[16,4,128]{2,1,0:T(4,128)S(1)} %bitcast.27), channel_id=1, replica_groups=mesh['y_lo'=2,'z'=4,'core'=2,'y_hi'=2,'x'=4] {'y_lo','z','core'}, dimensions={0} | all-to-all | bytes 65536 | tf_op jit(solution)/shard_map/all_to_all | solution.py:581
  106.9 1.2 update.2
  109.4 10.1 %all_to_all.59.parts_ref = f32[8,8,1024]{2,1,0:T(8,128)S(1)} all-to-all(f32[8,8,1024]{2,1,0:T(8,128)S(1)} %spread.4), channel_id=1, replica_groups=mesh['y_lo'=2,'z'=4,'core'=2,'y_hi'=2,'x'=4] {'y_lo','z'}, dimensions={0} | all-to-all | bytes 524288 | tf_op jit(solution)/shard_map/all_to_all | solution.py:624
  119.6 1.2 collective-permute-done.7.other_ref
  121.6 16.0 %all_to_all.60 = f32[128,1,640]{2,1,0:T(1,128)S(1)} all-to-all(f32[128,1,640]{2,1,0:T(1,128)S(1)} %bitcast.21), channel_id=1, replica_groups=mesh['y_lo'=2,'z'=4,'core'=2,'y_hi'=2,'x'=4] {'y_hi','x','y_lo','z','core'}, dimensions={0} | all-to-all | bytes 655360 | tf_op jit(solution)/shard_map/all_to_all | solution.py:581
  138.6 8.7 %all_to_all.61 = f32[16,4,128]{2,1,0:T(4,128)S(1)} all-to-all(f32[16,4,128]{2,1,0:T(4,128)S(1)} %bitcast.26), channel_id=1, replica_groups=mesh['y_lo'=2,'z'=4,'core'=2,'y_hi'=2,'x'=4] {'y_lo','z','core'}, dimensions={0} | all-to-all | bytes 65536 | tf_op jit(solution)/shard_map/all_to_all | solution.py:581
  147.3 1.2 update.3
  149.7 10.1 %all_to_all.62.parts_ref = f32[8,8,1024]{2,1,0:T(8,128)S(1)} all-to-all(f32[8,8,1024]{2,1,0:T(8,128)S(1)} %spread.5), channel_id=1, replica_groups=mesh['y_lo'=2,'z'=4,'core'=2,'y_hi'=2,'x'=4] {'y_lo','z'}, dimensions={0} | all-to-all | bytes 524288 | tf_op jit(solution)/shard_map/all_to_all | solution.py:624
  160.7 3.7 %all-to-all-start.10 = ((f32[16,8,128]{2,1,0:T(8,128)}), f32[16,8,128]{2,1,0:T(8,128)S(1)}, u32[]{:S(2)}, u32[]{:S(2)}) async-start(f32[16,8,128]{2,1,0:T(8,128)} %settle.1), calls=%async_computation.10 | async-start | bytes 131072 | tf_op jit(solution)/shard_map/all_to_all | solution.py:642
  165.7 6.4 %all-to-all-done.10.sums_ref = f32[16,8,128]{2,1,0:T(8,128)S(1)} async-done(((f32[16,8,128]{2,1,0:T(8,128)}), f32[16,8,128]{2,1,0:T(8,128)S(1)}, u32[]{:S(2)}, u32[]{:S(2)}) %all-to-all-start.10) | async-done | bytes 65568 | tf_op jit(solution)/shard_map/all_to_all | solution.py:642
  (56 shorter events, 14.1 us)
Async XLA Ops:
  0.6 33.6 %copy-start.5 = (s32[16,2048]{1,0:T(8,128)S(1)}, s32[16,2048]{1,0:T(8,128)}, u32[]{:S(2)}) copy-start(s32[16,2048]{1,0:T(8,128)} %index_ref.5) | copy-start | bytes 393220
  0.6 33.5 %copy-start.11 = (f32[16]{0:T(128)S(1)}, f32[16]{0:T(128)}, u32[]{:S(2)}) copy-start(f32[16]{0:T(128)} %table_ref.5) | copy-start | bytes 196
  21.2 20.2 %copy-start.6 = (s32[16,1,128]{2,1,0:T(1,128)}, s32[16,1,128]{2,1,0:T(1,128)S(1)}, u32[]{:S(2)}) copy-start(s32[16,1,128]{2,1,0:T(1,128)S(1)} %all_to_all.55) | copy-start | bytes 24580
  23.7 18.7 %all-to-all-start.1 = ((f32[128,4,128]{2,1,0:T(4,128)}), f32[128,4,128]{2,1,0:T(4,128)S(1)}, u32[]{:S(2)}, u32[]{:S(2)}) async-start(f32[128,4,128]{2,1,0:T(4,128)} %bitcast.5), calls=%async_computation.1 | async-start | bytes 524288 | tf_op jit(solution)/shard_map/all_to_all | solution.py:581
  31.6 9.9 %copy-start.3 = (f32[8,2048]{1,0:T(8,128)S(1)}, f32[8,2048]{1,0:T(8,128)}, u32[]{:S(2)}) copy-start(f32[8,2048]{1,0:T(8,128)} %get-tuple-element.53.part_ref) | copy-start | bytes 196612
  31.6 14.4 %copy-start = (f32[2,256,256]{2,1,0:T(8,128)S(1)}, f32[2,256,256]{2,1,0:T(8,128)}, u32[]{:S(2)}) copy-start(f32[2,256,256]{2,1,0:T(8,128)} %inverse_ref.5) | copy-start | bytes 1572868
  31.6 14.3 %copy-start.7 = (s32[1,512]{1,0:T(1,128)S(1)}, s32[1,512]{1,0:T(1,128)}, u32[]{:S(2)}) copy-start(s32[1,512]{1,0:T(1,128)} %get-tuple-element.56.holder_ref) | copy-start | bytes 6148
  31.6 14.3 %copy-start.8 = (s32[1,512]{1,0:T(1,128)S(1)}, s32[1,512]{1,0:T(1,128)}, u32[]{:S(2)}) copy-start(s32[1,512]{1,0:T(1,128)} %get-tuple-element.55.serial_ref) | copy-start | bytes 6148
  31.6 14.3 %copy-start.9 = (f32[8,448]{1,0:T(8,128)S(1)}, f32[8,448]{1,0:T(8,128)}, u32[]{:S(2)}) copy-start(f32[8,448]{1,0:T(8,128)} %beta_ref.1) | copy-start | bytes 43012
  31.6 9.8 %collective-permute-start = (f32[8,2048]{1,0:T(8,128)}, f32[8,2048]{1,0:T(8,128)S(1)}, u32[]{:S(2)}, u32[]{:S(2)}) collective-permute-start(f32[8,2048]{1,0:T(8,128)} %get-tuple-element.53.part_ref), channel_id=1, source_target_pairs={{0,4},{4,0},{1,5},{5,1},{2,6},{6,2},{3,7},{7,3},{8,12},{12,8},{9,1... | collective-permute-start | bytes 196616 | tf_op jit(solution)/shard_map/ppermute | solution.py:588
  42.4 18.4 %collective-permute-start.3 = (f32[8,2048]{1,0:T(8,128)S(1)}, f32[8,2048]{1,0:T(8,128)S(1)}, u32[]{:S(2)}, u32[]{:S(2)}) collective-permute-start(f32[8,2048]{1,0:T(8,128)S(1)} %add.3.own_ref), channel_id=1, source_target_pairs={{0,3},{1,0},{2,1},{3,2},{4,7},{5,4},{6,5},{7,6},{8,11},{9,8},{10,9... | collective-permute-start | bytes 196616 | tf_op jit(solution)/shard_map/ppermute | solution.py:588
  44.2 16.6 %collective-permute-start.2 = (f32[8,2048]{1,0:T(8,128)S(1)}, f32[8,2048]{1,0:T(8,128)S(1)}, u32[]{:S(2)}, u32[]{:S(2)}) collective-permute-start(f32[8,2048]{1,0:T(8,128)S(1)} %add.3.own_ref), channel_id=1, source_target_pairs={{0,2},{1,3},{2,0},{3,1},{4,6},{5,7},{6,4},{7,5},{8,10},{9,11},{10,... | collective-permute-start | bytes 196616 | tf_op jit(solution)/shard_map/ppermute | solution.py:588
  45.1 15.7 %collective-permute-start.1 = (f32[8,2048]{1,0:T(8,128)S(1)}, f32[8,2048]{1,0:T(8,128)S(1)}, u32[]{:S(2)}, u32[]{:S(2)}) collective-permute-start(f32[8,2048]{1,0:T(8,128)S(1)} %add.3.own_ref), channel_id=1, source_target_pairs={{0,1},{1,2},{2,3},{3,0},{4,5},{5,6},{6,7},{7,4},{8,9},{9,10},{10,1... | collective-permute-start | bytes 196616 | tf_op jit(solution)/shard_map/ppermute | solution.py:588
  47.6 13.2 %all-to-all-start.2 = ((f32[16,4,128]{2,1,0:T(4,128)}), f32[16,4,128]{2,1,0:T(4,128)S(1)}, u32[]{:S(2)}, u32[]{:S(2)}) async-start(f32[16,4,128]{2,1,0:T(4,128)} %bitcast.7), calls=%async_computation.2 | async-start | bytes 65536 | tf_op jit(solution)/shard_map/all_to_all | solution.py:581
  52.6 8.3 %copy-start.4 = (s32[8,128]{1,0:T(8,128)S(1)}, s32[8,128]{1,0:T(8,128)}, u32[]{:S(2)}) copy-start(s32[8,128]{1,0:T(8,128)} %get-tuple-element.65.core_ref) | copy-start | bytes 12292
  60.8 18.4 %copy-start.1 = (f32[8,2048]{1,0:T(8,128)S(1)}, f32[8,2048]{1,0:T(8,128)}, u32[]{:S(2)}) copy-start(f32[8,2048]{1,0:T(8,128)} %resid_in.1) | copy-start | bytes 196612
  60.8 18.4 %copy-start.10 = (s32[8,128]{1,0:T(8,128)S(1)}, s32[8,128]{1,0:T(8,128)}, u32[]{:S(2)}) copy-start(s32[8,128]{1,0:T(8,128)} %get-tuple-element.66.rank_ref) | copy-start | bytes 12292
  63.6 1.3 collective-permute-start.4
  77.9 1.3 collective-permute-start.5
  108.1 1.2 collective-permute-start.6
  119.5 1.3 collective-permute-start.7
  148.5 1.2 collective-permute-start.8
  160.7 11.4 %all-to-all-start.10 = ((f32[16,8,128]{2,1,0:T(8,128)}), f32[16,8,128]{2,1,0:T(8,128)S(1)}, u32[]{:S(2)}, u32[]{:S(2)}) async-start(f32[16,8,128]{2,1,0:T(8,128)} %settle.1), calls=%async_computation.10 | async-start | bytes 131072 | tf_op jit(solution)/shard_map/all_to_all | solution.py:642
  164.4 1.3 collective-permute-start.9
  (1 other events, 0.8 us)

commit v6 on v4

--- a/solution.py
+++ b/solution.py
@@ -23,6 +23,7 @@
 epsilon = 1e-06
 SMALL = pltpu.CompilerParams(vmem_limit_bytes=12 * 1024 * 1024)
 MEDIUM = pltpu.CompilerParams(vmem_limit_bytes=50 * 1024 * 1024)
+WIDE = pltpu.CompilerParams(vmem_limit_bytes=52 * 1024 * 1024)
 LARGE = pltpu.CompilerParams(vmem_limit_bytes=60 * 1024 * 1024)
 f32 = jnp.float32
 bf16 = jnp.bfloat16
@@ -107,12 +108,12 @@
     scales_ref[...] = scales
 
 
-def dequantized(geno_ref, scales_ref, step):
+def dequantized(geno_ref, scales_ref, first):
     rows = geno_ref.shape[0]
     group = 128
     out = []
     for g in range(rows // group):
-        scale = scales_ref[pl.ds(step * (rows // group) + g, 1), :]
+        scale = scales_ref[pl.ds(first // group + g, 1), :]
         wide = geno_ref[g * group : (g + 1) * group, :].astype(f32) * scale
         out.append(wide.astype(bf16))
     return jnp.concatenate(out, 0)
@@ -145,7 +146,7 @@
         look_up(table_ref, index_ref, scales_ref)
         out_ref[...] = jnp.zeros_like(out_ref)
 
-    out_ref[...] += dot(resid_ref[...].astype(bf16), dequantized(geno_ref, scales_ref, step))
+    out_ref[...] += dot(resid_ref[...].astype(bf16), dequantized(geno_ref, scales_ref, step * ROWS))
 
 
 def screen(table, geno, index, resid, active_ids, admit_ids):
@@ -178,56 +179,68 @@
     )(table, geno, index, resid, active_ids, admit_ids)
 
 
-def select_kernel(first, table_ref, packed_ref, geno_ref, index_ref, out_ref, scales_ref, pick_ref):
-    step = pl.program_id(0)
-
-    @pl.when(step == 0)
-    def _():
-        look_up(table_ref, index_ref, scales_ref)
-        wanted = column_row(packed_ref[...])
-
-        @pl.loop(0, pick_ref.shape[0], step=ROWS)
-        def _(at):
-            here = iota((ROWS, pick_ref.shape[1]), 0) + (at + 1) == wanted
-            pick_ref[pl.ds(pl.multiple_of(at, ROWS), ROWS), :] = here.astype(f32).astype(bf16)
-
-    x = dequantized(geno_ref, scales_ref, first + step)
-    out_ref[...] = dot(x, pick_ref[...]).astype(bf16)
-
-
-def select(half, table, packed, geno, index, params):
+def select_kernel(
+    own, table_ref, packed_ref, index_ref, geno_hbm, out_ref, scales_ref, pick_ref, geno_ref, sems
+):
+    samples = out_ref.shape[0]
+    chunks, rows = geno_ref.shape[:2]
+    core = lax.axis_index("core")
+    first = (core if own else 1 - core) * samples
+    copies = []
+    for n in range(chunks):
+        at = pl.multiple_of(first + n * rows, rows)
+        copies.append(
+            pltpu.make_async_copy(geno_hbm.at[pl.ds(at, rows)], geno_ref.at[n], sems.at[n])
+        )
+        copies[n].start()
+    look_up(table_ref, index_ref, scales_ref)
+    wanted = column_row(packed_ref[...])
+
+    @pl.loop(0, pick_ref.shape[0], step=ROWS)
+    def _(at):
+        here = iota((ROWS, pick_ref.shape[1]), 0) + (at + 1) == wanted
+        pick_ref[pl.ds(pl.multiple_of(at, ROWS), ROWS), :] = here.astype(f32).astype(bf16)
+
+    for n in range(chunks):
+        copies[n].wait()
+        x = dequantized(geno_ref.at[n], scales_ref, first + n * rows)
+        out_ref[n * rows : (n + 1) * rows, :] = dot(x, pick_ref[...]).astype(bf16)
+
+
+def select(own, table, packed, geno, index, params):
     samples, width = geno.shape[0] // 2, geno.shape[1]
     held = packed.shape[0] * CAP
-    rows = 2 * ROWS
-    first = half * (samples // rows)
-    return pl.pallas_call(
-        functools.partial(select_kernel, first),
-        grid=(samples // rows,),
+    chunks = 2
+    vmem = pl.BlockSpec(memory_space=pltpu.VMEM)
+    return pl.pallas_call(
+        functools.partial(select_kernel, own),
         in_specs=[
             pl.BlockSpec(memory_space=pltpu.SMEM),
-            pl.BlockSpec(packed.shape, lambda i: (0, 0)),
-            pl.BlockSpec((rows, width), lambda i: (i + first, 0)),
-            pl.BlockSpec(index.shape, lambda i: (0, 0)),
+            vmem,
+            vmem,
+            pl.BlockSpec(memory_space=pltpu.HBM),
         ],
-        out_specs=pl.BlockSpec((rows, held), lambda i: (i, 0)),
+        out_specs=vmem,
         out_shape=jax.ShapeDtypeStruct((samples, held), bf16),
-        scratch_shapes=[pltpu.VMEM(index.shape, f32), pltpu.VMEM((width, held), bf16)],
+        scratch_shapes=[
+            pltpu.VMEM(index.shape, f32),
+            pltpu.VMEM((width, held), bf16),
+            pltpu.VMEM((chunks, samples // chunks, width), bf16),
+            pltpu.SemaphoreType.DMA((chunks,)),
+        ],
         compiler_params=params,
         cost_estimate=pl.CostEstimate(
             flops=2 * samples * width * held, bytes_accessed=2 * samples * width, transcendentals=0
         ),
         name="select",
-    )(table, packed, geno, index)
+    )(table, packed, index, geno)
 
 
 def pick_kernel(
-    inv_root, own_ref, one_ref, two_ref, three_ref, packed_hbm, scores_ref, pay_ref, packed_ref, sem
-):
-    copy = pltpu.make_async_copy(packed_hbm, packed_ref, sem)
-    copy.start()
+    inv_root, own_ref, one_ref, two_ref, three_ref, packed_ref, scores_ref, pay_ref
+):
     scores = ((own_ref[...] + two_ref[...]) + (one_ref[...] + three_ref[...])) * inv_root
     scores_ref[...] = scores
-    copy.wait()
     wanted = column_row(packed_ref[...])
     stacked = jnp.concatenate(thirds(scores), 0)
     phenos, width = scores.shape
@@ -243,9 +256,6 @@
 def pick(parts, packed, inv_root):
     return pl.pallas_call(
         functools.partial(pick_kernel, inv_root),
-        in_specs=[pl.BlockSpec(memory_space=pltpu.VMEM)] * 4
-        + [pl.BlockSpec(memory_space=pltpu.HBM)],
-        scratch_shapes=[pltpu.VMEM(packed.shape, packed.dtype), pltpu.SemaphoreType.DMA],
         out_shape=(
             jax.ShapeDtypeStruct(parts[0].shape, f32),
             jax.ShapeDtypeStruct((packed.shape[0] * HALF, LANES), f32),
@@ -402,27 +412,25 @@
     )(data, serial, holder, inverse, *state, resid, update)
 
 
-def update_kernel(core_ref, pay_ref, first_ref, second_ref, keep_ref, send_ref):
+def update_kernel(pay_ref, columns_ref, out_ref):
     packed = jnp.concatenate(
         [swapped(pay_ref[at : at + 8, :]) for at in range(0, pay_ref.shape[0], 8)], 1
     ).astype(bf16)
-    first = core_ref[:, :1] == 0
-    half = keep_ref.shape[1]
-    for at in range(0, half, ROWS):
-        a = dot_t(packed, first_ref[at : at + ROWS, :])
-        b = dot_t(packed, second_ref[at : at + ROWS, :])
-        keep_ref[:, at : at + ROWS] = jnp.where(first, a, b)
-        send_ref[:, at : at + ROWS] = jnp.where(first, b, a)
-
-
-def partial_update(core, pay, first, second):
-    half = jax.ShapeDtypeStruct((2 * HALF, first.shape[0]), f32)
+    for at in range(0, out_ref.shape[1], ROWS):
+        out_ref[:, at : at + ROWS] = dot_t(packed, columns_ref[at : at + ROWS, :])
+
+
+def partial_update(pay, columns):
+    samples, held = columns.shape
     return pl.pallas_call(
         update_kernel,
-        out_shape=(half, half),
-        compiler_params=SMALL,
+        out_shape=jax.ShapeDtypeStruct((2 * HALF, samples), f32),
+        compiler_params=SMALL,
+        cost_estimate=pl.CostEstimate(
+            flops=512 * samples * held, bytes_accessed=2 * samples * held, transcendentals=0
+        ),
         name="update",
-    )(core, pay, first, second)
+    )(pay, columns)
 
 
 def spread_kernel(keep_ref, arrived_ref, out_ref):
@@ -464,6 +472,28 @@
     cross = jnp.sum(resid * update, 1, keepdims=True)
     square = jnp.sum(update * update, 1, keepdims=True)
     return jnp.where(iota((update.shape[0], LANES), 1) < CAP, cross, square)
+
+
+def two_parts(update):
+    high = update.astype(bf16)
+    return jnp.concatenate([high, (update - high.astype(f32)).astype(bf16)], 0)
+
+
+def gradient_kernel(inv_root, mine_ref, columns_ref, out_ref):
+    out_ref[...] = dot(two_parts(mine_ref[...] * inv_root), columns_ref[...])
+
+
+def own_gradient(mine, columns, inv_root):
+    samples, held = columns.shape
+    return pl.pallas_call(
+        functools.partial(gradient_kernel, inv_root),
+        out_shape=jax.ShapeDtypeStruct((2 * mine.shape[0], held), f32),
+        compiler_params=SMALL,
+        cost_estimate=pl.CostEstimate(
+            flops=512 * samples * held, bytes_accessed=2 * samples * held, transcendentals=0
+        ),
+        name="gradient",
+    )(mine, columns)
 
 
 def descent_kernel(
@@ -473,19 +503,15 @@
     mine_ref,
     other_ref,
     resid_ref,
-    first_ref,
-    second_ref,
+    own_ref,
+    columns_ref,
     out_ref,
     update_ref,
 ):
     update = whole_update(inv_root, core_ref, mine_ref, other_ref)
     update_ref[...] = update
     phenos = update.shape[0]
-    high = update.astype(bf16)
-    low = (update - high.astype(f32)).astype(bf16)
-    pair = jnp.concatenate([high, low], 0)
-    half = first_ref.shape[0]
-    grad = dot(pair[:, :half], first_ref[...]) + dot(pair[:, half:], second_ref[...])
+    grad = own_ref[...] + dot(two_parts(other_ref[...] * inv_root), columns_ref[...])
     grad = (grad[:phenos] + grad[phenos:]) * inv_root
     both = step_sums(resid_ref[...], update)
     mine = iota(both.shape, 0) == lax.rem(rank_ref[...], phenos)
@@ -503,35 +529,35 @@
             out_ref[at + chunk + HALF : at + 2 * chunk, :] = row
 
 
-def descent(rank, core, mine, other, resid, first, second, inv_root, copies):
-    out = (copies * (first.shape[1] // CAP) * (HALF + 1), LANES)
+def descent(rank, core, mine, other, resid, own, columns, inv_root, copies):
+    out = (copies * (columns.shape[1] // CAP) * (HALF + 1), LANES)
     return pl.pallas_call(
         functools.partial(descent_kernel, inv_root),
         out_shape=(jax.ShapeDtypeStruct(out, f32), jax.ShapeDtypeStruct(resid.shape, f32)),
         compiler_params=SMALL,
         name="descent",
-    )(rank, core, mine, other, resid, first, second)
-
-
-def settle_kernel(inv_root, core_ref, mine_ref, other_ref, resid_ref, sums_ref, update_ref):
-    update = whole_update(inv_root, core_ref, mine_ref, other_ref)
-    update_ref[...] = update
-    sums_ref[...] = jnp.broadcast_to(step_sums(resid_ref[...], update)[None], sums_ref.shape)
-
-
-def settle(core, mine, other, resid, inv_root, copies):
+    )(rank, core, mine, other, resid, own, columns)
+
+
+def settle_kernel(inv_root, core_ref, mine_ref, resid_ref, sums_ref):
+    half = mine_ref.shape[1]
+    resid = jnp.where(core_ref[:, :1] == 0, resid_ref[:, :half], resid_ref[:, half:])
+    sums = step_sums(resid, mine_ref[...] * inv_root)
+    sums_ref[...] = jnp.broadcast_to(sums[None], sums_ref.shape)
+
+
+def settle(core, mine, resid, inv_root, copies):
     return pl.pallas_call(
         functools.partial(settle_kernel, inv_root),
-        out_shape=(
-            jax.ShapeDtypeStruct((copies, resid.shape[0], LANES), f32),
-            jax.ShapeDtypeStruct(resid.shape, f32),
-        ),
+        out_shape=jax.ShapeDtypeStruct((copies, resid.shape[0], LANES), f32),
         compiler_params=SMALL,
         name="settle",
-    )(core, mine, other, resid)
-
-
-def last_kernel(sums_ref, b_ref, d_ref, resid_ref, update_ref, coeffs_ref, out_ref):
+    )(core, mine, resid)
+
+
+def last_kernel(
+    inv_root, sums_ref, core_ref, mine_ref, other_ref, b_ref, d_ref, resid_ref, coeffs_ref, out_ref
+):
     phenos, fit = coeffs_ref.shape
     total = sums_ref[0]
     for j in range(1, sums_ref.shape[0]):
@@ -541,20 +567,21 @@
         rows = slice(half * HALF, (half + 1) * HALF)
         cols = slice(half * fit, (half + 1) * fit)
         coeffs_ref[rows, :] = b_ref[:, cols] + factor[rows] * d_ref[:, cols]
-    out_ref[...] = resid_ref[...] - factor * update_ref[...]
-
-
-def last(sums, coeffs, direction, resid, update):
+    update = whole_update(inv_root, core_ref, mine_ref, other_ref)
+    out_ref[...] = resid_ref[...] - factor * update
+
+
+def last(sums, core, mine, other, coeffs, direction, resid, inv_root):
     phenos = resid.shape[0]
     return pl.pallas_call(
-        last_kernel,
+        functools.partial(last_kernel, inv_root),
         out_shape=(
             jax.ShapeDtypeStruct((phenos, coeffs.shape[1] // 2), f32),
             jax.ShapeDtypeStruct(resid.shape, f32),
         ),
         compiler_params=SMALL,
         name="last",
-    )(sums, coeffs, direction, resid, update)
+    )(sums, core, mine, other, coeffs, direction, resid)
 
 
 def exchange(pay, axes):
@@ -588,23 +615,25 @@
         packed.reshape(holders, 1, LANES), VAR, split_axis=0, concat_axis=0, tiled=True
     ).reshape(holders, LANES)
 
-    first = select(0, scale_table, packed, geno, scale_index, MEDIUM)
-    parts, first = lax.optimization_barrier((parts, first))
+    away = select(False, scale_table, packed, geno, scale_index, MEDIUM)
+    parts, away = lax.optimization_barrier((parts, away))
     scores, pay = pick(parts, packed, inv_root)
     pay, packed = lax.optimization_barrier((pay, packed))
-    second = select(1, scale_table, packed, geno, scale_index, LARGE)
-    pay, *state, second = owner_first(
-        exchange(pay, VAR), serial, holder, block_inverse, beta_active, second
+    home = select(True, scale_table, packed, geno, scale_index, WIDE)
+    pay, *state, home = owner_first(
+        exchange(pay, VAR), serial, holder, block_inverse, beta_active, home
     )
     current = residual
     for pass_index in range(PASSES):
-        keep, send = partial_update(core, exchange(pay, VAR), first, second)
-        mine = spread(keep, shifted(send, "core"), lax.axis_size(CHIPS))
+        pay = exchange(pay, VAR)
+        arrived = shifted(partial_update(pay, away), "core")
+        mine = spread(partial_update(pay, home), arrived, lax.axis_size(CHIPS))
         mine = total(lax.all_to_all(mine, CHIPS, split_axis=0, concat_axis=0, tiled=True))
         other = shifted(mine, "core")
         if pass_index + 1 == PASSES:
             break
-        data, update = descent(rank, core, mine, other, current, first, second, inv_root, copies)
+        own = own_gradient(mine, home, inv_root)
+        data, update = descent(rank, core, mine, other, current, own, away, inv_root, copies)
         pay, coeffs, direction, current, *gradient = owner_next(
             exchange(data, SAMP + VAR),
             serial,
@@ -617,9 +646,9 @@
         )
         state = (coeffs, direction, *gradient)
 
-    sums, update = settle(core, mine, other, current, inv_root, copies)
-    sums = lax.all_to_all(sums, SAMP, split_axis=0, concat_axis=0, tiled=True)
-    return (scores, *last(sums, coeffs, direction, current, update))
+    sums = settle(core, mine, current, inv_root, 2 * copies)
+    sums = lax.all_to_all(sums, ("core",) + SAMP, split_axis=0, concat_axis=0, tiled=True)
+    return (scores, *last(sums, core, mine, other, coeffs, direction, current, inv_root))
 
 
 def solution(mesh):

time: 168 us -> 166 us (0.988)
  blocking collectives: 104 us -> 92.6 us
  starting transfers between devices: 19.3 us -> 23.4 us
  waiting for transfers between devices: 7.48 us -> 10.8 us
    all_to_all x1 -> x0, blocking collectives: 11.2 us -> none  [on_device(): sums = lax.all_to_all(sums, SAMP, split_axis=0, concat_axis=0, tiled=True)]
    all_to_all x0 -> x1, waiting for transfers between devices: none -> 6.38 us  [on_device(): lax.all_to_all(sums, ('core',) + SAMP, split_axis=0, concat_axis=0, tiled...]
    all_to_all x0 -> x1, starting transfers between devices: none -> 3.72 us  [on_device(): lax.all_to_all(sums, ('core',) + SAMP, split_axis=0, concat_axis=0, tiled...]
    ppermute x10, waiting for transfers between devices: 6.87 us -> 3.86 us  [shifted(): return lax.ppermute(x, axis, [(i, (i + by) % size) for i in range(size)])]
    pallas_call x8 -> x13, Pallas kernels: 21.5 us -> 22.7 us  [the longest x2 15 us: select(): pl.pallas_call(functools.partial(select_kernel, own), in_specs=[pl.BlockS...]
  transfers between devices with their start and end apart: 12 -> 13, of which waited for: 7 -> 8; matrix products, arithmetic and copies ran while one was open for 1% -> 1% of each run, Pallas kernels for 9% -> 11%
where the time goes in v6:
time: 166 us; the launch traced here: 164 us
  blocking collectives  92.6 us (56%)
  Pallas kernels  35.5 us (21%)
  starting transfers between devices  23.4 us (14%)
  waiting for transfers between devices  10.8 us (7%)
    all_to_all x5, blocking collectives, exchange(): lax.all_to_all(pay.reshape(shape), axes, split_axis=0, concat_axis=0, til...  62.2 us
    all_to_all x3, blocking collectives, on_device(): lax.all_to_all(mine, CHIPS, split_axis=0, concat_axis=0, tiled=True)  30.4 us
    pallas_call x2, Pallas kernels, select(): pl.pallas_call(functools.partial(select_kernel, own), in_specs=[pl.BlockS...  15 us
    ppermute x10, starting transfers between devices, shifted(): return lax.ppermute(x, axis, [(i, (i + by) % size) for i in range(size)])  9.03 us
    pallas_call x1, Pallas kernels, screen(): pl.pallas_call(screen_kernel, grid=(samples // ROWS,), in_specs=[pl.Block...  8.09 us
    all_to_all x1, waiting for transfers between devices, on_device(): lax.all_to_all(sums, ('core',) + SAMP, split_axis=0, concat_axis=0, tiled...  6.38 us
    all_to_all x1, starting transfers between devices, on_device(): lax.all_to_all(packed.reshape(holders, 1, LANES), VAR, split_axis=0, conc...  5.53 us
    all_to_all x1, starting transfers between devices, exchange(): lax.all_to_all(pay.reshape(shape), axes, split_axis=0, concat_axis=0, til...  5.12 us
  transfers between devices with their start and end apart: 13, of which 8 were waited for; matrix products, arithmetic and copies ran while one was open for 1% of the time, Pallas kernels for 11%

profile of v6, /device:TPU:0, one launch (start us, length us, event | category | flops | bytes accessed | tf_op | source)
XLA Modules:
  0.0 164.1 jit_solution(13202166677770929222)
XLA Ops:
  0.7 8.1 %screen.1 = (f32[8,2048]{1,0:T(8,128)}, s32[1,512]{1,0:T(1,128)}, s32[1,512]{1,0:T(1,128)}, s32[16,128]{1,0:T(8,128)}, s32[8,128]{1,0:T(8,128)}, /*index=5*/s32[8,128]{1,0:T(8,128)}) custom-call(f32[16]{0:T(128)} %table_ref.5, bf16[2048,2048]{1,0:T(8,128)(2,1)} %geno_hbm.3, s32[16,2048]{1,0:T(8,128)} %index_ref.5, f32[8,2048]{1,0:T(8,128)} %resid_in.1, ...), custom_call_target="tpu_custom_call" | custom-call | flops 67108864 | bytes 8388608 | tf_op jit(solution)/shard_map/screen/pallas_call | solution.py:160
  8.7 3.4 %collective-permute-start = (f32[8,2048]{1,0:T(8,128)}, f32[8,2048]{1,0:T(8,128)S(1)}, u32[]{:S(2)}, u32[]{:S(2)}) collective-permute-start(f32[8,2048]{1,0:T(8,128)} %get-tuple-element.38), channel_id=1, source_target_pairs={{0,4},{4,0},{1,5},{5,1},{2,6},{6,2},{3,7},{7,3},{8,12},{12,8},{9,1... | collective-permute-start | bytes 196616 | tf_op jit(solution)/shard_map/ppermute | solution.py:598
  12.1 5.5 %all-to-all-start = ((s32[16,1,128]{2,1,0:T(1,128)}), s32[16,1,128]{2,1,0:T(1,128)S(1)}, u32[]{:S(2)}, u32[]{:S(2)}) async-start(s32[16,1,128]{2,1,0:T(1,128)} %bitcast.35), calls=%async_computation | async-start | bytes 16384 | tf_op jit(solution)/shard_map/all_to_all | solution.py:614
  17.7 0.9 add.3.own_ref
  18.5 2.8 %collective-permute-start.3 = (f32[8,2048]{1,0:T(8,128)S(1)}, f32[8,2048]{1,0:T(8,128)S(1)}, u32[]{:S(2)}, u32[]{:S(2)}) collective-permute-start(f32[8,2048]{1,0:T(8,128)S(1)} %add.3.own_ref), channel_id=1, source_target_pairs={{0,3},{1,0},{2,1},{3,2},{4,7},{5,4},{6,5},{7,6},{8,11},{9,8},{10,9... | collective-permute-start | bytes 196616 | tf_op jit(solution)/shard_map/ppermute | solution.py:598
  22.1 0.9 collective-permute-start.1
  23.6 6.8 %select.2.columns_ref = bf16[1024,1024]{1,0:T(8,128)(2,1)S(1)} custom-call(f32[16]{0:T(128)S(1)} %copy-done.8, s32[16,128]{1,0:T(8,128)S(1)} %bitcast.29, s32[16,2048]{1,0:T(8,128)S(1)} %copy-done.2, bf16[2048,2048]{1,0:T(8,128)(2,1)} %geno_hbm.3), custom_call_target="tpu_custom_call" | custom-call | flops 4294967296 | bytes 4194304 | tf_op jit(solution)/shard_map/select/pallas_call | solution.py:215
  30.5 1.5 pick.1
  32.0 5.1 %all-to-all-start.1 = ((f32[16,4,128]{2,1,0:T(4,128)}), f32[16,4,128]{2,1,0:T(4,128)S(1)}, u32[]{:S(2)}, u32[]{:S(2)}) async-start(f32[16,4,128]{2,1,0:T(4,128)} %bitcast.5), calls=%async_computation.1 | async-start | bytes 65536 | tf_op jit(solution)/shard_map/all_to_all | solution.py:591
  37.2 8.2 %select.3.columns_hbm = bf16[1024,1024]{1,0:T(8,128)(2,1)} custom-call(f32[16]{0:T(128)S(1)} %copy-done.8, s32[16,128]{1,0:T(8,128)S(1)} %bitcast.31, s32[16,2048]{1,0:T(8,128)S(1)} %copy-done.2, bf16[2048,2048]{1,0:T(8,128)(2,1)} %geno_hbm.3), custom_call_target="tpu_custom_call" | custom-call | flops 4294967296 | bytes 4194304 | tf_op jit(solution)/shard_map/select/pallas_call | solution.py:215
  45.4 1.6 owner_first.1
  47.0 11.6 %all_to_all.55 = f32[16,4,128]{2,1,0:T(4,128)S(1)} all-to-all(f32[16,4,128]{2,1,0:T(4,128)S(1)} %bitcast.34), channel_id=1, replica_groups=mesh['y_lo'=2,'z'=4,'core'=2,'y_hi'=2,'x'=4] {'y_lo','z','core'}, dimensions={0} | all-to-all | bytes 65536 | tf_op jit(solution)/shard_map/all_to_all | solution.py:591
  60.5 10.1 %all_to_all.56.parts_ref = f32[8,8,1024]{2,1,0:T(8,128)S(1)} all-to-all(f32[8,8,1024]{2,1,0:T(8,128)S(1)} %spread.3), channel_id=1, replica_groups=mesh['y_lo'=2,'z'=4,'core'=2,'y_hi'=2,'x'=4] {'y_lo','z'}, dimensions={0} | all-to-all | bytes 524288 | tf_op jit(solution)/shard_map/all_to_all | solution.py:631
  72.6 17.3 %all_to_all.57 = f32[128,1,640]{2,1,0:T(1,128)S(1)} all-to-all(f32[128,1,640]{2,1,0:T(1,128)S(1)} %bitcast.21), channel_id=1, replica_groups=mesh['y_lo'=2,'z'=4,'core'=2,'y_hi'=2,'x'=4] {'y_hi','x','y_lo','z','core'}, dimensions={0} | all-to-all | bytes 655360 | tf_op jit(solution)/shard_map/all_to_all | solution.py:591
  89.9 1.0 owner_next.2
  90.9 8.7 %all_to_all.58 = f32[16,4,128]{2,1,0:T(4,128)S(1)} all-to-all(f32[16,4,128]{2,1,0:T(4,128)S(1)} %bitcast.33), channel_id=1, replica_groups=mesh['y_lo'=2,'z'=4,'core'=2,'y_hi'=2,'x'=4] {'y_lo','z','core'}, dimensions={0} | all-to-all | bytes 65536 | tf_op jit(solution)/shard_map/all_to_all | solution.py:591
  101.5 10.1 %all_to_all.59.parts_ref = f32[8,8,1024]{2,1,0:T(8,128)S(1)} all-to-all(f32[8,8,1024]{2,1,0:T(8,128)S(1)} %spread.4), channel_id=1, replica_groups=mesh['y_lo'=2,'z'=4,'core'=2,'y_hi'=2,'x'=4] {'y_lo','z'}, dimensions={0} | all-to-all | bytes 524288 | tf_op jit(solution)/shard_map/all_to_all | solution.py:631
  113.4 16.0 %all_to_all.60 = f32[128,1,640]{2,1,0:T(1,128)S(1)} all-to-all(f32[128,1,640]{2,1,0:T(1,128)S(1)} %bitcast.20), channel_id=1, replica_groups=mesh['y_lo'=2,'z'=4,'core'=2,'y_hi'=2,'x'=4] {'y_hi','x','y_lo','z','core'}, dimensions={0} | all-to-all | bytes 655360 | tf_op jit(solution)/shard_map/all_to_all | solution.py:591
  129.4 1.0 owner_next.3
  130.4 8.7 %all_to_all.61 = f32[16,4,128]{2,1,0:T(4,128)S(1)} all-to-all(f32[16,4,128]{2,1,0:T(4,128)S(1)} %bitcast.32), channel_id=1, replica_groups=mesh['y_lo'=2,'z'=4,'core'=2,'y_hi'=2,'x'=4] {'y_lo','z','core'}, dimensions={0} | all-to-all | bytes 65536 | tf_op jit(solution)/shard_map/all_to_all | solution.py:591
  141.0 10.1 %all_to_all.62.parts_ref = f32[8,8,1024]{2,1,0:T(8,128)S(1)} all-to-all(f32[8,8,1024]{2,1,0:T(8,128)S(1)} %spread.5), channel_id=1, replica_groups=mesh['y_lo'=2,'z'=4,'core'=2,'y_hi'=2,'x'=4] {'y_lo','z'}, dimensions={0} | all-to-all | bytes 524288 | tf_op jit(solution)/shard_map/all_to_all | solution.py:631
  151.9 3.7 %all-to-all-start.10 = ((f32[16,8,128]{2,1,0:T(8,128)}), f32[16,8,128]{2,1,0:T(8,128)S(1)}, u32[]{:S(2)}, u32[]{:S(2)}) async-start(f32[16,8,128]{2,1,0:T(8,128)} %settle.1), calls=%async_computation.10 | async-start | bytes 131072 | tf_op jit(solution)/shard_map/all_to_all | solution.py:650
  156.1 0.9 collective-permute-done.9.other_ref
  156.9 6.4 %all-to-all-done.10.sums_ref = f32[16,8,128]{2,1,0:T(8,128)S(1)} async-done(((f32[16,8,128]{2,1,0:T(8,128)}), f32[16,8,128]{2,1,0:T(8,128)S(1)}, u32[]{:S(2)}, u32[]{:S(2)}) %all-to-all-start.10) | async-done | bytes 65568 | tf_op jit(solution)/shard_map/all_to_all | solution.py:650
  (54 shorter events, 12.9 us)
Async XLA Ops:
  0.6 23.0 %copy-start.2 = (s32[16,2048]{1,0:T(8,128)S(1)}, s32[16,2048]{1,0:T(8,128)}, u32[]{:S(2)}) copy-start(s32[16,2048]{1,0:T(8,128)} %index_ref.5) | copy-start | bytes 393220
  0.6 23.0 %copy-start.8 = (f32[16]{0:T(128)S(1)}, f32[16]{0:T(128)}, u32[]{:S(2)}) copy-start(f32[16]{0:T(128)} %table_ref.5) | copy-start | bytes 196
  8.7 8.9 %collective-permute-start = (f32[8,2048]{1,0:T(8,128)}, f32[8,2048]{1,0:T(8,128)S(1)}, u32[]{:S(2)}, u32[]{:S(2)}) collective-permute-start(f32[8,2048]{1,0:T(8,128)} %get-tuple-element.38), channel_id=1, source_target_pairs={{0,4},{4,0},{1,5},{5,1},{2,6},{6,2},{3,7},{7,3},{8,12},{12,8},{9,1... | collective-permute-start | bytes 196616 | tf_op jit(solution)/shard_map/ppermute | solution.py:598
  12.1 11.5 %all-to-all-start = ((s32[16,1,128]{2,1,0:T(1,128)}), s32[16,1,128]{2,1,0:T(1,128)S(1)}, u32[]{:S(2)}, u32[]{:S(2)}) async-start(s32[16,1,128]{2,1,0:T(1,128)} %bitcast.35), calls=%async_computation | async-start | bytes 16384 | tf_op jit(solution)/shard_map/all_to_all | solution.py:614
  18.5 11.9 %collective-permute-start.3 = (f32[8,2048]{1,0:T(8,128)S(1)}, f32[8,2048]{1,0:T(8,128)S(1)}, u32[]{:S(2)}, u32[]{:S(2)}) collective-permute-start(f32[8,2048]{1,0:T(8,128)S(1)} %add.3.own_ref), channel_id=1, source_target_pairs={{0,3},{1,0},{2,1},{3,2},{4,7},{5,4},{6,5},{7,6},{8,11},{9,8},{10,9... | collective-permute-start | bytes 196616 | tf_op jit(solution)/shard_map/ppermute | solution.py:598
  21.3 9.1 %collective-permute-start.2 = (f32[8,2048]{1,0:T(8,128)S(1)}, f32[8,2048]{1,0:T(8,128)S(1)}, u32[]{:S(2)}, u32[]{:S(2)}) collective-permute-start(f32[8,2048]{1,0:T(8,128)S(1)} %add.3.own_ref), channel_id=1, source_target_pairs={{0,2},{1,3},{2,0},{3,1},{4,6},{5,7},{6,4},{7,5},{8,10},{9,11},{10,... | collective-permute-start | bytes 196616 | tf_op jit(solution)/shard_map/ppermute | solution.py:598
  22.1 8.4 %collective-permute-start.1 = (f32[8,2048]{1,0:T(8,128)S(1)}, f32[8,2048]{1,0:T(8,128)S(1)}, u32[]{:S(2)}, u32[]{:S(2)}) collective-permute-start(f32[8,2048]{1,0:T(8,128)S(1)} %add.3.own_ref), channel_id=1, source_target_pairs={{0,1},{1,2},{2,3},{3,0},{4,5},{5,6},{6,7},{7,4},{8,9},{9,10},{10,1... | collective-permute-start | bytes 196616 | tf_op jit(solution)/shard_map/ppermute | solution.py:598
  32.0 13.4 %all-to-all-start.1 = ((f32[16,4,128]{2,1,0:T(4,128)}), f32[16,4,128]{2,1,0:T(4,128)S(1)}, u32[]{:S(2)}, u32[]{:S(2)}) async-start(f32[16,4,128]{2,1,0:T(4,128)} %bitcast.5), calls=%async_computation.1 | async-start | bytes 65536 | tf_op jit(solution)/shard_map/all_to_all | solution.py:591
  37.1 8.2 %copy-start = (f32[2,256,256]{2,1,0:T(8,128)S(1)}, f32[2,256,256]{2,1,0:T(8,128)}, u32[]{:S(2)}) copy-start(f32[2,256,256]{2,1,0:T(8,128)} %inverse_ref.5) | copy-start | bytes 1572868
  37.1 8.2 %copy-start.4 = (s32[1,512]{1,0:T(1,128)S(1)}, s32[1,512]{1,0:T(1,128)}, u32[]{:S(2)}) copy-start(s32[1,512]{1,0:T(1,128)} %get-tuple-element.50.holder_ref) | copy-start | bytes 6148
  37.2 8.2 %copy-start.5 = (s32[1,512]{1,0:T(1,128)S(1)}, s32[1,512]{1,0:T(1,128)}, u32[]{:S(2)}) copy-start(s32[1,512]{1,0:T(1,128)} %get-tuple-element.49.serial_ref) | copy-start | bytes 6148
  37.2 8.2 %copy-start.6 = (f32[8,448]{1,0:T(8,128)S(1)}, f32[8,448]{1,0:T(8,128)}, u32[]{:S(2)}) copy-start(f32[8,448]{1,0:T(8,128)} %beta_ref.1) | copy-start | bytes 43012
  59.3 1.2 collective-permute-start.4
  60.1 12.1 %copy-start.1 = (f32[8,2048]{1,0:T(8,128)S(1)}, f32[8,2048]{1,0:T(8,128)}, u32[]{:S(2)}) copy-start(f32[8,2048]{1,0:T(8,128)} %resid_in.1) | copy-start | bytes 196612
  60.1 12.1 %copy-start.3 = (s32[8,128]{1,0:T(8,128)S(1)}, s32[8,128]{1,0:T(8,128)}, u32[]{:S(2)}) copy-start(s32[8,128]{1,0:T(8,128)} %get-tuple-element.45.core_ref) | copy-start | bytes 12292
  60.1 12.1 %copy-start.7 = (s32[8,128]{1,0:T(8,128)S(1)}, s32[8,128]{1,0:T(8,128)}, u32[]{:S(2)}) copy-start(s32[8,128]{1,0:T(8,128)} %get-tuple-element.46.rank_ref) | copy-start | bytes 12292
  70.7 1.5 collective-permute-start.5
  100.2 1.2 collective-permute-start.6
  111.6 1.3 collective-permute-start.7
  139.7 1.2 collective-permute-start.8
  151.9 11.4 %all-to-all-start.10 = ((f32[16,8,128]{2,1,0:T(8,128)}), f32[16,8,128]{2,1,0:T(8,128)S(1)}, u32[]{:S(2)}, u32[]{:S(2)}) async-start(f32[16,8,128]{2,1,0:T(8,128)} %settle.1), calls=%async_computation.10 | async-start | bytes 131072 | tf_op jit(solution)/shard_map/all_to_all | solution.py:650
  155.6 1.3 collective-permute-start.9

commit v7 on v6

--- a/solution.py
+++ b/solution.py
@@ -121,32 +121,42 @@
 
 def screen_kernel(
     table_ref,
-    geno_ref,
-    index_ref,
-    resid_ref,
     active_ref,
     admit_ref,
+    index_hbm,
+    resid_hbm,
+    geno_hbm,
     out_ref,
     holder_ref,
     serial_ref,
     packed_ref,
     rank_ref,
     core_ref,
+    index_ref,
+    resid_ref,
+    geno_ref,
     scales_ref,
     ids_ref,
+    sems,
 ):
-    step = pl.program_id(0)
-
-    @pl.when(step == 0)
-    def _():
-        rank_ref[...] = jnp.full(rank_ref.shape, lax.axis_index(VAR), jnp.int32)
-        core_ref[...] = jnp.full(core_ref.shape, lax.axis_index("core"), jnp.int32)
-        width = geno_ref.shape[1]
-        lay_out(width, active_ref, admit_ref, holder_ref, serial_ref, packed_ref, ids_ref)
-        look_up(table_ref, index_ref, scales_ref)
-        out_ref[...] = jnp.zeros_like(out_ref)
-
-    out_ref[...] += dot(resid_ref[...].astype(bf16), dequantized(geno_ref, scales_ref, step * ROWS))
+    chunks, rows, width = geno_ref.shape
+    pieces = [(index_hbm, index_ref), (resid_hbm, resid_ref)]
+    pieces += [(geno_hbm.at[pl.ds(n * rows, rows)], geno_ref.at[n]) for n in range(chunks)]
+    copies = [pltpu.make_async_copy(*piece, sems.at[n]) for n, piece in enumerate(pieces)]
+    for copy in copies:
+        copy.start()
+    rank_ref[...] = jnp.full(rank_ref.shape, lax.axis_index(VAR), jnp.int32)
+    core_ref[...] = jnp.full(core_ref.shape, lax.axis_index("core"), jnp.int32)
+    lay_out(width, active_ref, admit_ref, holder_ref, serial_ref, packed_ref, ids_ref)
+    copies[0].wait()
+    look_up(table_ref, index_ref, scales_ref)
+    copies[1].wait()
+    scores = jnp.zeros(out_ref.shape, f32)
+    for n in range(chunks):
+        copies[2 + n].wait()
+        x = dequantized(geno_ref.at[n], scales_ref, n * rows)
+        scores += dot(resid_ref[:, n * rows : (n + 1) * rows].astype(bf16), x)
+    out_ref[...] = scores
 
 
 def screen(table, geno, index, resid, active_ids, admit_ids):
@@ -154,33 +164,45 @@
     phenos = resid.shape[0]
     active_ids, admit_ids = active_ids[None], admit_ids[None]
     fit = active_ids.size + admit_ids.size
-    outs = [(phenos, width, f32), (1, fit, jnp.int32), (1, fit, jnp.int32)]
-    outs += [(lax.axis_size(VAR), LANES, jnp.int32)] + [(2 * HALF, LANES, jnp.int32)] * 2
-    whole = lambda shape: pl.BlockSpec(shape, lambda i: (0, 0))
+    tile = (2 * HALF, LANES)
+    integers = [(1, fit), (1, fit), (lax.axis_size(VAR), LANES), tile, tile]
+    chunks = 8
+    vmem = pl.BlockSpec(memory_space=pltpu.VMEM)
+    hbm = pl.BlockSpec(memory_space=pltpu.HBM)
     return pl.pallas_call(
         screen_kernel,
-        grid=(samples // ROWS,),
-        in_specs=[
-            pl.BlockSpec(memory_space=pltpu.SMEM),
-            pl.BlockSpec((ROWS, width), lambda i: (i, 0)),
-            whole(index.shape),
-            pl.BlockSpec((phenos, ROWS), lambda i: (0, i)),
-            whole(active_ids.shape),
-            whole(admit_ids.shape),
+        in_specs=[pl.BlockSpec(memory_space=pltpu.SMEM), vmem, vmem, hbm, hbm, hbm],
+        out_shape=[jax.ShapeDtypeStruct((phenos, width), f32)]
+        + [jax.ShapeDtypeStruct(shape, jnp.int32) for shape in integers],
+        scratch_shapes=[
+            pltpu.VMEM(index.shape, jnp.int32),
+            pltpu.VMEM(resid.shape, f32),
+            pltpu.VMEM((chunks, samples // chunks, width), bf16),
+            pltpu.VMEM(index.shape, f32),
+            pltpu.VMEM((1, fit), jnp.int32),
+            pltpu.SemaphoreType.DMA((2 + chunks,)),
         ],
-        out_specs=[whole(out[:2]) for out in outs],
-        out_shape=[jax.ShapeDtypeStruct(out[:2], out[2]) for out in outs],
-        scratch_shapes=[pltpu.VMEM(index.shape, f32), pltpu.VMEM((1, fit), jnp.int32)],
         compiler_params=LARGE,
         cost_estimate=pl.CostEstimate(
             flops=2 * phenos * samples * width, bytes_accessed=2 * samples * width, transcendentals=0
         ),
         name="screen",
-    )(table, geno, index, resid, active_ids, admit_ids)
+    )(table, active_ids, admit_ids, index, resid, geno)
 
 
 def select_kernel(
-    own, table_ref, packed_ref, index_ref, geno_hbm, out_ref, scales_ref, pick_ref, geno_ref, sems
+    own,
+    table_ref,
+    packed_ref,
+    index_ref,
+    geno_hbm,
+    out_ref,
+    scales_ref,
+    pick_ref,
+    geno_ref,
+    sems,
+    piece_ref=None,
+    out_sems=None,
 ):
     samples = out_ref.shape[0]
     chunks, rows = geno_ref.shape[:2]
@@ -201,17 +223,31 @@
         here = iota((ROWS, pick_ref.shape[1]), 0) + (at + 1) == wanted
         pick_ref[pl.ds(pl.multiple_of(at, ROWS), ROWS), :] = here.astype(f32).astype(bf16)
 
+    outs = []
     for n in range(chunks):
         copies[n].wait()
         x = dequantized(geno_ref.at[n], scales_ref, first + n * rows)
-        out_ref[n * rows : (n + 1) * rows, :] = dot(x, pick_ref[...]).astype(bf16)
+        piece = dot(x, pick_ref[...]).astype(bf16)
+        there = pl.ds(n * rows, rows)
+        if piece_ref is None:
+            out_ref[there, :] = piece
+        else:
+            piece_ref[n] = piece
+            outs.append(
+                pltpu.make_async_copy(piece_ref.at[n], out_ref.at[there], out_sems.at[n])
+            )
+            outs[n].start()
+    for out in outs:
+        out.wait()
 
 
 def select(own, table, packed, geno, index, params):
     samples, width = geno.shape[0] // 2, geno.shape[1]
     held = packed.shape[0] * CAP
-    chunks = 2
+    chunks = 4 if own else 2
+    rows = samples // chunks
     vmem = pl.BlockSpec(memory_space=pltpu.VMEM)
+    pieces = [pltpu.VMEM((chunks, rows, held), bf16), pltpu.SemaphoreType.DMA((chunks,))]
     return pl.pallas_call(
         functools.partial(select_kernel, own),
         in_specs=[
@@ -220,13 +256,14 @@
             vmem,
             pl.BlockSpec(memory_space=pltpu.HBM),
         ],
-        out_specs=vmem,
+        out_specs=pl.BlockSpec(memory_space=pltpu.HBM) if own else vmem,
         out_shape=jax.ShapeDtypeStruct((samples, held), bf16),
         scratch_shapes=[
             pltpu.VMEM(index.shape, f32),
             pltpu.VMEM((width, held), bf16),
-            pltpu.VMEM((chunks, samples // chunks, width), bf16),
+            pltpu.VMEM((chunks, rows, width), bf16),
             pltpu.SemaphoreType.DMA((chunks,)),
+            *(pieces if own else ()),
         ],
         compiler_params=params,
         cost_estimate=pl.CostEstimate(
@@ -647,6 +684,7 @@
         state = (coeffs, direction, *gradient)
 
     sums = settle(core, mine, current, inv_root, 2 * copies)
+    sums, other = lax.optimization_barrier((sums, other))
     sums = lax.all_to_all(sums, ("core",) + SAMP, split_axis=0, concat_axis=0, tiled=True)
     return (scores, *last(sums, core, mine, other, coeffs, direction, current, inv_root))
 

time: 166 us -> 163 us (0.982)
  blocking collectives: 92.6 us -> 104 us
  waiting for transfers between devices: 10.8 us -> 4.64 us
  starting transfers between devices: 23.4 us -> 19.2 us
  Pallas kernels: 35.5 us -> 31.6 us
    all_to_all x0 -> x1, blocking collectives: none -> 11.2 us  [on_device(): lax.all_to_all(sums, ('core',) + SAMP, split_axis=0, concat_axis=0, tiled...]
    all_to_all x1 -> x0, waiting for transfers between devices: 6.38 us -> none  [on_device(): lax.all_to_all(sums, ('core',) + SAMP, split_axis=0, concat_axis=0, tiled...]
    all_to_all x1 -> x0, starting transfers between devices: 3.72 us -> none  [on_device(): lax.all_to_all(sums, ('core',) + SAMP, split_axis=0, concat_axis=0, tiled...]
    pallas_call x1, Pallas kernels: 8.09 us -> 5.34 us  [screen(): pl.pallas_call(screen_kernel, in_specs=[pl.BlockSpec(memory_space=pltpu.S...]
  transfers between devices with their start and end apart: 13 -> 12, of which waited for: 8 -> 7; matrix products, arithmetic and copies ran while one was open for 1% -> 1% of each run, Pallas kernels for 11% -> 11%
where the time goes in v7:
time: 163 us; the launch traced here: 161 us
  blocking collectives  104 us (64%)
  Pallas kernels  31.6 us (19%)
  starting transfers between devices  19.2 us (12%)
  waiting for transfers between devices  4.64 us (3%)
    all_to_all x5, blocking collectives, exchange(): lax.all_to_all(pay.reshape(shape), axes, split_axis=0, concat_axis=0, til...  62.2 us
    all_to_all x3, blocking collectives, on_device(): lax.all_to_all(mine, CHIPS, split_axis=0, concat_axis=0, tiled=True)  30.4 us
    pallas_call x2, Pallas kernels, select(): pl.pallas_call(functools.partial(select_kernel, own), in_specs=[pl.BlockS...  14.5 us
    all_to_all x1, blocking collectives, on_device(): lax.all_to_all(sums, ('core',) + SAMP, split_axis=0, concat_axis=0, tiled...  11.2 us
    ppermute x10, starting transfers between devices, shifted(): return lax.ppermute(x, axis, [(i, (i + by) % size) for i in range(size)])  8.53 us
    all_to_all x1, starting transfers between devices, on_device(): lax.all_to_all(packed.reshape(holders, 1, LANES), VAR, split_axis=0, conc...  5.53 us
    pallas_call x1, Pallas kernels, screen(): pl.pallas_call(screen_kernel, in_specs=[pl.BlockSpec(memory_space=pltpu.S...  5.34 us
    all_to_all x1, starting transfers between devices, exchange(): lax.all_to_all(pay.reshape(shape), axes, split_axis=0, concat_axis=0, til...  5.12 us
  transfers between devices with their start and end apart: 12, of which 7 were waited for; matrix products, arithmetic and copies ran while one was open for 1% of the time, Pallas kernels for 11%

profile of v7, /device:TPU:0, one launch (start us, length us, event | category | flops | bytes accessed | tf_op | source)
XLA Modules:
  0.0 160.9 jit_solution(7201606880890815187)
XLA Ops:
  0.7 5.3 %screen.1 = (f32[8,2048]{1,0:T(8,128)}, s32[1,512]{1,0:T(1,128)}, s32[1,512]{1,0:T(1,128)}, s32[16,128]{1,0:T(8,128)}, s32[8,128]{1,0:T(8,128)}, /*index=5*/s32[8,128]{1,0:T(8,128)}) custom-call(f32[16]{0:T(128)} %table_ref.5, s32[1,448]{1,0:T(1,128)} %bitcast.36, s32[1,64]{1,0:T(1,128)} %bitcast.37, s32[16,2048]{1,0:T(8,128)} %index_ref.3, ...), custom_call_target="tpu_custom_call" | custom-call | flops 67108864 | bytes 8388608 | tf_op jit(solution)/shard_map/screen/pallas_call | solution.py:172
  6.0 3.4 %collective-permute-start = (f32[8,2048]{1,0:T(8,128)}, f32[8,2048]{1,0:T(8,128)S(1)}, u32[]{:S(2)}, u32[]{:S(2)}) collective-permute-start(f32[8,2048]{1,0:T(8,128)} %get-tuple-element.40), channel_id=1, source_target_pairs={{0,4},{4,0},{1,5},{5,1},{2,6},{6,2},{3,7},{7,3},{8,12},{12,8},{9,1... | collective-permute-start | bytes 196616 | tf_op jit(solution)/shard_map/ppermute | solution.py:635
  9.4 5.5 %all-to-all-start = ((s32[16,1,128]{2,1,0:T(1,128)}), s32[16,1,128]{2,1,0:T(1,128)S(1)}, u32[]{:S(2)}, u32[]{:S(2)}) async-start(s32[16,1,128]{2,1,0:T(1,128)} %bitcast.35), calls=%async_computation | async-start | bytes 16384 | tf_op jit(solution)/shard_map/all_to_all | solution.py:651
  14.9 0.9 add.3.own_ref
  15.8 2.8 %collective-permute-start.3 = (f32[8,2048]{1,0:T(8,128)S(1)}, f32[8,2048]{1,0:T(8,128)S(1)}, u32[]{:S(2)}, u32[]{:S(2)}) collective-permute-start(f32[8,2048]{1,0:T(8,128)S(1)} %add.3.own_ref), channel_id=1, source_target_pairs={{0,3},{1,0},{2,1},{3,2},{4,7},{5,4},{6,5},{7,6},{8,11},{9,8},{10,9... | collective-permute-start | bytes 196616 | tf_op jit(solution)/shard_map/ppermute | solution.py:635
  19.4 0.9 collective-permute-start.1
  20.9 6.8 %select.2.columns_ref = bf16[1024,1024]{1,0:T(8,128)(2,1)S(1)} custom-call(f32[16]{0:T(128)S(1)} %copy-done.8, s32[16,128]{1,0:T(8,128)S(1)} %bitcast.29, s32[16,2048]{1,0:T(8,128)S(1)} %copy-done.2, bf16[2048,2048]{1,0:T(8,128)(2,1)} %geno_hbm.5), custom_call_target="tpu_custom_call" | custom-call | flops 4294967296 | bytes 4194304 | tf_op jit(solution)/shard_map/select/pallas_call | solution.py:251
  27.7 1.5 pick.1
  29.3 5.1 %all-to-all-start.1 = ((f32[16,4,128]{2,1,0:T(4,128)}), f32[16,4,128]{2,1,0:T(4,128)S(1)}, u32[]{:S(2)}, u32[]{:S(2)}) async-start(f32[16,4,128]{2,1,0:T(4,128)} %bitcast.5), calls=%async_computation.1 | async-start | bytes 65536 | tf_op jit(solution)/shard_map/all_to_all | solution.py:628
  34.4 7.6 %select.3.columns_hbm = bf16[1024,1024]{1,0:T(8,128)(2,1)} custom-call(f32[16]{0:T(128)S(1)} %copy-done.8, s32[16,128]{1,0:T(8,128)S(1)} %bitcast.31, s32[16,2048]{1,0:T(8,128)S(1)} %copy-done.2, bf16[2048,2048]{1,0:T(8,128)(2,1)} %geno_hbm.5), custom_call_target="tpu_custom_call" | custom-call | flops 4294967296 | bytes 4194304 | tf_op jit(solution)/shard_map/select/pallas_call | solution.py:251
  42.1 1.6 owner_first.1
  43.8 11.6 %all_to_all.55 = f32[16,4,128]{2,1,0:T(4,128)S(1)} all-to-all(f32[16,4,128]{2,1,0:T(4,128)S(1)} %bitcast.34), channel_id=1, replica_groups=mesh['y_lo'=2,'z'=4,'core'=2,'y_hi'=2,'x'=4] {'y_lo','z','core'}, dimensions={0} | all-to-all | bytes 65536 | tf_op jit(solution)/shard_map/all_to_all | solution.py:628
  57.3 10.1 %all_to_all.56.parts_ref = f32[8,8,1024]{2,1,0:T(8,128)S(1)} all-to-all(f32[8,8,1024]{2,1,0:T(8,128)S(1)} %spread.3), channel_id=1, replica_groups=mesh['y_lo'=2,'z'=4,'core'=2,'y_hi'=2,'x'=4] {'y_lo','z'}, dimensions={0} | all-to-all | bytes 524288 | tf_op jit(solution)/shard_map/all_to_all | solution.py:668
  67.9 0.8 collective-permute-done.5.other_ref
  69.2 17.3 %all_to_all.57 = f32[128,1,640]{2,1,0:T(1,128)S(1)} all-to-all(f32[128,1,640]{2,1,0:T(1,128)S(1)} %bitcast.21), channel_id=1, replica_groups=mesh['y_lo'=2,'z'=4,'core'=2,'y_hi'=2,'x'=4] {'y_hi','x','y_lo','z','core'}, dimensions={0} | all-to-all | bytes 655360 | tf_op jit(solution)/shard_map/all_to_all | solution.py:628
  86.5 1.0 owner_next.2
  87.5 8.7 %all_to_all.58 = f32[16,4,128]{2,1,0:T(4,128)S(1)} all-to-all(f32[16,4,128]{2,1,0:T(4,128)S(1)} %bitcast.33), channel_id=1, replica_groups=mesh['y_lo'=2,'z'=4,'core'=2,'y_hi'=2,'x'=4] {'y_lo','z','core'}, dimensions={0} | all-to-all | bytes 65536 | tf_op jit(solution)/shard_map/all_to_all | solution.py:628
  98.0 10.1 %all_to_all.59.parts_ref = f32[8,8,1024]{2,1,0:T(8,128)S(1)} all-to-all(f32[8,8,1024]{2,1,0:T(8,128)S(1)} %spread.4), channel_id=1, replica_groups=mesh['y_lo'=2,'z'=4,'core'=2,'y_hi'=2,'x'=4] {'y_lo','z'}, dimensions={0} | all-to-all | bytes 524288 | tf_op jit(solution)/shard_map/all_to_all | solution.py:668
  109.9 16.0 %all_to_all.60 = f32[128,1,640]{2,1,0:T(1,128)S(1)} all-to-all(f32[128,1,640]{2,1,0:T(1,128)S(1)} %bitcast.20), channel_id=1, replica_groups=mesh['y_lo'=2,'z'=4,'core'=2,'y_hi'=2,'x'=4] {'y_hi','x','y_lo','z','core'}, dimensions={0} | all-to-all | bytes 655360 | tf_op jit(solution)/shard_map/all_to_all | solution.py:628
  125.9 1.0 owner_next.3
  126.9 8.7 %all_to_all.61 = f32[16,4,128]{2,1,0:T(4,128)S(1)} all-to-all(f32[16,4,128]{2,1,0:T(4,128)S(1)} %bitcast.32), channel_id=1, replica_groups=mesh['y_lo'=2,'z'=4,'core'=2,'y_hi'=2,'x'=4] {'y_lo','z','core'}, dimensions={0} | all-to-all | bytes 65536 | tf_op jit(solution)/shard_map/all_to_all | solution.py:628
  137.5 10.1 %all_to_all.62.parts_ref = f32[8,8,1024]{2,1,0:T(8,128)S(1)} all-to-all(f32[8,8,1024]{2,1,0:T(8,128)S(1)} %spread.5), channel_id=1, replica_groups=mesh['y_lo'=2,'z'=4,'core'=2,'y_hi'=2,'x'=4] {'y_lo','z'}, dimensions={0} | all-to-all | bytes 524288 | tf_op jit(solution)/shard_map/all_to_all | solution.py:668
  147.9 1.0 collective-permute-done.9.other_ref
  149.0 11.2 %all_to_all.63.sums_ref = f32[16,8,128]{2,1,0:T(8,128)S(1)} all-to-all(f32[16,8,128]{2,1,0:T(8,128)S(1)} %settle.1), channel_id=1, replica_groups=mesh['y_lo'=2,'z'=4,'core'=2,'y_hi'=2,'x'=4] {'core','y_hi','x'}, dimensions={0} | all-to-all | bytes 131072 | tf_op jit(solution)/shard_map/all_to_all | solution.py:688
  (53 shorter events, 10.9 us)
Async XLA Ops:
  0.6 20.2 %copy-start.2 = (s32[16,2048]{1,0:T(8,128)S(1)}, s32[16,2048]{1,0:T(8,128)}, u32[]{:S(2)}) copy-start(s32[16,2048]{1,0:T(8,128)} %index_ref.3) | copy-start | bytes 393220
  0.6 20.2 %copy-start.8 = (f32[16]{0:T(128)S(1)}, f32[16]{0:T(128)}, u32[]{:S(2)}) copy-start(f32[16]{0:T(128)} %table_ref.5) | copy-start | bytes 196
  6.0 8.9 %collective-permute-start = (f32[8,2048]{1,0:T(8,128)}, f32[8,2048]{1,0:T(8,128)S(1)}, u32[]{:S(2)}, u32[]{:S(2)}) collective-permute-start(f32[8,2048]{1,0:T(8,128)} %get-tuple-element.40), channel_id=1, source_target_pairs={{0,4},{4,0},{1,5},{5,1},{2,6},{6,2},{3,7},{7,3},{8,12},{12,8},{9,1... | collective-permute-start | bytes 196616 | tf_op jit(solution)/shard_map/ppermute | solution.py:635
  9.4 11.5 %all-to-all-start = ((s32[16,1,128]{2,1,0:T(1,128)}), s32[16,1,128]{2,1,0:T(1,128)S(1)}, u32[]{:S(2)}, u32[]{:S(2)}) async-start(s32[16,1,128]{2,1,0:T(1,128)} %bitcast.35), calls=%async_computation | async-start | bytes 16384 | tf_op jit(solution)/shard_map/all_to_all | solution.py:651
  15.8 12.0 %collective-permute-start.3 = (f32[8,2048]{1,0:T(8,128)S(1)}, f32[8,2048]{1,0:T(8,128)S(1)}, u32[]{:S(2)}, u32[]{:S(2)}) collective-permute-start(f32[8,2048]{1,0:T(8,128)S(1)} %add.3.own_ref), channel_id=1, source_target_pairs={{0,3},{1,0},{2,1},{3,2},{4,7},{5,4},{6,5},{7,6},{8,11},{9,8},{10,9... | collective-permute-start | bytes 196616 | tf_op jit(solution)/shard_map/ppermute | solution.py:635
  18.6 9.1 %collective-permute-start.2 = (f32[8,2048]{1,0:T(8,128)S(1)}, f32[8,2048]{1,0:T(8,128)S(1)}, u32[]{:S(2)}, u32[]{:S(2)}) collective-permute-start(f32[8,2048]{1,0:T(8,128)S(1)} %add.3.own_ref), channel_id=1, source_target_pairs={{0,2},{1,3},{2,0},{3,1},{4,6},{5,7},{6,4},{7,5},{8,10},{9,11},{10,... | collective-permute-start | bytes 196616 | tf_op jit(solution)/shard_map/ppermute | solution.py:635
  19.4 8.4 %collective-permute-start.1 = (f32[8,2048]{1,0:T(8,128)S(1)}, f32[8,2048]{1,0:T(8,128)S(1)}, u32[]{:S(2)}, u32[]{:S(2)}) collective-permute-start(f32[8,2048]{1,0:T(8,128)S(1)} %add.3.own_ref), channel_id=1, source_target_pairs={{0,1},{1,2},{2,3},{3,0},{4,5},{5,6},{6,7},{7,4},{8,9},{9,10},{10,1... | collective-permute-start | bytes 196616 | tf_op jit(solution)/shard_map/ppermute | solution.py:635
  29.3 12.8 %all-to-all-start.1 = ((f32[16,4,128]{2,1,0:T(4,128)}), f32[16,4,128]{2,1,0:T(4,128)S(1)}, u32[]{:S(2)}, u32[]{:S(2)}) async-start(f32[16,4,128]{2,1,0:T(4,128)} %bitcast.5), calls=%async_computation.1 | async-start | bytes 65536 | tf_op jit(solution)/shard_map/all_to_all | solution.py:628
  34.4 7.7 %copy-start = (f32[2,256,256]{2,1,0:T(8,128)S(1)}, f32[2,256,256]{2,1,0:T(8,128)}, u32[]{:S(2)}) copy-start(f32[2,256,256]{2,1,0:T(8,128)} %inverse_ref.5) | copy-start | bytes 1572868
  34.4 7.7 %copy-start.4 = (s32[1,512]{1,0:T(1,128)S(1)}, s32[1,512]{1,0:T(1,128)}, u32[]{:S(2)}) copy-start(s32[1,512]{1,0:T(1,128)} %get-tuple-element.52.holder_ref) | copy-start | bytes 6148
  34.4 7.7 %copy-start.5 = (s32[1,512]{1,0:T(1,128)S(1)}, s32[1,512]{1,0:T(1,128)}, u32[]{:S(2)}) copy-start(s32[1,512]{1,0:T(1,128)} %get-tuple-element.51.serial_ref) | copy-start | bytes 6148
  34.4 7.7 %copy-start.6 = (f32[8,448]{1,0:T(8,128)S(1)}, f32[8,448]{1,0:T(8,128)}, u32[]{:S(2)}) copy-start(f32[8,448]{1,0:T(8,128)} %beta_ref.1) | copy-start | bytes 43012
  56.0 1.2 collective-permute-start.4
  56.8 11.9 %copy-start.1 = (f32[8,2048]{1,0:T(8,128)S(1)}, f32[8,2048]{1,0:T(8,128)}, u32[]{:S(2)}) copy-start(f32[8,2048]{1,0:T(8,128)} %resid_in.1) | copy-start | bytes 196612
  56.8 11.9 %copy-start.3 = (s32[8,128]{1,0:T(8,128)S(1)}, s32[8,128]{1,0:T(8,128)}, u32[]{:S(2)}) copy-start(s32[8,128]{1,0:T(8,128)} %get-tuple-element.47.core_ref) | copy-start | bytes 12292
  56.8 11.9 %copy-start.7 = (s32[8,128]{1,0:T(8,128)S(1)}, s32[8,128]{1,0:T(8,128)}, u32[]{:S(2)}) copy-start(s32[8,128]{1,0:T(8,128)} %get-tuple-element.48.rank_ref) | copy-start | bytes 12292
  67.4 1.3 collective-permute-start.5
  96.8 1.2 collective-permute-start.6
  108.2 1.3 collective-permute-start.7
  136.3 1.2 collective-permute-start.8
  147.7 1.3 collective-permute-start.9

commit v8 on v7

--- a/solution.py
+++ b/solution.py
@@ -22,8 +22,8 @@
 penalty = 0.5
 epsilon = 1e-06
 SMALL = pltpu.CompilerParams(vmem_limit_bytes=12 * 1024 * 1024)
-MEDIUM = pltpu.CompilerParams(vmem_limit_bytes=50 * 1024 * 1024)
-WIDE = pltpu.CompilerParams(vmem_limit_bytes=52 * 1024 * 1024)
+MEDIUM = pltpu.CompilerParams(vmem_limit_bytes=48 * 1024 * 1024)
+WIDE = pltpu.CompilerParams(vmem_limit_bytes=53 * 1024 * 1024)
 LARGE = pltpu.CompilerParams(vmem_limit_bytes=60 * 1024 * 1024)
 f32 = jnp.float32
 bf16 = jnp.bfloat16
@@ -192,6 +192,7 @@
 
 def select_kernel(
     own,
+    skip,
     table_ref,
     packed_ref,
     index_ref,
@@ -204,10 +205,10 @@
     piece_ref=None,
     out_sems=None,
 ):
-    samples = out_ref.shape[0]
+    half = geno_hbm.shape[0] // 2
     chunks, rows = geno_ref.shape[:2]
     core = lax.axis_index("core")
-    first = (core if own else 1 - core) * samples
+    first = (core if own else 1 - core) * half + skip
     copies = []
     for n in range(chunks):
         at = pl.multiple_of(first + n * rows, rows)
@@ -241,15 +242,15 @@
         out.wait()
 
 
-def select(own, table, packed, geno, index, params):
-    samples, width = geno.shape[0] // 2, geno.shape[1]
+def select(own, part, parts, table, packed, geno, index, params):
+    samples, width = geno.shape[0] // 2 // parts, geno.shape[1]
     held = packed.shape[0] * CAP
-    chunks = 4 if own else 2
+    chunks = 2
     rows = samples // chunks
     vmem = pl.BlockSpec(memory_space=pltpu.VMEM)
     pieces = [pltpu.VMEM((chunks, rows, held), bf16), pltpu.SemaphoreType.DMA((chunks,))]
     return pl.pallas_call(
-        functools.partial(select_kernel, own),
+        functools.partial(select_kernel, own, part * samples),
         in_specs=[
             pl.BlockSpec(memory_space=pltpu.SMEM),
             vmem,
@@ -333,17 +334,12 @@
     holder_ref,
     inverse_ref,
     beta_ref,
-    columns_hbm,
     pay_ref,
     b_ref,
     d_ref,
     g_ref,
-    columns_ref,
     wide_ref,
-    sem,
 ):
-    copy = pltpu.make_async_copy(columns_hbm, columns_ref, sem)
-    copy.start()
     fit = serial_ref.shape[1]
     active = beta_ref.shape[1]
     b_ref[...] = jnp.zeros_like(b_ref)
@@ -357,7 +353,6 @@
     direction_step(
         data_ref[...], serial_ref, holder_ref, inverse_ref, advance, wide_ref, d_ref, pay_ref
     )
-    copy.wait()
 
 
 def owner_kernel(
@@ -406,25 +401,16 @@
     )
 
 
-def owner_first(data, serial, holder, inverse, beta, columns):
+def owner_first(data, serial, holder, inverse, beta):
     fit = serial.shape[1]
     held = jax.ShapeDtypeStruct((HALF, 2 * fit), f32)
-    vmem = pl.BlockSpec(memory_space=pltpu.VMEM)
     return pl.pallas_call(
         first_owner_kernel,
-        in_specs=[vmem] * 5 + [pl.BlockSpec(memory_space=pltpu.HBM)],
-        out_specs=(vmem,) * 5,
-        out_shape=(
-            jax.ShapeDtypeStruct(data.shape, f32),
-            held,
-            held,
-            held,
-            jax.ShapeDtypeStruct(columns.shape, columns.dtype),
-        ),
-        scratch_shapes=[pltpu.VMEM((2 * HALF, fit), f32), pltpu.SemaphoreType.DMA],
-        compiler_params=MEDIUM,
+        out_shape=(jax.ShapeDtypeStruct(data.shape, f32), held, held, held),
+        scratch_shapes=[pltpu.VMEM((2 * HALF, fit), f32)],
+        compiler_params=SMALL,
         name="owner_first",
-    )(data, serial, holder, inverse, beta, columns)
+    )(data, serial, holder, inverse, beta)
 
 
 def owner_next(data, serial, holder, inverse, state, resid, update, final):
@@ -449,12 +435,47 @@
     )(data, serial, holder, inverse, *state, resid, update)
 
 
-def update_kernel(pay_ref, columns_ref, out_ref):
+def update_kernel(pay_ref, columns_ref, out_ref, ready=lambda at: None):
     packed = jnp.concatenate(
         [swapped(pay_ref[at : at + 8, :]) for at in range(0, pay_ref.shape[0], 8)], 1
     ).astype(bf16)
     for at in range(0, out_ref.shape[1], ROWS):
+        ready(at)
         out_ref[:, at : at + ROWS] = dot_t(packed, columns_ref[at : at + ROWS, :])
+
+
+def fetching_kernel(pay_ref, one_hbm, two_hbm, out_ref, columns_ref, sems):
+    rows = one_hbm.shape[0]
+    copies = {}
+    for n, piece in enumerate((one_hbm, two_hbm)):
+        for at in range(0, rows, ROWS):
+            to = n * rows + at
+            copies[to] = pltpu.make_async_copy(
+                piece.at[pl.ds(at, ROWS)], columns_ref.at[pl.ds(to, ROWS)], sems.at[to // ROWS]
+            )
+            copies[to].start()
+    update_kernel(pay_ref, columns_ref, out_ref, lambda at: copies[at].wait())
+
+
+def first_update(pay, one, two):
+    samples, held = 2 * one.shape[0], one.shape[1]
+    vmem = pl.BlockSpec(memory_space=pltpu.VMEM)
+    hbm = pl.BlockSpec(memory_space=pltpu.HBM)
+    return pl.pallas_call(
+        fetching_kernel,
+        in_specs=[vmem, hbm, hbm],
+        out_specs=(vmem, vmem),
+        out_shape=(
+            jax.ShapeDtypeStruct((2 * HALF, samples), f32),
+            jax.ShapeDtypeStruct((samples, held), bf16),
+        ),
+        scratch_shapes=[pltpu.SemaphoreType.DMA((samples // ROWS,))],
+        compiler_params=MEDIUM,
+        cost_estimate=pl.CostEstimate(
+            flops=512 * samples * held, bytes_accessed=2 * samples * held, transcendentals=0
+        ),
+        name="update_first",
+    )(pay, one, two)
 
 
 def partial_update(pay, columns):
@@ -652,19 +673,26 @@
         packed.reshape(holders, 1, LANES), VAR, split_axis=0, concat_axis=0, tiled=True
     ).reshape(holders, LANES)
 
-    away = select(False, scale_table, packed, geno, scale_index, MEDIUM)
+    away = select(False, 0, 1, scale_table, packed, geno, scale_index, MEDIUM)
     parts, away = lax.optimization_barrier((parts, away))
     scores, pay = pick(parts, packed, inv_root)
     pay, packed = lax.optimization_barrier((pay, packed))
-    home = select(True, scale_table, packed, geno, scale_index, WIDE)
-    pay, *state, home = owner_first(
-        exchange(pay, VAR), serial, holder, block_inverse, beta_active, home
-    )
+    one = select(True, 0, 2, scale_table, packed, geno, scale_index, WIDE)
+    data, one = lax.optimization_barrier((exchange(pay, VAR), one))
+    pay, *state = owner_first(data, serial, holder, block_inverse, beta_active)
+    pay, packed = lax.optimization_barrier((pay, packed))
+    two = select(True, 1, 2, scale_table, packed, geno, scale_index, WIDE)
+    pay, two = lax.optimization_barrier((exchange(pay, VAR), two))
     current = residual
     for pass_index in range(PASSES):
-        pay = exchange(pay, VAR)
+        if pass_index > 0:
+            pay = exchange(pay, VAR)
         arrived = shifted(partial_update(pay, away), "core")
-        mine = spread(partial_update(pay, home), arrived, lax.axis_size(CHIPS))
+        if pass_index > 0:
+            keep = partial_update(pay, home)
+        else:
+            keep, home = first_update(pay, one, two)
+        mine = spread(keep, arrived, lax.axis_size(CHIPS))
         mine = total(lax.all_to_all(mine, CHIPS, split_axis=0, concat_axis=0, tiled=True))
         other = shifted(mine, "core")
         if pass_index + 1 == PASSES:
@@ -684,7 +712,6 @@
         state = (coeffs, direction, *gradient)
 
     sums = settle(core, mine, current, inv_root, 2 * copies)
-    sums, other = lax.optimization_barrier((sums, other))
     sums = lax.all_to_all(sums, ("core",) + SAMP, split_axis=0, concat_axis=0, tiled=True)
     return (scores, *last(sums, core, mine, other, coeffs, direction, current, inv_root))
 

time: 163 us -> 163 us (level)
  blocking collectives: 104 us -> 81 us
  starting transfers between devices: 19.2 us -> 29.8 us
  waiting for transfers between devices: 4.64 us -> 11.7 us
  Pallas kernels: 31.6 us -> 36 us
    all_to_all x5 -> x4, blocking collectives: 62.2 us -> 48.8 us  [exchange(): lax.all_to_all(pay.reshape(shape), axes, split_axis=0, concat_axis=0, til...]
    all_to_all x1 -> x0, blocking collectives: 11.2 us -> none  [on_device(): lax.all_to_all(sums, ('core',) + SAMP, split_axis=0, concat_axis=0, tiled...]
    all_to_all x0 -> x1, waiting for transfers between devices: none -> 6.38 us  [on_device(): lax.all_to_all(sums, ('core',) + SAMP, split_axis=0, concat_axis=0, tiled...]
    all_to_all x1 -> x2, starting transfers between devices: 5.12 us -> 10.5 us  [exchange(): lax.all_to_all(pay.reshape(shape), axes, split_axis=0, concat_axis=0, til...]
    pallas_call x3 -> x5, Pallas kernels: 16.1 us -> 20.5 us  [the longest x3 17 us: select(): pl.pallas_call(functools.partial(select_kernel, own, part * samples), in_...]
    all_to_all x0 -> x1, starting transfers between devices: none -> 3.72 us  [on_device(): lax.all_to_all(sums, ('core',) + SAMP, split_axis=0, concat_axis=0, tiled...]
    all_to_all x1 -> x2, waiting for transfers between devices: 0.01 us -> 1.9 us  [exchange(): lax.all_to_all(pay.reshape(shape), axes, split_axis=0, concat_axis=0, til...]
    all_to_all x3, blocking collectives: 30.4 us -> 32.2 us  [on_device(): lax.all_to_all(mine, CHIPS, split_axis=0, concat_axis=0, tiled=True)]
  transfers between devices with their start and end apart: 12 -> 14, of which waited for: 7 -> 8; matrix products, arithmetic and copies ran while one was open for 1% -> 1% of each run, Pallas kernels for 11% -> 13%
where the time goes in v8:
time: 163 us; the launch traced here: 161 us
  blocking collectives  81 us (50%)
  Pallas kernels  36 us (22%)
  starting transfers between devices  29.8 us (18%)
  waiting for transfers between devices  11.7 us (7%)
    all_to_all x4, blocking collectives, exchange(): lax.all_to_all(pay.reshape(shape), axes, split_axis=0, concat_axis=0, til...  48.8 us
    all_to_all x3, blocking collectives, on_device(): lax.all_to_all(mine, CHIPS, split_axis=0, concat_axis=0, tiled=True)  32.2 us
    pallas_call x3, Pallas kernels, select(): pl.pallas_call(functools.partial(select_kernel, own, part * samples), in_...  17 us
    all_to_all x2, starting transfers between devices, exchange(): lax.all_to_all(pay.reshape(shape), axes, split_axis=0, concat_axis=0, til...  10.5 us
    ppermute x10, starting transfers between devices, shifted(): return lax.ppermute(x, axis, [(i, (i + by) % size) for i in range(size)])  10.1 us
    all_to_all x1, waiting for transfers between devices, on_device(): lax.all_to_all(sums, ('core',) + SAMP, split_axis=0, concat_axis=0, tiled...  6.38 us
    all_to_all x1, starting transfers between devices, on_device(): lax.all_to_all(packed.reshape(holders, 1, LANES), VAR, split_axis=0, conc...  5.53 us
    pallas_call x1, Pallas kernels, screen(): pl.pallas_call(screen_kernel, in_specs=[pl.BlockSpec(memory_space=pltpu.S...  5.34 us
  transfers between devices with their start and end apart: 14, of which 8 were waited for; matrix products, arithmetic and copies ran while one was open for 1% of the time, Pallas kernels for 13%

profile of v8, /device:TPU:0, one launch (start us, length us, event | category | flops | bytes accessed | tf_op | source)
XLA Modules:
  0.0 161.1 jit_solution(5777762191269813012)
XLA Ops:
  0.7 5.3 %screen.1 = (f32[8,2048]{1,0:T(8,128)}, s32[1,512]{1,0:T(1,128)}, s32[1,512]{1,0:T(1,128)}, s32[16,128]{1,0:T(8,128)}, s32[8,128]{1,0:T(8,128)}, /*index=5*/s32[8,128]{1,0:T(8,128)}) custom-call(f32[16]{0:T(128)} %table_ref.7, s32[1,448]{1,0:T(1,128)} %bitcast.36, s32[1,64]{1,0:T(1,128)} %bitcast.37, s32[16,2048]{1,0:T(8,128)} %index_ref.5, ...), custom_call_target="tpu_custom_call" | custom-call | flops 67108864 | bytes 8388608 | tf_op jit(solution)/shard_map/screen/pallas_call | solution.py:172
  6.0 3.4 %collective-permute-start = (f32[8,2048]{1,0:T(8,128)}, f32[8,2048]{1,0:T(8,128)S(1)}, u32[]{:S(2)}, u32[]{:S(2)}) collective-permute-start(f32[8,2048]{1,0:T(8,128)} %get-tuple-element.45), channel_id=1, source_target_pairs={{0,4},{4,0},{1,5},{5,1},{2,6},{6,2},{3,7},{7,3},{8,12},{12,8},{9,1... | collective-permute-start | bytes 196616 | tf_op jit(solution)/shard_map/ppermute | solution.py:656
  9.4 5.5 %all-to-all-start = ((s32[16,1,128]{2,1,0:T(1,128)}), s32[16,1,128]{2,1,0:T(1,128)S(1)}, u32[]{:S(2)}, u32[]{:S(2)}) async-start(s32[16,1,128]{2,1,0:T(1,128)} %bitcast.35), calls=%async_computation | async-start | bytes 16384 | tf_op jit(solution)/shard_map/all_to_all | solution.py:672
  15.8 1.6 collective-permute-start.1
  17.3 2.7 %collective-permute-start.2 = (f32[8,2048]{1,0:T(8,128)S(1)}, f32[8,2048]{1,0:T(8,128)S(1)}, u32[]{:S(2)}, u32[]{:S(2)}) collective-permute-start(f32[8,2048]{1,0:T(8,128)S(1)} %add.3.own_ref), channel_id=1, source_target_pairs={{0,2},{1,3},{2,0},{3,1},{4,6},{5,7},{6,4},{7,5},{8,10},{9,11},{10,... | collective-permute-start | bytes 196616 | tf_op jit(solution)/shard_map/ppermute | solution.py:656
  20.0 1.4 collective-permute-start.3
  21.5 6.8 %select.3.columns_ref = bf16[1024,1024]{1,0:T(8,128)(2,1)S(1)} custom-call(f32[16]{0:T(128)S(1)} %copy-done.10, s32[16,128]{1,0:T(8,128)S(1)} %bitcast.29, s32[16,2048]{1,0:T(8,128)S(1)} %copy-done.3, bf16[2048,2048]{1,0:T(8,128)(2,1)} %geno_hbm.7), custom_call_target="tpu_custom_call" | custom-call | flops 4294967296 | bytes 4194304 | tf_op jit(solution)/shard_map/select/pallas_call | solution.py:252
  28.4 1.5 pick.1
  29.9 5.7 %all-to-all-start.1 = ((f32[16,4,128]{2,1,0:T(4,128)}), f32[16,4,128]{2,1,0:T(4,128)S(1)}, u32[]{:S(2)}, u32[]{:S(2)}) async-start(f32[16,4,128]{2,1,0:T(4,128)} %bitcast.5), calls=%async_computation.1 | async-start | bytes 65536 | tf_op jit(solution)/shard_map/all_to_all | solution.py:649
  35.6 5.1 %select.4.one_hbm = bf16[512,1024]{1,0:T(8,128)(2,1)} custom-call(f32[16]{0:T(128)S(1)} %copy-done.10, s32[16,128]{1,0:T(8,128)S(1)} %bitcast.31, s32[16,2048]{1,0:T(8,128)S(1)} %copy-done.3, bf16[2048,2048]{1,0:T(8,128)(2,1)} %geno_hbm.7), custom_call_target="tpu_custom_call" | custom-call | flops 2147483648 | bytes 2097152 | tf_op jit(solution)/shard_map/select/pallas_call | solution.py:252
  41.7 1.6 %owner_first.1 = (f32[64,128]{1,0:T(8,128)}, f32[4,1024]{1,0:T(4,128)S(1)}, f32[4,1024]{1,0:T(4,128)S(1)}, f32[4,1024]{1,0:T(4,128)S(1)}) custom-call(f32[64,128]{1,0:T(8,128)S(1)} %bitcast.28, s32[1,512]{1,0:T(1,128)S(1)} %copy-done.7, s32[1,512]{1,0:T(1,128)S(1)} %copy-done.6, f32[2,256,256]{2,1,0:T(8,128)S(1)} %copy-done, f32[8,448]{1,0:T(8,128)S(1)} %copy-done.9), custom_call_target="tpu_custom_call" | custom-call | tf_op jit(solution)/shard_map/owner_first/pallas_call | solution.py:407
  43.4 4.8 %all-to-all-start.2 = ((f32[16,4,128]{2,1,0:T(4,128)}), f32[16,4,128]{2,1,0:T(4,128)S(1)}, u32[]{:S(2)}, u32[]{:S(2)}) async-start(f32[16,4,128]{2,1,0:T(4,128)} %bitcast.7), calls=%async_computation.2 | async-start | bytes 65536 | tf_op jit(solution)/shard_map/all_to_all | solution.py:649
  48.2 5.1 %select.5.two_hbm = bf16[512,1024]{1,0:T(8,128)(2,1)} custom-call(f32[16]{0:T(128)S(1)} %copy-done.10, s32[16,128]{1,0:T(8,128)S(1)} %bitcast.32, s32[16,2048]{1,0:T(8,128)S(1)} %copy-done.3, bf16[2048,2048]{1,0:T(8,128)(2,1)} %geno_hbm.7), custom_call_target="tpu_custom_call" | custom-call | flops 2147483648 | bytes 2097152 | tf_op jit(solution)/shard_map/select/pallas_call | solution.py:252
  55.8 1.8 %update_first.1 = (f32[8,1024]{1,0:T(8,128)S(1)}, bf16[1024,1024]{1,0:T(8,128)(2,1)S(1)}) custom-call(f32[64,128]{1,0:T(8,128)S(1)} %bitcast.23, bf16[512,1024]{1,0:T(8,128)(2,1)S(1)} %copy-done.1, bf16[512,1024]{1,0:T(8,128)(2,1)S(1)} %copy-done.2), custom_call_target="tpu_custom_call" | custom-call | flops 536870912 | bytes 2097152 | tf_op jit(solution)/shard_map/update_first/pallas_call | solution.py:464
  57.7 12.0 %all_to_all.55.parts_ref = f32[8,8,1024]{2,1,0:T(8,128)S(1)} all-to-all(f32[8,8,1024]{2,1,0:T(8,128)S(1)} %spread.3), channel_id=1, replica_groups=mesh['y_lo'=2,'z'=4,'core'=2,'y_hi'=2,'x'=4] {'y_lo','z'}, dimensions={0} | all-to-all | bytes 524288 | tf_op jit(solution)/shard_map/all_to_all | solution.py:696
  71.5 15.4 %all_to_all.56 = f32[128,1,640]{2,1,0:T(1,128)S(1)} all-to-all(f32[128,1,640]{2,1,0:T(1,128)S(1)} %bitcast.21), channel_id=1, replica_groups=mesh['y_lo'=2,'z'=4,'core'=2,'y_hi'=2,'x'=4] {'y_hi','x','y_lo','z','core'}, dimensions={0} | all-to-all | bytes 655360 | tf_op jit(solution)/shard_map/all_to_all | solution.py:649
  86.9 1.0 owner_next.2
  87.9 8.7 %all_to_all.57 = f32[16,4,128]{2,1,0:T(4,128)S(1)} all-to-all(f32[16,4,128]{2,1,0:T(4,128)S(1)} %bitcast.34), channel_id=1, replica_groups=mesh['y_lo'=2,'z'=4,'core'=2,'y_hi'=2,'x'=4] {'y_lo','z','core'}, dimensions={0} | all-to-all | bytes 65536 | tf_op jit(solution)/shard_map/all_to_all | solution.py:649
  98.5 10.1 %all_to_all.58.parts_ref = f32[8,8,1024]{2,1,0:T(8,128)S(1)} all-to-all(f32[8,8,1024]{2,1,0:T(8,128)S(1)} %spread.4), channel_id=1, replica_groups=mesh['y_lo'=2,'z'=4,'core'=2,'y_hi'=2,'x'=4] {'y_lo','z'}, dimensions={0} | all-to-all | bytes 524288 | tf_op jit(solution)/shard_map/all_to_all | solution.py:696
  110.4 16.0 %all_to_all.59 = f32[128,1,640]{2,1,0:T(1,128)S(1)} all-to-all(f32[128,1,640]{2,1,0:T(1,128)S(1)} %bitcast.20), channel_id=1, replica_groups=mesh['y_lo'=2,'z'=4,'core'=2,'y_hi'=2,'x'=4] {'y_hi','x','y_lo','z','core'}, dimensions={0} | all-to-all | bytes 655360 | tf_op jit(solution)/shard_map/all_to_all | solution.py:649
  127.4 8.7 %all_to_all.60 = f32[16,4,128]{2,1,0:T(4,128)S(1)} all-to-all(f32[16,4,128]{2,1,0:T(4,128)S(1)} %bitcast.33), channel_id=1, replica_groups=mesh['y_lo'=2,'z'=4,'core'=2,'y_hi'=2,'x'=4] {'y_lo','z','core'}, dimensions={0} | all-to-all | bytes 65536 | tf_op jit(solution)/shard_map/all_to_all | solution.py:649
  137.9 10.1 %all_to_all.61.parts_ref = f32[8,8,1024]{2,1,0:T(8,128)S(1)} all-to-all(f32[8,8,1024]{2,1,0:T(8,128)S(1)} %spread.5), channel_id=1, replica_groups=mesh['y_lo'=2,'z'=4,'core'=2,'y_hi'=2,'x'=4] {'y_lo','z'}, dimensions={0} | all-to-all | bytes 524288 | tf_op jit(solution)/shard_map/all_to_all | solution.py:696
  148.9 3.7 %all-to-all-start.10 = ((f32[16,8,128]{2,1,0:T(8,128)}), f32[16,8,128]{2,1,0:T(8,128)S(1)}, u32[]{:S(2)}, u32[]{:S(2)}) async-start(f32[16,8,128]{2,1,0:T(8,128)} %settle.1), calls=%async_computation.10 | async-start | bytes 131072 | tf_op jit(solution)/shard_map/all_to_all | solution.py:715
  153.9 6.4 %all-to-all-done.10.sums_ref = f32[16,8,128]{2,1,0:T(8,128)S(1)} async-done(((f32[16,8,128]{2,1,0:T(8,128)}), f32[16,8,128]{2,1,0:T(8,128)S(1)}, u32[]{:S(2)}, u32[]{:S(2)}) %all-to-all-start.10) | async-done | bytes 65568 | tf_op jit(solution)/shard_map/all_to_all | solution.py:715
  (60 shorter events, 15.6 us)
Async XLA Ops:
  0.6 20.9 %copy-start.3 = (s32[16,2048]{1,0:T(8,128)S(1)}, s32[16,2048]{1,0:T(8,128)}, u32[]{:S(2)}) copy-start(s32[16,2048]{1,0:T(8,128)} %index_ref.5) | copy-start | bytes 393220
  0.6 20.8 %copy-start.10 = (f32[16]{0:T(128)S(1)}, f32[16]{0:T(128)}, u32[]{:S(2)}) copy-start(f32[16]{0:T(128)} %table_ref.7) | copy-start | bytes 196
  6.0 8.9 %collective-permute-start = (f32[8,2048]{1,0:T(8,128)}, f32[8,2048]{1,0:T(8,128)S(1)}, u32[]{:S(2)}, u32[]{:S(2)}) collective-permute-start(f32[8,2048]{1,0:T(8,128)} %get-tuple-element.45), channel_id=1, source_target_pairs={{0,4},{4,0},{1,5},{5,1},{2,6},{6,2},{3,7},{7,3},{8,12},{12,8},{9,1... | collective-permute-start | bytes 196616 | tf_op jit(solution)/shard_map/ppermute | solution.py:656
  9.4 12.1 %all-to-all-start = ((s32[16,1,128]{2,1,0:T(1,128)}), s32[16,1,128]{2,1,0:T(1,128)S(1)}, u32[]{:S(2)}, u32[]{:S(2)}) async-start(s32[16,1,128]{2,1,0:T(1,128)} %bitcast.35), calls=%async_computation | async-start | bytes 16384 | tf_op jit(solution)/shard_map/all_to_all | solution.py:672
  15.8 12.6 %collective-permute-start.1 = (f32[8,2048]{1,0:T(8,128)S(1)}, f32[8,2048]{1,0:T(8,128)S(1)}, u32[]{:S(2)}, u32[]{:S(2)}) collective-permute-start(f32[8,2048]{1,0:T(8,128)S(1)} %add.3.own_ref), channel_id=1, source_target_pairs={{0,1},{1,2},{2,3},{3,0},{4,5},{5,6},{6,7},{7,4},{8,9},{9,10},{10,1... | collective-permute-start | bytes 196616 | tf_op jit(solution)/shard_map/ppermute | solution.py:656
  17.3 11.0 %collective-permute-start.2 = (f32[8,2048]{1,0:T(8,128)S(1)}, f32[8,2048]{1,0:T(8,128)S(1)}, u32[]{:S(2)}, u32[]{:S(2)}) collective-permute-start(f32[8,2048]{1,0:T(8,128)S(1)} %add.3.own_ref), channel_id=1, source_target_pairs={{0,2},{1,3},{2,0},{3,1},{4,6},{5,7},{6,4},{7,5},{8,10},{9,11},{10,... | collective-permute-start | bytes 196616 | tf_op jit(solution)/shard_map/ppermute | solution.py:656
  20.0 8.3 %collective-permute-start.3 = (f32[8,2048]{1,0:T(8,128)S(1)}, f32[8,2048]{1,0:T(8,128)S(1)}, u32[]{:S(2)}, u32[]{:S(2)}) collective-permute-start(f32[8,2048]{1,0:T(8,128)S(1)} %add.3.own_ref), channel_id=1, source_target_pairs={{0,3},{1,0},{2,1},{3,2},{4,7},{5,4},{6,5},{7,6},{8,11},{9,8},{10,9... | collective-permute-start | bytes 196616 | tf_op jit(solution)/shard_map/ppermute | solution.py:656
  29.9 11.8 %all-to-all-start.1 = ((f32[16,4,128]{2,1,0:T(4,128)}), f32[16,4,128]{2,1,0:T(4,128)S(1)}, u32[]{:S(2)}, u32[]{:S(2)}) async-start(f32[16,4,128]{2,1,0:T(4,128)} %bitcast.5), calls=%async_computation.1 | async-start | bytes 65536 | tf_op jit(solution)/shard_map/all_to_all | solution.py:649
  35.6 6.1 %copy-start = (f32[2,256,256]{2,1,0:T(8,128)S(1)}, f32[2,256,256]{2,1,0:T(8,128)}, u32[]{:S(2)}) copy-start(f32[2,256,256]{2,1,0:T(8,128)} %inverse_ref.5) | copy-start | bytes 1572868
  35.6 6.1 %copy-start.6 = (s32[1,512]{1,0:T(1,128)S(1)}, s32[1,512]{1,0:T(1,128)}, u32[]{:S(2)}) copy-start(s32[1,512]{1,0:T(1,128)} %get-tuple-element.59.holder_ref) | copy-start | bytes 6148
  35.6 6.1 %copy-start.7 = (s32[1,512]{1,0:T(1,128)S(1)}, s32[1,512]{1,0:T(1,128)}, u32[]{:S(2)}) copy-start(s32[1,512]{1,0:T(1,128)} %get-tuple-element.58.serial_ref) | copy-start | bytes 6148
  35.6 6.1 %copy-start.9 = (f32[8,448]{1,0:T(8,128)S(1)}, f32[8,448]{1,0:T(8,128)}, u32[]{:S(2)}) copy-start(f32[8,448]{1,0:T(8,128)} %beta_ref.1) | copy-start | bytes 43012
  43.4 10.9 %all-to-all-start.2 = ((f32[16,4,128]{2,1,0:T(4,128)}), f32[16,4,128]{2,1,0:T(4,128)S(1)}, u32[]{:S(2)}, u32[]{:S(2)}) async-start(f32[16,4,128]{2,1,0:T(4,128)} %bitcast.7), calls=%async_computation.2 | async-start | bytes 65536 | tf_op jit(solution)/shard_map/all_to_all | solution.py:649
  54.3 1.5 copy-start.2
  54.9 2.7 %collective-permute-start.4 = (f32[8,1024]{1,0:T(8,128)S(1)}, f32[8,1024]{1,0:T(8,128)S(1)}, u32[]{:S(2)}, u32[]{:S(2)}) collective-permute-start(f32[8,1024]{1,0:T(8,128)S(1)} %update.5), channel_id=1, source_target_pairs={{0,8},{8,0},{1,9},{9,1},{2,10},{10,2},{3,11},{11,3},{4,12},{12,4},... | collective-permute-start | bytes 98312 | tf_op jit(solution)/shard_map/ppermute | solution.py:656
  57.6 13.3 %copy-start.4 = (f32[8,2048]{1,0:T(8,128)S(1)}, f32[8,2048]{1,0:T(8,128)}, u32[]{:S(2)}) copy-start(f32[8,2048]{1,0:T(8,128)} %resid_in.1) | copy-start | bytes 196612
  57.6 13.3 %copy-start.5 = (s32[8,128]{1,0:T(8,128)S(1)}, s32[8,128]{1,0:T(8,128)}, u32[]{:S(2)}) copy-start(s32[8,128]{1,0:T(8,128)} %get-tuple-element.52.core_ref) | copy-start | bytes 12292
  57.6 13.3 %copy-start.8 = (s32[8,128]{1,0:T(8,128)S(1)}, s32[8,128]{1,0:T(8,128)}, u32[]{:S(2)}) copy-start(s32[8,128]{1,0:T(8,128)} %get-tuple-element.53.rank_ref) | copy-start | bytes 12292
  69.7 1.3 collective-permute-start.5
  97.2 1.2 collective-permute-start.6
  108.6 1.3 collective-permute-start.7
  136.7 1.2 collective-permute-start.8
  148.9 11.4 %all-to-all-start.10 = ((f32[16,8,128]{2,1,0:T(8,128)}), f32[16,8,128]{2,1,0:T(8,128)S(1)}, u32[]{:S(2)}, u32[]{:S(2)}) async-start(f32[16,8,128]{2,1,0:T(8,128)} %settle.1), calls=%async_computation.10 | async-start | bytes 131072 | tf_op jit(solution)/shard_map/all_to_all | solution.py:715
  152.6 1.3 collective-permute-start.9
  (1 other events, 1.2 us)

commit v9 on v7

--- a/solution.py
+++ b/solution.py
@@ -273,10 +273,8 @@
     )(table, packed, index, geno)
 
 
-def pick_kernel(
-    inv_root, own_ref, one_ref, two_ref, three_ref, packed_ref, scores_ref, pay_ref
-):
-    scores = ((own_ref[...] + two_ref[...]) + (one_ref[...] + three_ref[...])) * inv_root
+def pick_kernel(inv_root, own_ref, other_ref, packed_ref, scores_ref, pay_ref):
+    scores = (own_ref[...] + other_ref[...]) * inv_root
     scores_ref[...] = scores
     wanted = column_row(packed_ref[...])
     stacked = jnp.concatenate(thirds(scores), 0)
@@ -646,8 +644,8 @@
     part, holder, serial, packed, rank, core = screen(
         scale_table, geno, scale_index, residual, active_ids, admit_ids
     )
-    part = part + shifted(part, "y_hi")
-    parts = [part] + [shifted(part, "x", n) for n in range(1, lax.axis_size("x"))]
+    part = (part + shifted(part, "x", 2)) + (shifted(part, "x", 1) + shifted(part, "x", 3))
+    parts = (part, shifted(part, "y_hi"))
     packed = lax.all_to_all(
         packed.reshape(holders, 1, LANES), VAR, split_axis=0, concat_axis=0, tiled=True
     ).reshape(holders, LANES)
@@ -684,7 +682,6 @@
         state = (coeffs, direction, *gradient)
 
     sums = settle(core, mine, current, inv_root, 2 * copies)
-    sums, other = lax.optimization_barrier((sums, other))
     sums = lax.all_to_all(sums, ("core",) + SAMP, split_axis=0, concat_axis=0, tiled=True)
     return (scores, *last(sums, core, mine, other, coeffs, direction, current, inv_root))
 

time: 163 us -> 164 us (level)
  blocking collectives: 104 us -> 92.9 us
  waiting for transfers between devices: 4.64 us -> 12.3 us
  starting transfers between devices: 19.2 us -> 23 us
    all_to_all x1 -> x0, blocking collectives: 11.2 us -> none  [on_device(): lax.all_to_all(sums, ('core',) + SAMP, split_axis=0, concat_axis=0, tiled...]
    all_to_all x0 -> x1, waiting for transfers between devices: none -> 6.38 us  [on_device(): lax.all_to_all(sums, ('core',) + SAMP, split_axis=0, concat_axis=0, tiled...]
    all_to_all x0 -> x1, starting transfers between devices: none -> 3.72 us  [on_device(): lax.all_to_all(sums, ('core',) + SAMP, split_axis=0, concat_axis=0, tiled...]
  transfers between devices with their start and end apart: 12 -> 13, of which waited for: 7 -> 8; matrix products, arithmetic and copies ran while one was open for 1% -> 1% of each run, Pallas kernels for 11% -> 11%
where the time goes in v9:
time: 164 us; the launch traced here: 162 us
  blocking collectives  92.9 us (57%)
  Pallas kernels  32.2 us (20%)
  starting transfers between devices  23 us (14%)
  waiting for transfers between devices  12.3 us (8%)
    all_to_all x5, blocking collectives, exchange(): lax.all_to_all(pay.reshape(shape), axes, split_axis=0, concat_axis=0, til...  62.5 us
    all_to_all x3, blocking collectives, on_device(): lax.all_to_all(mine, CHIPS, split_axis=0, concat_axis=0, tiled=True)  30.4 us
    pallas_call x2, Pallas kernels, select(): pl.pallas_call(functools.partial(select_kernel, own), in_specs=[pl.BlockS...  14.5 us
    ppermute x10, starting transfers between devices, shifted(): return lax.ppermute(x, axis, [(i, (i + by) % size) for i in range(size)])  9.17 us
    all_to_all x1, starting transfers between devices, on_device(): lax.all_to_all(packed.reshape(holders, 1, LANES), VAR, split_axis=0, conc...  6.43 us
    all_to_all x1, waiting for transfers between devices, on_device(): lax.all_to_all(sums, ('core',) + SAMP, split_axis=0, concat_axis=0, tiled...  6.38 us
    pallas_call x1, Pallas kernels, screen(): pl.pallas_call(screen_kernel, in_specs=[pl.BlockSpec(memory_space=pltpu.S...  5.34 us
    ppermute x10, waiting for transfers between devices, shifted(): return lax.ppermute(x, axis, [(i, (i + by) % size) for i in range(size)])  3.86 us
  transfers between devices with their start and end apart: 13, of which 8 were waited for; matrix products, arithmetic and copies ran while one was open for 1% of the time, Pallas kernels for 11%

profile of v9, /device:TPU:0, one launch (start us, length us, event | category | flops | bytes accessed | tf_op | source)
XLA Modules:
  0.0 162.2 jit_solution(1775514460936168371)
XLA Ops:
  0.7 5.3 %screen.1 = (f32[8,2048]{1,0:T(8,128)}, s32[1,512]{1,0:T(1,128)}, s32[1,512]{1,0:T(1,128)}, s32[16,128]{1,0:T(8,128)}, s32[8,128]{1,0:T(8,128)}, /*index=5*/s32[8,128]{1,0:T(8,128)}) custom-call(f32[16]{0:T(128)} %table_ref.5, s32[1,448]{1,0:T(1,128)} %bitcast.36, s32[1,64]{1,0:T(1,128)} %bitcast.37, s32[16,2048]{1,0:T(8,128)} %index_ref.3, ...), custom_call_target="tpu_custom_call" | custom-call | flops 67108864 | bytes 8388608 | tf_op jit(solution)/shard_map/screen/pallas_call | solution.py:172
  6.0 2.9 %collective-permute-start.2 = (f32[8,2048]{1,0:T(8,128)}, f32[8,2048]{1,0:T(8,128)S(1)}, u32[]{:S(2)}, u32[]{:S(2)}) collective-permute-start(f32[8,2048]{1,0:T(8,128)} %get-tuple-element.36), channel_id=1, source_target_pairs={{0,3},{1,0},{2,1},{3,2},{4,7},{5,4},{6,5},{7,6},{8,11},{9,8},{10,9... | collective-permute-start | bytes 196616 | tf_op jit(solution)/shard_map/ppermute | solution.py:633
  8.9 2.3 %collective-permute-start = (f32[8,2048]{1,0:T(8,128)}, f32[8,2048]{1,0:T(8,128)S(1)}, u32[]{:S(2)}, u32[]{:S(2)}) collective-permute-start(f32[8,2048]{1,0:T(8,128)} %get-tuple-element.36), channel_id=1, source_target_pairs={{0,2},{1,3},{2,0},{3,1},{4,6},{5,7},{6,4},{7,5},{8,10},{9,11},{10,... | collective-permute-start | bytes 196616 | tf_op jit(solution)/shard_map/ppermute | solution.py:633
  11.2 6.4 %all-to-all-start = ((s32[16,1,128]{2,1,0:T(1,128)}), s32[16,1,128]{2,1,0:T(1,128)S(1)}, u32[]{:S(2)}, u32[]{:S(2)}) async-start(s32[16,1,128]{2,1,0:T(1,128)} %bitcast.35), calls=%async_computation | async-start | bytes 16384 | tf_op jit(solution)/shard_map/all_to_all | solution.py:649
  18.5 3.0 %collective-permute-start.3 = (f32[8,2048]{1,0:T(8,128)S(1)}, f32[8,2048]{1,0:T(8,128)S(1)}, u32[]{:S(2)}, u32[]{:S(2)}) collective-permute-start(f32[8,2048]{1,0:T(8,128)S(1)} %add_add_fusion.own_ref), channel_id=1, source_target_pairs={{0,4},{4,0},{1,5},{5,1},{2,6},{6,2},{3,7},{7,3},{8,12},{12,8},{9,1... | collective-permute-start | bytes 196616 | tf_op jit(solution)/shard_map/ppermute | solution.py:633
  21.5 2.1 %all-to-all-done = s32[16,1,128]{2,1,0:T(1,128)S(1)} async-done(((s32[16,1,128]{2,1,0:T(1,128)}), s32[16,1,128]{2,1,0:T(1,128)S(1)}, u32[]{:S(2)}, u32[]{:S(2)}) %all-to-all-start) | async-done | bytes 8224 | tf_op jit(solution)/shard_map/all_to_all | solution.py:649
  23.6 6.8 %select.2.columns_ref = bf16[1024,1024]{1,0:T(8,128)(2,1)S(1)} custom-call(f32[16]{0:T(128)S(1)} %copy-done.8, s32[16,128]{1,0:T(8,128)S(1)} %bitcast.29, s32[16,2048]{1,0:T(8,128)S(1)} %copy-done.2, bf16[2048,2048]{1,0:T(8,128)(2,1)} %geno_hbm.5), custom_call_target="tpu_custom_call" | custom-call | flops 4294967296 | bytes 4194304 | tf_op jit(solution)/shard_map/select/pallas_call | solution.py:251
  30.5 1.5 pick.1
  32.0 3.7 %all-to-all-start.1 = ((f32[16,4,128]{2,1,0:T(4,128)}), f32[16,4,128]{2,1,0:T(4,128)S(1)}, u32[]{:S(2)}, u32[]{:S(2)}) async-start(f32[16,4,128]{2,1,0:T(4,128)} %bitcast.5), calls=%async_computation.1 | async-start | bytes 65536 | tf_op jit(solution)/shard_map/all_to_all | solution.py:626
  35.7 7.7 %select.3.columns_hbm = bf16[1024,1024]{1,0:T(8,128)(2,1)} custom-call(f32[16]{0:T(128)S(1)} %copy-done.8, s32[16,128]{1,0:T(8,128)S(1)} %bitcast.31, s32[16,2048]{1,0:T(8,128)S(1)} %copy-done.2, bf16[2048,2048]{1,0:T(8,128)(2,1)} %geno_hbm.5), custom_call_target="tpu_custom_call" | custom-call | flops 4294967296 | bytes 4194304 | tf_op jit(solution)/shard_map/select/pallas_call | solution.py:251
  43.4 1.6 owner_first.1
  45.0 11.4 %all_to_all.55 = f32[16,4,128]{2,1,0:T(4,128)S(1)} all-to-all(f32[16,4,128]{2,1,0:T(4,128)S(1)} %bitcast.34), channel_id=1, replica_groups=mesh['y_lo'=2,'z'=4,'core'=2,'y_hi'=2,'x'=4] {'y_lo','z','core'}, dimensions={0} | all-to-all | bytes 65536 | tf_op jit(solution)/shard_map/all_to_all | solution.py:626
  58.3 10.1 %all_to_all.56.parts_ref = f32[8,8,1024]{2,1,0:T(8,128)S(1)} all-to-all(f32[8,8,1024]{2,1,0:T(8,128)S(1)} %spread.3), channel_id=1, replica_groups=mesh['y_lo'=2,'z'=4,'core'=2,'y_hi'=2,'x'=4] {'y_lo','z'}, dimensions={0} | all-to-all | bytes 524288 | tf_op jit(solution)/shard_map/all_to_all | solution.py:666
  70.2 17.8 %all_to_all.57 = f32[128,1,640]{2,1,0:T(1,128)S(1)} all-to-all(f32[128,1,640]{2,1,0:T(1,128)S(1)} %bitcast.21), channel_id=1, replica_groups=mesh['y_lo'=2,'z'=4,'core'=2,'y_hi'=2,'x'=4] {'y_hi','x','y_lo','z','core'}, dimensions={0} | all-to-all | bytes 655360 | tf_op jit(solution)/shard_map/all_to_all | solution.py:626
  88.0 1.0 owner_next.2
  89.0 8.7 %all_to_all.58 = f32[16,4,128]{2,1,0:T(4,128)S(1)} all-to-all(f32[16,4,128]{2,1,0:T(4,128)S(1)} %bitcast.33), channel_id=1, replica_groups=mesh['y_lo'=2,'z'=4,'core'=2,'y_hi'=2,'x'=4] {'y_lo','z','core'}, dimensions={0} | all-to-all | bytes 65536 | tf_op jit(solution)/shard_map/all_to_all | solution.py:626
  99.6 10.1 %all_to_all.59.parts_ref = f32[8,8,1024]{2,1,0:T(8,128)S(1)} all-to-all(f32[8,8,1024]{2,1,0:T(8,128)S(1)} %spread.4), channel_id=1, replica_groups=mesh['y_lo'=2,'z'=4,'core'=2,'y_hi'=2,'x'=4] {'y_lo','z'}, dimensions={0} | all-to-all | bytes 524288 | tf_op jit(solution)/shard_map/all_to_all | solution.py:666
  111.5 16.0 %all_to_all.60 = f32[128,1,640]{2,1,0:T(1,128)S(1)} all-to-all(f32[128,1,640]{2,1,0:T(1,128)S(1)} %bitcast.20), channel_id=1, replica_groups=mesh['y_lo'=2,'z'=4,'core'=2,'y_hi'=2,'x'=4] {'y_hi','x','y_lo','z','core'}, dimensions={0} | all-to-all | bytes 655360 | tf_op jit(solution)/shard_map/all_to_all | solution.py:626
  127.5 1.0 owner_next.3
  128.5 8.7 %all_to_all.61 = f32[16,4,128]{2,1,0:T(4,128)S(1)} all-to-all(f32[16,4,128]{2,1,0:T(4,128)S(1)} %bitcast.32), channel_id=1, replica_groups=mesh['y_lo'=2,'z'=4,'core'=2,'y_hi'=2,'x'=4] {'y_lo','z','core'}, dimensions={0} | all-to-all | bytes 65536 | tf_op jit(solution)/shard_map/all_to_all | solution.py:626
  139.1 10.1 %all_to_all.62.parts_ref = f32[8,8,1024]{2,1,0:T(8,128)S(1)} all-to-all(f32[8,8,1024]{2,1,0:T(8,128)S(1)} %spread.5), channel_id=1, replica_groups=mesh['y_lo'=2,'z'=4,'core'=2,'y_hi'=2,'x'=4] {'y_lo','z'}, dimensions={0} | all-to-all | bytes 524288 | tf_op jit(solution)/shard_map/all_to_all | solution.py:666
  150.0 3.7 %all-to-all-start.10 = ((f32[16,8,128]{2,1,0:T(8,128)}), f32[16,8,128]{2,1,0:T(8,128)S(1)}, u32[]{:S(2)}, u32[]{:S(2)}) async-start(f32[16,8,128]{2,1,0:T(8,128)} %settle.1), calls=%async_computation.10 | async-start | bytes 131072 | tf_op jit(solution)/shard_map/all_to_all | solution.py:685
  154.2 0.9 collective-permute-done.9.other_ref
  155.0 6.4 %all-to-all-done.10.sums_ref = f32[16,8,128]{2,1,0:T(8,128)S(1)} async-done(((f32[16,8,128]{2,1,0:T(8,128)}), f32[16,8,128]{2,1,0:T(8,128)S(1)}, u32[]{:S(2)}, u32[]{:S(2)}) %all-to-all-start.10) | async-done | bytes 65568 | tf_op jit(solution)/shard_map/all_to_all | solution.py:685
  (54 shorter events, 12.1 us)
Async XLA Ops:
  0.6 23.0 %copy-start.2 = (s32[16,2048]{1,0:T(8,128)S(1)}, s32[16,2048]{1,0:T(8,128)}, u32[]{:S(2)}) copy-start(s32[16,2048]{1,0:T(8,128)} %index_ref.3) | copy-start | bytes 393220
  0.6 23.0 %copy-start.8 = (f32[16]{0:T(128)S(1)}, f32[16]{0:T(128)}, u32[]{:S(2)}) copy-start(f32[16]{0:T(128)} %table_ref.5) | copy-start | bytes 196
  6.0 11.6 %collective-permute-start.2 = (f32[8,2048]{1,0:T(8,128)}, f32[8,2048]{1,0:T(8,128)S(1)}, u32[]{:S(2)}, u32[]{:S(2)}) collective-permute-start(f32[8,2048]{1,0:T(8,128)} %get-tuple-element.36), channel_id=1, source_target_pairs={{0,3},{1,0},{2,1},{3,2},{4,7},{5,4},{6,5},{7,6},{8,11},{9,8},{10,9... | collective-permute-start | bytes 196616 | tf_op jit(solution)/shard_map/ppermute | solution.py:633
  8.9 8.7 %collective-permute-start.1 = (f32[8,2048]{1,0:T(8,128)}, f32[8,2048]{1,0:T(8,128)S(1)}, u32[]{:S(2)}, u32[]{:S(2)}) collective-permute-start(f32[8,2048]{1,0:T(8,128)} %get-tuple-element.36), channel_id=1, source_target_pairs={{0,1},{1,2},{2,3},{3,0},{4,5},{5,6},{6,7},{7,4},{8,9},{9,10},{10,1... | collective-permute-start | bytes 196616 | tf_op jit(solution)/shard_map/ppermute | solution.py:633
  8.9 8.8 %collective-permute-start = (f32[8,2048]{1,0:T(8,128)}, f32[8,2048]{1,0:T(8,128)S(1)}, u32[]{:S(2)}, u32[]{:S(2)}) collective-permute-start(f32[8,2048]{1,0:T(8,128)} %get-tuple-element.36), channel_id=1, source_target_pairs={{0,2},{1,3},{2,0},{3,1},{4,6},{5,7},{6,4},{7,5},{8,10},{9,11},{10,... | collective-permute-start | bytes 196616 | tf_op jit(solution)/shard_map/ppermute | solution.py:633
  11.2 12.4 %all-to-all-start = ((s32[16,1,128]{2,1,0:T(1,128)}), s32[16,1,128]{2,1,0:T(1,128)S(1)}, u32[]{:S(2)}, u32[]{:S(2)}) async-start(s32[16,1,128]{2,1,0:T(1,128)} %bitcast.35), calls=%async_computation | async-start | bytes 16384 | tf_op jit(solution)/shard_map/all_to_all | solution.py:649
  18.5 11.9 %collective-permute-start.3 = (f32[8,2048]{1,0:T(8,128)S(1)}, f32[8,2048]{1,0:T(8,128)S(1)}, u32[]{:S(2)}, u32[]{:S(2)}) collective-permute-start(f32[8,2048]{1,0:T(8,128)S(1)} %add_add_fusion.own_ref), channel_id=1, source_target_pairs={{0,4},{4,0},{1,5},{5,1},{2,6},{6,2},{3,7},{7,3},{8,12},{12,8},{9,1... | collective-permute-start | bytes 196616 | tf_op jit(solution)/shard_map/ppermute | solution.py:633
  32.0 11.4 %all-to-all-start.1 = ((f32[16,4,128]{2,1,0:T(4,128)}), f32[16,4,128]{2,1,0:T(4,128)S(1)}, u32[]{:S(2)}, u32[]{:S(2)}) async-start(f32[16,4,128]{2,1,0:T(4,128)} %bitcast.5), calls=%async_computation.1 | async-start | bytes 65536 | tf_op jit(solution)/shard_map/all_to_all | solution.py:626
  35.7 7.7 %copy-start = (f32[2,256,256]{2,1,0:T(8,128)S(1)}, f32[2,256,256]{2,1,0:T(8,128)}, u32[]{:S(2)}) copy-start(f32[2,256,256]{2,1,0:T(8,128)} %inverse_ref.5) | copy-start | bytes 1572868
  35.7 7.7 %copy-start.4 = (s32[1,512]{1,0:T(1,128)S(1)}, s32[1,512]{1,0:T(1,128)}, u32[]{:S(2)}) copy-start(s32[1,512]{1,0:T(1,128)} %get-tuple-element.46.holder_ref) | copy-start | bytes 6148
  35.7 7.7 %copy-start.5 = (s32[1,512]{1,0:T(1,128)S(1)}, s32[1,512]{1,0:T(1,128)}, u32[]{:S(2)}) copy-start(s32[1,512]{1,0:T(1,128)} %get-tuple-element.45.serial_ref) | copy-start | bytes 6148
  35.7 7.7 %copy-start.6 = (f32[8,448]{1,0:T(8,128)S(1)}, f32[8,448]{1,0:T(8,128)}, u32[]{:S(2)}) copy-start(f32[8,448]{1,0:T(8,128)} %beta_ref.1) | copy-start | bytes 43012
  57.1 1.2 collective-permute-start.4
  57.8 11.9 %copy-start.1 = (f32[8,2048]{1,0:T(8,128)S(1)}, f32[8,2048]{1,0:T(8,128)}, u32[]{:S(2)}) copy-start(f32[8,2048]{1,0:T(8,128)} %resid_in.1) | copy-start | bytes 196612
  57.8 11.9 %copy-start.3 = (s32[8,128]{1,0:T(8,128)S(1)}, s32[8,128]{1,0:T(8,128)}, u32[]{:S(2)}) copy-start(s32[8,128]{1,0:T(8,128)} %get-tuple-element.41.core_ref) | copy-start | bytes 12292
  57.9 11.9 %copy-start.7 = (s32[8,128]{1,0:T(8,128)S(1)}, s32[8,128]{1,0:T(8,128)}, u32[]{:S(2)}) copy-start(s32[8,128]{1,0:T(8,128)} %get-tuple-element.42.rank_ref) | copy-start | bytes 12292
  68.5 1.3 collective-permute-start.5
  98.4 1.2 collective-permute-start.6
  109.8 1.3 collective-permute-start.7
  137.8 1.2 collective-permute-start.8
  150.0 11.4 %all-to-all-start.10 = ((f32[16,8,128]{2,1,0:T(8,128)}), f32[16,8,128]{2,1,0:T(8,128)S(1)}, u32[]{:S(2)}, u32[]{:S(2)}) async-start(f32[16,8,128]{2,1,0:T(8,128)} %settle.1), calls=%async_computation.10 | async-start | bytes 131072 | tf_op jit(solution)/shard_map/all_to_all | solution.py:685
  153.8 1.3 collective-permute-start.9
